TPU v7x, 32 devices: a whole 2x2x4 slice. The times are simulated.
32 devices in a mesh: slab: 8 (over z, x), img: 4 (over y, core).
Axes of the slice: x: 2, y: 2, z: 4, core: 2. Of those that a mesh axis runs over, the one named last changes fastest.
Arguments:
- volume: bfloat16 [4096, 256], P('slab'), may hold values from -6 to 6
- interp: bfloat16 [4, 8, 16, 4096], P('img', None, None, 'slab'), may hold values from -0.25 to 0.25
- block_index: int32 [4, 8, 8], P('img'), may hold values from 0 to 7
- images: bfloat16 [4, 128, 128, 256], P('img', 'slab'), may hold values from -6 to 6
- defocus: float32 [4, 128], P('img', 'slab'), may hold values from 5000 to 25000
- orient: int32 [4, 128, 4], P('img', 'slab'), may hold values from 0 to 7, all different within a row
Outputs:
- update: float32 [4096, 256], P('slab')
- weights: float32 [4, 128, 64], P('img', 'slab')
Inputs may be any that keep to these rules, and one draw needn't show every extreme that they name: `orient`: each image lists 4 different orientations of its group.
All inputs are finite; a program needn't handle non-finite values.
Results may differ from a plain program's by a relative error of at most 0.0077.
Values may be sent and summed in bfloat16 or wider, within the bound.
No kernel may reach another device: no remote copies, remote signals or barrier semaphores. Data moves between devices by JAX's collectives and lax.ppermute only.
A program may use at most 64 MiB of HBM per device.

v0:
```python
import math

import jax
import jax.numpy as jnp
from jax import lax
from jax.sharding import PartitionSpec as P

BOX = 256
NS = 16


wave_length = 0.0197
aberration = 27000000.0
amplitude = 0.1
grid_side = 4


def phase_tables(fourier, shifts, box):
    freq = (jnp.arange(fourier, dtype=jnp.int32) - fourier // 2).astype(jnp.float32)
    shift_steps = jnp.arange(shifts, dtype=jnp.int32)
    shift_x = (2 * (shift_steps // grid_side) - (grid_side - 1)).astype(jnp.float32)
    shift_y = (2 * (shift_steps % grid_side) - (grid_side - 1)).astype(jnp.float32)
    angle = 2.0 * math.pi / box * (freq[:, None, None] * shift_x + freq[None, :, None] * shift_y)
    forward = jnp.stack([jnp.cos(angle), jnp.sin(angle)], axis=1).reshape(
        2 * fourier * fourier, shifts
    )
    backward = jnp.stack([jnp.cos(angle), -jnp.sin(angle)], axis=1).reshape(
        2 * fourier * fourier, shifts
    )
    return (forward.astype(jnp.bfloat16), backward.T.astype(jnp.bfloat16))


def contrast(defocus_blk, fourier, box):
    freq = (jnp.arange(fourier, dtype=jnp.int32) - fourier // 2).astype(jnp.float32)
    wave_sq = (freq[:, None] * freq[:, None] + freq[None, :] * freq[None, :]) / (box * box)
    phase = math.pi * wave_length * defocus_blk[:, None, None] * wave_sq
    phase = phase - 0.5 * math.pi * aberration * wave_length**3 * wave_sq * wave_sq
    return -(math.sqrt(1.0 - amplitude * amplitude) * jnp.sin(phase) + amplitude * jnp.cos(phase))


def correlate(panels, image_blk, list_blk, defocus_blk, phase_fwd, phase_back, box):
    count = image_blk.shape[0]
    fourier = image_blk.shape[1]
    picks = list_blk.shape[1]
    shifts = phase_fwd.shape[1]
    ctf = contrast(defocus_blk, fourier, box)
    weighted = ctf[:, :, None, :] * image_blk.astype(jnp.float32).reshape(
        count, fourier, 2, fourier
    )
    real_u = weighted[:, None, :, 0]
    imag_u = weighted[:, None, :, 1]
    chosen = panels[list_blk].astype(jnp.float32).reshape(count, picks, fourier, 2, fourier)
    real_p = chosen[:, :, :, 0]
    imag_p = chosen[:, :, :, 1]
    product = jnp.stack(
        [real_p * real_u + imag_p * imag_u, real_p * imag_u - imag_p * real_u], axis=3
    )
    product = product.astype(jnp.bfloat16).reshape(count * picks, 2 * fourier * fourier)
    scores = jnp.dot(product, phase_fwd, preferred_element_type=jnp.float32) / fourier
    scores = scores.reshape(count, picks * shifts)
    squared = scores * scores
    weights = squared / (jnp.mean(squared, axis=1, keepdims=True) + 1e-05)
    rounded = weights.astype(jnp.bfloat16).reshape(count * picks, shifts)
    spread = jnp.dot(rounded, phase_back, preferred_element_type=jnp.float32)
    spread = spread.reshape(count, picks, fourier, 2, fourier)
    real_e = spread[:, :, :, 0]
    imag_e = spread[:, :, :, 1]
    backed = jnp.stack(
        [real_u * real_e - imag_u * imag_e, real_u * imag_e + imag_u * real_e], axis=3
    )
    backed = backed.astype(jnp.bfloat16).reshape(count * picks, 2 * fourier * fourier)
    return (weights, backed)


def on_device(volume, interp, block_index, images, defocus, orient):
    slab_count = lax.axis_size("slab")
    slab_index = lax.axis_index("slab")
    orient_count = interp.shape[1]
    ori_dev = orient_count // slab_count
    block_rows = interp.shape[2]
    fourier = images.shape[2]
    block_count = fourier // block_rows
    img_dev = images.shape[1]
    picks = orient.shape[2]
    levels = jnp.arange(block_count, dtype=jnp.int32)
    partial_value = jnp.einsum("jpr,rx->jpx", interp[0], volume, preferred_element_type=jnp.float32)
    owned_idx = lax.dynamic_slice_in_dim(block_index[0], slab_index * ori_dev, ori_dev, 0)
    arrived = lax.all_to_all(partial_value, "slab", split_axis=0, concat_axis=0, tiled=True)
    arrived = arrived.reshape(slab_count, ori_dev, block_rows, 2 * fourier)
    chosen = (owned_idx[:, :, None] == levels).astype(jnp.float32)
    summed = jnp.einsum("osb,sopx->obpx", chosen, arrived, precision=lax.Precision.HIGHEST)
    summed = summed.reshape(ori_dev, fourier, 2 * fourier)
    panels = lax.all_gather(summed.astype(jnp.bfloat16), "slab", axis=0, tiled=True)
    phase_fwd, phase_back = phase_tables(fourier, NS, BOX)
    blk = math.gcd(img_dev, 32)
    blk_total = img_dev // blk

    def per_block(pieces):
        image_blk, list_blk, defocus_blk = pieces
        return correlate(panels, image_blk, list_blk, defocus_blk, phase_fwd, phase_back, BOX)

    weights, backs = lax.map(
        per_block,
        (
            images[0].reshape(blk_total, blk, fourier, 2 * fourier),
            orient[0].reshape(blk_total, blk, picks),
            defocus[0].reshape(blk_total, blk),
        ),
    )
    all_slices = backs.reshape(img_dev * picks, 2 * fourier * fourier)
    member = (
        orient[0].reshape(-1)[:, None] == jnp.arange(orient_count, dtype=jnp.int32)[None, :]
    ).astype(jnp.bfloat16)
    back_own = lax.psum_scatter(
        lax.dot_general(
            member, all_slices, (((0,), (0,)), ((), ())), preferred_element_type=jnp.float32
        ),
        "slab",
        scatter_dimension=0,
        tiled=True,
    ).astype(jnp.bfloat16)
    back_own = back_own.reshape(ori_dev, block_count, block_rows, 2 * fourier)
    chosen_back = (owned_idx[:, :, None] == levels).astype(jnp.bfloat16)
    outgoing = jnp.einsum(
        "osb,obpx->sopx", chosen_back, back_own, preferred_element_type=jnp.float32
    )
    outgoing = outgoing.astype(jnp.bfloat16).reshape(slab_count * ori_dev, block_rows, 2 * fourier)
    incoming = lax.all_to_all(outgoing, "slab", split_axis=0, concat_axis=0, tiled=True)
    column = jnp.einsum("jpr,jpx->rx", interp[0], incoming, preferred_element_type=jnp.float32)
    summed_cols = lax.psum(column, "img")
    update = summed_cols / math.sqrt(img_dev * slab_count)
    return (update, weights)


def solution(mesh):
    return jax.shard_map(
        on_device,
        mesh=mesh,
        in_specs=(
            P("slab", None),
            P("img", None, None, "slab"),
            P("img", None, None),
            P("img", "slab", None, None),
            P("img", "slab"),
            P("img", "slab", None),
        ),
        out_specs=(P("slab", None), P("img", "slab", None)),
        check_vma=False,
    )
```

profile of v0, /device:TPU:0, one launch (start us, length us, event | category | flops | bytes accessed | tf_op | source)
XLA Modules:
  0.0 272.3 jit_solution(15767036161899373310)
XLA Ops:
  7.2 0.9 copy-done
  8.1 1.7 fusion.8
  9.9 7.3 %all-to-all-start = ((f32[8,16,256]{2,1,0:T(8,128)}), f32[8,16,256]{2,1,0:T(8,128)S(1)}, u32[]{:S(2)}, u32[]{:S(2)}) async-start(f32[8,16,256]{2,1,0:T(8,128)} %fusion.8), calls=%async_computation | async-start | bytes 262144 | tf_op jit(solution)/shard_map/all_to_all | solution.py:88
  19.6 2.1 reshape.428
  21.9 5.4 %fusion.7 = (bf16[128,1,128,16]{2,3,1,0:T(8,128)(2,1)S(1)}, bf16[128,1,128,16]{2,3,1,0:T(8,128)(2,1)}, bf16[128,1,128,16]{2,3,1,0:T(8,128)(2,1)S(1)}) fusion(f32[128,16]{0,1:T(8,128)S(1)} %get-tuple-element.51, f32[128,16]{1,0:T(8,128)S(1)} %copy.65), kind=kLoop, calls=%fused_computation.25 | loop fusion | flops 1572864 | bytes 1589248 | tf_op jit(solution)/shard_map/convert.7
  28.1 1.0 copy.66
  29.1 1.6 convert_element_type.148
  31.5 3.9 %add_negate_fusion = f32[16,128,128]{2,0,1:T(8,128)S(1)} fusion(f32[128,128]{1,0:T(8,128)S(1)} %get-tuple-element.49, f32[128,128]{1,0:T(8,128)S(1)} %get-tuple-element.48, f32[16]{0:T(128)S(1)} %multiply_bitcast_fusion), kind=kLoop, calls=%fused_computation.26 | loop fusion | flops 1572864 | bytes 1179712 | tf_op jit(solution)/shard_map/while/body/eval_jaxpr/neg | solution.py:38
  35.4 2.6 copy_multiply_fusion
  38.6 1.7 slice_bitcast_fusion.1
  40.6 32.1 %all_gather.3 = bf16[8,128,256]{2,1,0:T(8,128)(2,1)S(1)} all-gather(bf16[1,128,256]{2,1,0:T(8,128)(2,1)S(1)} %bitcast.56), channel_id=1, replica_groups=mesh['slab'=8,'img'=4] {'slab'}, dimensions={0}, use_global_device_ids=true | all-gather | bytes 589824 | tf_op jit(solution)/shard_map/all_gather | solution.py:93
  72.6 2.8 %gather_fusion = bf16[64,128,256]{2,1,0:T(8,128)(2,1)} fusion(bf16[8,128,256]{2,1,0:T(8,128)(2,1)S(1)} %all_gather.3, s32[1024]{0:T(1024)S(1)} %pad_clamp_fusion), kind=kCustom, calls=%fused_computation | custom fusion | bytes 8388864 | tf_op jit(solution)/shard_map/while/body/eval_jaxpr/gather | solution.py:52
  75.4 7.0 %copy.61 = f32[64,128,256]{1,2,0:T(8,128)} copy(bf16[64,128,256]{2,1,0:T(8,128)(2,1)} %gather_fusion) | data formatting | bytes 12582912 | tf_op jit(solution)/shard_map/while/body/eval_jaxpr/convert_element_type | solution.py:52
  82.4 7.8 %fusion.33 = (f32[16,4,128,1,128]{2,4,3,1,0:T(8,128)}, f32[16,4,128,1,128]{2,4,3,1,0:T(8,128)}) fusion(f32[16,4,128,2,128]{2,4,3,1,0:T(8,128)} %bitcast.55), kind=kLoop, calls=%fused_computation.72 | loop fusion | bytes 16777216 | tf_op jit(solution)/shard_map/while/body/eval_jaxpr/slice | solution.py:53
  90.2 5.4 %copy.79 = f32[16,4,128,1,128]{4,0,3,2,1:T(8,128)} copy(f32[16,4,128,1,128]{2,4,3,1,0:T(8,128)} %get-tuple-element.41) | data formatting | bytes 8388608
  95.6 5.5 %copy.80 = f32[16,4,128,1,128]{4,0,3,2,1:T(8,128)} copy(f32[16,4,128,1,128]{2,4,3,1,0:T(8,128)} %get-tuple-element.42) | data formatting | bytes 8388608
  101.1 4.7 %add_convert_fusion.1 = (bf16[16,4,128,1,128]{4,0,3,2,1:T(8,128)(2,1)S(1)}, bf16[16,4,128,1,128]{4,0,3,2,1:T(8,128)(2,1)S(1)}) fusion(f32[16,4,128,1,128]{4,0,3,2,1:T(8,128)} %copy.80, f32[16,4,128,1,128]{4,0,3,2,1:T(8,128)} %copy.79, f32[16,128,128]{2,0,1:T(8,128)S(1)} %get-tuple-element.44, f32[16,128,128]{2,0,1:T(8,128)S(1)} %get-tuple-element.43), kind=kLoop, calls=%fused_computation.6 | loop fusion | flops 8388608 | bytes 14680064 | tf_op jit(solution)/shard_map/convert.8
  106.2 6.6 %copy.64 = bf16[16,4,128,2,128]{4,3,2,1,0:T(2,128)(2,1)} copy(bf16[16,4,128,2,128]{4,0,3,2,1:T(8,128)(2,1)S(1)} %pad_maximum_fusion) | data formatting | bytes 8388608 | tf_op jit(solution)/shard_map/while/body/eval_jaxpr/stack | solution.py:55
  112.8 7.8 %convert_element_type.145 = bf16[64,32768]{1,0:T(8,128)(2,1)} reshape(bf16[16,4,128,2,128]{4,3,2,1,0:T(2,128)(2,1)} %copy.64) | data formatting | bytes 8388608 | tf_op jit(solution)/shard_map/while/body/eval_jaxpr/convert_element_type | solution.py:58
  120.6 3.7 %fusion.34 = (f32[64]{0:T(128)S(1)}, f32[64,16]{0,1:T(8,128)S(1)}) fusion(bf16[64,32768]{1,0:T(8,128)(2,1)} %convert_element_type.145, bf16[32768,16]{0,1:T(8,128)(2,1)} %convert_element_type.148), kind=kOutput, calls=%fused_computation.73 | convolution fusion | flops 67111872 | bytes 5247232 | tf_op jit(solution)/shard_map/while/body/eval_jaxpr/dot_general | solution.py:59
  124.8 2.3 fusion.3
  127.1 1.5 subtract_convert_fusion
  129.0 6.5 %copy.69 = bf16[16,4,128,2,128]{4,3,2,1,0:T(2,128)(2,1)} copy(bf16[16,4,128,2,128]{4,0,3,2,1:T(8,128)(2,1)S(1)} %pad_maximum_fusion.1) | data formatting | bytes 8388608 | tf_op jit(solution)/shard_map/while/body/eval_jaxpr/stack | solution.py:68
  135.6 7.9 %convert_element_type.150 = bf16[64,32768]{1,0:T(8,128)(2,1)} reshape(bf16[16,4,128,2,128]{4,3,2,1,0:T(2,128)(2,1)} %copy.69) | data formatting | bytes 8388608 | tf_op jit(solution)/shard_map/while/body/eval_jaxpr/convert_element_type | solution.py:71
  143.4 3.0 %fusion.16 = f32[8,32768]{1,0:T(8,128)S(1)} fusion(bf16[64,32768]{1,0:T(8,128)(2,1)} %convert_element_type.150, s32[64]{0:T(128)S(1)} %eq.65), kind=kOutput, calls=%fused_computation.40 | convolution fusion | flops 33554944 | bytes 5243136 | tf_op jit(solution)/shard_map/dot_general | solution.py:115
  146.4 74.0 %all-reduce.5 = bf16[8,32768]{1,0:T(8,128)(2,1)S(1)} all-reduce(f32[8,32768]{1,0:T(8,128)S(1)} %fusion.16), channel_id=2, replica_groups=mesh['slab'=8,'img'=4] {'slab'}, use_global_device_ids=true, to_apply=%region_2.3.clone | all-reduce | flops 262144 | bytes 1572864
  220.4 1.0 fusion.10
  221.7 9.3 %all_to_all.10 = bf16[8,16,256]{2,1,0:T(8,128)(2,1)S(1)} all-to-all(bf16[8,16,256]{2,1,0:T(8,128)(2,1)S(1)} %copy.71), channel_id=1, replica_groups=mesh['slab'=8,'img'=4] {'slab'}, dimensions={0} | all-to-all | bytes 131072 | tf_op jit(solution)/shard_map/all_to_all | solution.py:128
  231.0 1.0 convolution_bitcast_fusion
  232.9 30.4 %all-reduce.4.cloned.1.call-done = f32[512,256]{0,1:T(8,128)} async-done(((f32[512,256]{0,1:T(8,128)}), f32[512,256]{0,1:T(8,128)}) %all-reduce.4.cloned.1.call-update) | async-done | bytes 524304 | tf_op jit(solution)/shard_map/psum | solution.py:130
  263.4 1.1 broadcast_multiply_fusion
  264.5 1.0 copy.73
  (47 shorter events, 7.5 us)
Async XLA Ops:
  7.2 1.0 copy-start
  9.9 30.4 %all-to-all-start = ((f32[8,16,256]{2,1,0:T(8,128)}), f32[8,16,256]{2,1,0:T(8,128)S(1)}, u32[]{:S(2)}, u32[]{:S(2)}) async-start(f32[8,16,256]{2,1,0:T(8,128)} %fusion.8), calls=%async_computation | async-start | bytes 262144 | tf_op jit(solution)/shard_map/all_to_all | solution.py:88
  17.1 246.3 %all-reduce.4.cloned.1.call-start = ((), (), s32[]{:S(2)}) async-start(), calls=%async_computation.2 | async-start | bytes 1048576 | tf_op jit(solution)/shard_map/psum | solution.py:130
  27.2 0.8 copy-start.2
  29.1 8.9 %copy-start.5 = (u32[32]{0:T(128)S(1)}, u32[32]{0:T(128)}, u32[]{:S(2)}) copy-start(u32[32]{0:T(128)} %constant.113) | copy-start | bytes 388
  120.6 4.3 %copy-start.3 = (bf16[128,1,128,16]{2,3,1,0:T(8,128)(2,1)S(1)}, bf16[128,1,128,16]{2,3,1,0:T(8,128)(2,1)}, u32[]{:S(2)}) copy-start(bf16[128,1,128,16]{2,3,1,0:T(8,128)(2,1)} %copy-done.2) | copy-start | bytes 1572868
  143.4 87.6 %copy-start.4 = (bf16[1,8,16,512]{3,2,1,0:T(8,128)(2,1)S(1)}, bf16[1,8,16,512]{3,2,1,0:T(8,128)(2,1)}, u32[]{:S(2)}) copy-start(bf16[1,8,16,512]{3,2,1,0:T(8,128)(2,1)} %param.7) | copy-start | bytes 393220
  143.4 122.1 %copy-start.1 = (bf16[512,256]{1,0:T(8,128)(2,1)S(1)}, bf16[512,256]{1,0:T(8,128)(2,1)}, u32[]{:S(2)}) copy-start(bf16[512,256]{1,0:T(8,128)(2,1)} %param.6) | copy-start | bytes 786436
Sparse Core Ops, SparseCore 0:
  232.2 31.1 all-reduce.3
where the time goes:
time: 273 us; the launch traced here: 272 us
  blocking collectives  115 us (42%)
  local copies, waits for them, and re-layouts  70.4 us (26%)
  waiting for transfers between devices  30.5 us (11%)
  other arithmetic  22.3 us (8%)
  between operations  14.2 us (5%)
  matrix products  12.3 us (5%)
  starting transfers between devices  7.29 us (3%)
    unnamed x1, blocking collectives  74 us
    all_gather x1, blocking collectives, on_device(): lax.all_gather(summed.astype(jnp.bfloat16), 'slab', axis=0, tiled=True)  32.1 us
    psum x1, waiting for transfers between devices, on_device(): summed_cols = lax.psum(column, 'img')  30.4 us
    unnamed x17, local copies, waits for them, and re-layouts  15 us
    another operation x3, other arithmetic  11.6 us
    all_to_all x1, blocking collectives, on_device(): lax.all_to_all(outgoing, 'slab', split_axis=0, concat_axis=0, tiled=True)  9.29 us
    convert_element_type x1, local copies, waits for them, and re-layouts, correlate(): backed.astype(jnp.bfloat16).reshape(count * picks, 2 * fourier * fourier)  7.86 us
    slice x1, local copies, waits for them, and re-layouts, correlate(): real_p = chosen[:, :, :, 0]  7.81 us
  transfers between devices with their start and end apart: 2, of which 1 were waited for; matrix products, arithmetic and copies ran while one was open for 8% of the time, Pallas kernels for 0%

commit v1 on v0

--- a/solution.py
+++ b/solution.py
@@ -2,17 +2,238 @@
 
 import jax
 import jax.numpy as jnp
+import numpy as np
 from jax import lax
+from jax.experimental import pallas as pl
+from jax.experimental.pallas import tpu as pltpu
 from jax.sharding import PartitionSpec as P
 
 BOX = 256
 NS = 16
-
 
 wave_length = 0.0197
 aberration = 27000000.0
 amplitude = 0.1
 grid_side = 4
+LANES = 128
+DIRECT_BYTES = 4 << 20
+
+
+def split_bf16(values):
+    high = values.astype(jnp.bfloat16)
+    low = (values - high.astype(np.float64)).astype(jnp.bfloat16)
+    return high, low
+
+
+def separable_tables(fourier):
+    freq = np.arange(fourier) - fourier // 2
+    shift = np.arange(NS)
+    shift_x = 2 * (shift // grid_side) - (grid_side - 1)
+    shift_y = 2 * (shift % grid_side) - (grid_side - 1)
+    row = 2.0 * math.pi / BOX * freq[:, None] * shift_x
+    col = 2.0 * math.pi / BOX * freq[:, None] * shift_y
+    row_table = np.concatenate([np.cos(row), np.sin(row)] * 4, axis=1).astype(np.float32)
+    even = np.concatenate([np.cos(col), np.sin(col)], axis=0)
+    odd = np.concatenate([-np.sin(col), np.cos(col)], axis=0)
+    even_high, even_low = split_bf16(even)
+    odd_high, odd_low = split_bf16(odd)
+    col_fwd = np.concatenate([even_high, odd_high, even_low, odd_low] * 2, axis=1)
+    even = np.concatenate([np.cos(col), -np.sin(col)], axis=0).T
+    odd = np.concatenate([-np.sin(col), -np.cos(col)], axis=0).T
+    even_high, even_low = split_bf16(even)
+    odd_high, odd_low = split_bf16(odd)
+    blank = np.zeros((LANES - 4 * NS, 2 * fourier), jnp.bfloat16)
+    col_back = np.concatenate([even_high, odd_high, even_low, odd_low, blank], axis=0)
+    return row_table, col_fwd, col_back
+
+
+def contrast_tables(fourier):
+    freq = np.arange(fourier) - fourier // 2
+    wave_sq = (freq[:, None] ** 2 + freq[None, :] ** 2) / float(BOX * BOX)
+    slope = wave_length * wave_sq / 2.0
+    offset = -0.25 * aberration * wave_length**3 * wave_sq * wave_sq
+    offset = offset + math.asin(amplitude) / (2.0 * math.pi)
+    return slope.astype(np.float32), offset.astype(np.float32)
+
+
+def sin_turns(turns):
+    part = turns - jnp.round(turns)
+    folded = jnp.where(part > 0.25, 0.5 - part, jnp.where(part < -0.25, -0.5 - part, part))
+    x = folded * (2.0 * math.pi)
+    y = x * x
+    poly = -1.0 / 39916800.0
+    for coefficient in (1.0 / 362880.0, -1.0 / 5040.0, 1.0 / 120.0, -1.0 / 6.0, 1.0):
+        poly = poly * y + coefficient
+    return x * poly
+
+
+def weigh_images(slope, offset, images, defocus):
+    count, fourier, width = images.shape
+
+    def kernel(defocus_ref, slope_ref, offset_ref, image_ref, u_ref):
+        def one(i, _):
+            ctf = -sin_turns(defocus_ref[0, i] * slope_ref[...] + offset_ref[...])
+            u_ref[i, :, :fourier] = ctf * image_ref[i, :, :fourier].astype(jnp.float32)
+            u_ref[i, :, fourier:] = ctf * image_ref[i, :, fourier:].astype(jnp.float32)
+            return 0
+
+        lax.fori_loop(0, count, one, 0)
+
+    return pl.pallas_call(
+        kernel,
+        out_shape=jax.ShapeDtypeStruct(images.shape, jnp.float32),
+        in_specs=[pl.BlockSpec(memory_space=pltpu.SMEM)] + [pl.BlockSpec(memory_space=pltpu.VMEM)] * 3,
+        out_specs=pl.BlockSpec(memory_space=pltpu.VMEM),
+        compiler_params=pltpu.CompilerParams(vmem_limit_bytes=24 << 20),
+        cost_estimate=pl.CostEstimate(
+            flops=30 * count * fourier * fourier, bytes_accessed=6 * count * fourier * width, transcendentals=0
+        ),
+        name="weigh_images",
+    )(defocus, slope, offset, images)
+
+
+def expectation(tables, u, parts, slabs, block_index, orient):
+    count, fourier, width = u.shape
+    orient_count, block_rows, _ = parts[0].shape
+    slab_count = len(parts)
+    picks = orient.shape[1]
+    row_table, col_fwd, col_back = tables
+
+    def kernel(slabs_ref, index_ref, orient_ref, row_ref, fwd_ref, back_ref, u_ref, *rest):
+        part_refs = rest[:slab_count]
+        weights_ref, rows_ref, panel, total, score = rest[slab_count:]
+        panel[...] = jnp.zeros_like(panel)
+        for part in range(slab_count):
+            slab = slabs_ref[part]
+            for j in range(orient_count):
+                where = pl.ds(pl.multiple_of(index_ref[j, slab] * block_rows, block_rows), block_rows)
+                panel[j, where, :] += part_refs[part][j].astype(jnp.float32)
+        for j in range(orient_count):
+            panel[j] = panel[j].astype(jnp.bfloat16).astype(jnp.float32)
+        total[...] = jnp.zeros_like(total)
+
+        def forward(i, _):
+            real_u = u_ref[i, :, :fourier]
+            imag_u = u_ref[i, :, fourier:]
+            products = []
+            for k in range(picks):
+                j = orient_ref[i, k]
+                real_p = panel[j, :, :fourier]
+                imag_p = panel[j, :, fourier:]
+                products.append(
+                    jnp.concatenate(
+                        [
+                            (real_p * real_u + imag_p * imag_u).astype(jnp.bfloat16),
+                            (real_p * imag_u - imag_p * real_u).astype(jnp.bfloat16),
+                        ],
+                        axis=1,
+                    )
+                )
+            by_row = jnp.dot(
+                jnp.concatenate(products, axis=0), fwd_ref[...], preferred_element_type=jnp.float32
+            )
+            for k in range(picks):
+                mixed = by_row[k * fourier : (k + 1) * fourier] * row_ref[...]
+                score[k, pl.ds(i, 1), :] = jnp.sum(mixed, axis=0, keepdims=True)
+            return 0
+
+        lax.fori_loop(0, count, forward, 0)
+
+        squared = []
+        for k in range(picks):
+            value = score[k]
+            value = value + pltpu.roll(value, 2 * NS, 1)
+            value = value + pltpu.roll(value, NS, 1)
+            value = value * (1.0 / fourier)
+            squared.append(value * value)
+        mean = jnp.sum(sum(squared), axis=1, keepdims=True) * (1.0 / (LANES * picks))
+        scale = 1.0 / (mean + 1e-05)
+        lane = lax.broadcasted_iota(jnp.int32, (count, LANES), 1) // NS
+        merged = jnp.zeros((count, LANES), jnp.float32)
+        for k in range(picks):
+            value = squared[k] * scale
+            merged = jnp.where(lane == k, value, merged)
+            score[k] = value.astype(jnp.bfloat16).astype(jnp.float32)
+        weights_ref[...] = merged[:, : picks * NS]
+
+        def backward(i, _):
+            real_u = u_ref[i, :, :fourier]
+            imag_u = u_ref[i, :, fourier:]
+            mixed = [(row_ref[...] * score[k, pl.ds(i, 1), :]).astype(jnp.bfloat16) for k in range(picks)]
+            spread = jnp.dot(jnp.concatenate(mixed, axis=0), back_ref[...], preferred_element_type=jnp.float32)
+            for k in range(picks):
+                j = orient_ref[i, k]
+                real_e = spread[k * fourier : (k + 1) * fourier, :fourier]
+                imag_e = spread[k * fourier : (k + 1) * fourier, fourier:]
+                total[j, :, :fourier] += real_u * real_e - imag_u * imag_e
+                total[j, :, fourier:] += real_u * imag_e + imag_u * real_e
+            return 0
+
+        lax.fori_loop(0, count, backward, 0)
+
+        for slab in range(slab_count):
+            for j in range(orient_count):
+                where = pl.ds(pl.multiple_of(index_ref[j, slab] * block_rows, block_rows), block_rows)
+                rows_ref[slab, j] = total[j, where, :].astype(jnp.bfloat16)
+
+    smem = pl.BlockSpec(memory_space=pltpu.SMEM)
+    vmem = pl.BlockSpec(memory_space=pltpu.VMEM)
+    return pl.pallas_call(
+        kernel,
+        out_shape=(
+            jax.ShapeDtypeStruct((count, picks * NS), jnp.float32),
+            jax.ShapeDtypeStruct((slab_count, orient_count, block_rows, width), jnp.bfloat16),
+        ),
+        in_specs=[smem] * 3 + [vmem] * (4 + slab_count),
+        out_specs=(vmem, vmem),
+        scratch_shapes=[
+            pltpu.VMEM((orient_count, fourier, width), jnp.float32),
+            pltpu.VMEM((orient_count, fourier, width), jnp.float32),
+            pltpu.VMEM((picks, count, LANES), jnp.float32),
+        ],
+        compiler_params=pltpu.CompilerParams(vmem_limit_bytes=32 << 20),
+        cost_estimate=pl.CostEstimate(
+            flops=64 * count * picks * fourier * width, bytes_accessed=6 * count * fourier * width, transcendentals=0
+        ),
+        name="expectation",
+    )(slabs, block_index, orient, row_table, col_fwd, col_back, u, *parts)
+
+
+def exchange(value, axis, size):
+    return [
+        lax.ppermute(value, axis, [(source, (source + step) % size) for source in range(size)])
+        for step in range(1, size)
+    ]
+
+
+def direct(volume, interp, block_index, images, defocus, orient):
+    slab_count = lax.axis_size("slab")
+    group_count = lax.axis_size("img")
+    slab_index = lax.axis_index("slab")
+    orient_count, block_rows, slab_rows = interp.shape[1:]
+    fourier = images.shape[2]
+    width = images.shape[3]
+    image_count = images.shape[1] * slab_count
+    weigher = interp[0].reshape(orient_count * block_rows, slab_rows)
+    partial_value = jnp.dot(weigher, volume, preferred_element_type=jnp.float32).astype(jnp.bfloat16)
+    partial_value = partial_value.reshape(orient_count, block_rows, width)
+    parts = [partial_value] + exchange(partial_value, "slab", slab_count)
+    slabs = lax.rem(slab_index - jnp.arange(slab_count, dtype=jnp.int32) + slab_count, slab_count)
+    weighers = [weigher] + exchange(weigher, "img", group_count)
+    slope, offset = contrast_tables(fourier)
+    u = weigh_images(slope, offset, images[0], defocus)
+    weights, rows = expectation(separable_tables(fourier), u, parts, slabs, block_index[0], orient[0])
+    arrived = lax.all_to_all(rows, "slab", split_axis=0, concat_axis=0, tiled=True)
+    back = jnp.sum(arrived.astype(jnp.float32), axis=0).astype(jnp.bfloat16)
+    back = back.reshape(orient_count * block_rows, width)
+    backs = [back] + exchange(back, "img", group_count)
+    update = lax.dot_general(
+        jnp.concatenate(weighers, axis=0),
+        jnp.concatenate(backs, axis=0),
+        (((0,), (0,)), ((), ())),
+        preferred_element_type=jnp.float32,
+    )
+    return update / math.sqrt(image_count), weights[None]
 
 
 def phase_tables(fourier, shifts, box):
@@ -72,7 +293,7 @@
     return (weights, backed)
 
 
-def on_device(volume, interp, block_index, images, defocus, orient):
+def through_owners(volume, interp, block_index, images, defocus, orient):
     slab_count = lax.axis_size("slab")
     slab_index = lax.axis_index("slab")
     orient_count = interp.shape[1]
@@ -132,6 +353,13 @@
     return (update, weights)
 
 
+def on_device(volume, interp, block_index, images, defocus, orient):
+    orient_count, block_rows = interp.shape[1:3]
+    gathered = lax.axis_size("slab") * orient_count * block_rows * images.shape[3] * 2
+    plan = direct if gathered <= DIRECT_BYTES else through_owners
+    return plan(volume, interp, block_index, images, defocus, orient)
+
+
 def solution(mesh):
     return jax.shard_map(
         on_device,

time: 273 us -> 59.3 us (0.22)
  blocking collectives: 115 us -> 0 us
  local copies, waits for them, and re-layouts: 70.4 us -> 5.25 us
  other arithmetic: 22.3 us -> 0.08 us
  starting transfers between devices: 7.29 us -> 25.3 us
  waiting for transfers between devices: 30.5 us -> 13.3 us
  between operations: 14.2 us -> 0.76 us
  Pallas kernels: 0 us -> 11.7 us
  matrix products: 12.3 us -> 2.22 us
    unnamed x1 -> x0, blocking collectives: 74 us -> none
    all_gather x1 -> x0, blocking collectives: 32.1 us -> none  [on_device(): lax.all_gather(summed.astype(jnp.bfloat16), 'slab', axis=0, tiled=True)]
    psum x1 -> x0, waiting for transfers between devices: 30.4 us -> none  [on_device(): summed_cols = lax.psum(column, 'img')]
    convert_element_type x8 -> x0, local copies, waits for them, and re-layouts: 27.5 us -> none  [the longest x1 7.86 us: correlate(): backed.astype(jnp.bfloat16).reshape(count * picks, 2 * fourier * fourier)]
    ppermute x0 -> x13, starting transfers between devices: none -> 19.9 us  [exchange(): lax.ppermute(value, axis, [(source, (source + step) % size) for source in...]
    another operation x4 -> x0, local copies, waits for them, and re-layouts: 14.2 us -> none  [the longest x1 6.59 us: correlate(): jnp.stack([real_p * real_u + imag_p * imag_u, real_p * imag_u - imag_p *...]
    another operation x6 -> x0, other arithmetic: 12.4 us -> none
    pallas_call x0 -> x2, Pallas kernels: none -> 11.7 us  [the longest x1 10.1 us: expectation(): pl.pallas_call(kernel, out_shape=(jax.ShapeDtypeStruct((count, picks * NS...]
  transfers between devices with their start and end apart: 2 -> 14, of which waited for: 1 -> 6; matrix products, arithmetic and copies ran while one was open for 8% -> 1% of each run, Pallas kernels for 0% -> 3%
where the time goes in v1:
time: 59.3 us; the launch traced here: 58.6 us
  starting transfers between devices  25.3 us (43%)
  waiting for transfers between devices  13.3 us (22%)
  Pallas kernels  11.7 us (20%)
  local copies, waits for them, and re-layouts  5.25 us (9%)
  matrix products  2.22 us (4%)
  between operations  0.76 us (1%)
    ppermute x13, starting transfers between devices, exchange(): lax.ppermute(value, axis, [(source, (source + step) % size) for source in...  19.9 us
    pallas_call x1, Pallas kernels, expectation(): pl.pallas_call(kernel, out_shape=(jax.ShapeDtypeStruct((count, picks * NS...  10.1 us
    all_to_all x1, waiting for transfers between devices, direct(): lax.all_to_all(rows, 'slab', split_axis=0, concat_axis=0, tiled=True)  8.61 us
    all_to_all x1, starting transfers between devices, direct(): lax.all_to_all(rows, 'slab', split_axis=0, concat_axis=0, tiled=True)  5.39 us
    ppermute x13, waiting for transfers between devices, exchange(): lax.ppermute(value, axis, [(source, (source + step) % size) for source in...  4.72 us
    unnamed x20, local copies, waits for them, and re-layouts  4.49 us
    pallas_call x1, Pallas kernels, weigh_images(): pl.pallas_call(kernel, out_shape=jax.ShapeDtypeStruct(images.shape, jnp.f...  1.66 us
  transfers between devices with their start and end apart: 14, of which 6 were waited for; matrix products, arithmetic and copies ran while one was open for 1% of the time, Pallas kernels for 3%

profile of v1, /device:TPU:0, one launch (start us, length us, event | category | flops | bytes accessed | tf_op | source)
XLA Modules:
  0.0 58.6 jit_solution(1851808804327621422)
XLA Ops:
  0.6 0.0 copy-start
  0.7 0.9 %copy-done = bf16[512,256]{1,0:T(8,128)(2,1)S(1)} copy-done((bf16[512,256]{1,0:T(8,128)(2,1)S(1)}, bf16[512,256]{1,0:T(8,128)(2,1)}, u32[]{:S(2)}) %copy-start) | copy-done | bytes 262168
  1.6 1.1 %convolution_convert_fusion = bf16[128,256]{1,0:T(8,128)(2,1)S(1)} fusion(bf16[128,512]{1,0:T(8,128)(2,1)} %bitcast.19, bf16[512,256]{1,0:T(8,128)(2,1)S(1)} %copy-done), kind=kOutput, calls=%fused_computation.1 | convolution fusion | flops 33587200 | bytes 458752 | tf_op jit(solution)/shard_map/dot_general | solution.py:218
  2.7 3.0 %collective-permute-start.3 = (bf16[8,16,256]{2,1,0:T(8,128)(2,1)S(1)}, bf16[8,16,256]{2,1,0:T(8,128)(2,1)S(1)}, u32[]{:S(2)}, u32[]{:S(2)}) collective-permute-start(bf16[8,16,256]{2,1,0:T(8,128)(2,1)S(1)} %bitcast.10), channel_id=1, source_target_pairs={{0,4},{4,8},{8,12},{12,16},{16,20},{20,24},{24,28},{28,0},{1,5},{5... | collective-permute-start | bytes 196616 | tf_op jit(solution)/shard_map/ppermute | solution.py:204
  5.7 1.6 %collective-permute-start.4 = (bf16[8,16,256]{2,1,0:T(8,128)(2,1)S(1)}, bf16[8,16,256]{2,1,0:T(8,128)(2,1)S(1)}, u32[]{:S(2)}, u32[]{:S(2)}) collective-permute-start(bf16[8,16,256]{2,1,0:T(8,128)(2,1)S(1)} %bitcast.11), channel_id=1, source_target_pairs={{0,8},{4,12},{8,16},{12,20},{16,24},{20,28},{24,0},{28,4},{1,9},{5... | collective-permute-start | bytes 196616 | tf_op jit(solution)/shard_map/ppermute | solution.py:204
  7.2 2.6 %collective-permute-start.5 = (bf16[8,16,256]{2,1,0:T(8,128)(2,1)S(1)}, bf16[8,16,256]{2,1,0:T(8,128)(2,1)S(1)}, u32[]{:S(2)}, u32[]{:S(2)}) collective-permute-start(bf16[8,16,256]{2,1,0:T(8,128)(2,1)S(1)} %bitcast.12), channel_id=1, source_target_pairs={{0,12},{4,16},{8,20},{12,24},{16,28},{20,0},{24,4},{28,8},{1,13},{... | collective-permute-start | bytes 196616 | tf_op jit(solution)/shard_map/ppermute | solution.py:204
  9.8 1.2 %collective-permute-start.6 = (bf16[8,16,256]{2,1,0:T(8,128)(2,1)S(1)}, bf16[8,16,256]{2,1,0:T(8,128)(2,1)S(1)}, u32[]{:S(2)}, u32[]{:S(2)}) collective-permute-start(bf16[8,16,256]{2,1,0:T(8,128)(2,1)S(1)} %bitcast.13), channel_id=1, source_target_pairs={{0,16},{4,20},{8,24},{12,28},{16,0},{20,4},{24,8},{28,12},{1,17},{... | collective-permute-start | bytes 196616 | tf_op jit(solution)/shard_map/ppermute | solution.py:204
  11.0 2.6 %collective-permute-start.7 = (bf16[8,16,256]{2,1,0:T(8,128)(2,1)S(1)}, bf16[8,16,256]{2,1,0:T(8,128)(2,1)S(1)}, u32[]{:S(2)}, u32[]{:S(2)}) collective-permute-start(bf16[8,16,256]{2,1,0:T(8,128)(2,1)S(1)} %bitcast.14), channel_id=1, source_target_pairs={{0,20},{4,24},{8,28},{12,0},{16,4},{20,8},{24,12},{28,16},{1,21},{... | collective-permute-start | bytes 196616 | tf_op jit(solution)/shard_map/ppermute | solution.py:204
  13.7 0.8 %copy.13.orient_ref = s32[16,4]{1,0:T(8,128)S(1)} copy(s32[16,4]{0,1:T(4,128)} %bitcast.28) | data formatting | bytes 512 | tf_op jit(solution)/shard_map/squeeze | solution.py:225
  14.4 1.2 %copy-done.1 = bf16[1,16,128,256]{3,2,1,0:T(8,128)(2,1)S(1)} copy-done((bf16[1,16,128,256]{3,2,1,0:T(8,128)(2,1)S(1)}, bf16[1,16,128,256]{3,2,1,0:T(8,128)(2,1)}, u32[]{:S(2)}) %copy-start.1) | copy-done | bytes 1048600
  15.7 0.8 %copy-done.5 = f32[128,128]{1,0:T(8,128)S(1)} copy-done((f32[128,128]{1,0:T(8,128)S(1)}, f32[128,128]{1,0:T(8,128)}, u32[]{:S(2)}) %copy-start.5) | copy-done | bytes 65560
  16.5 0.8 %copy-done.6 = f32[128,128]{1,0:T(8,128)S(1)} copy-done((f32[128,128]{1,0:T(8,128)S(1)}, f32[128,128]{1,0:T(8,128)}, u32[]{:S(2)}) %copy-start.6) | copy-done | bytes 65560
  17.3 0.7 %copy-done.8 = f32[1,16]{1,0:T(1,128)S(1)} copy-done((f32[1,16]{1,0:T(1,128)S(1)}, f32[1,16]{1,0:T(1,128)}, u32[]{:S(2)}) %copy-start.8) | copy-done | bytes 88
  18.0 1.7 %weigh_images.1.u_ref = f32[16,128,256]{2,1,0:T(8,128)S(1)} custom-call(f32[1,16]{1,0:T(1,128)S(1)} %copy-done.8, f32[128,128]{1,0:T(8,128)S(1)} %copy-done.5, f32[128,128]{1,0:T(8,128)S(1)} %copy-done.6, bf16[16,128,256]{2,1,0:T(8,128)(2,1)S(1)} %bitcast.9), custom_call_target="tpu_custom_call" | custom-call | flops 7864320 | bytes 3145728 | tf_op jit(solution)/shard_map/weigh_images/pallas_call | solution.py:82
  19.7 1.4 %collective-permute-start.8 = (bf16[8,16,256]{2,1,0:T(8,128)(2,1)S(1)}, bf16[8,16,256]{2,1,0:T(8,128)(2,1)S(1)}, u32[]{:S(2)}, u32[]{:S(2)}) collective-permute-start(bf16[8,16,256]{2,1,0:T(8,128)(2,1)S(1)} %bitcast.15), channel_id=1, source_target_pairs={{0,24},{4,28},{8,0},{12,4},{16,8},{20,12},{24,16},{28,20},{1,25},{... | collective-permute-start | bytes 196616 | tf_op jit(solution)/shard_map/ppermute | solution.py:204
  21.1 1.4 %collective-permute-start.9 = (bf16[8,16,256]{2,1,0:T(8,128)(2,1)S(1)}, bf16[8,16,256]{2,1,0:T(8,128)(2,1)S(1)}, u32[]{:S(2)}, u32[]{:S(2)}) collective-permute-start(bf16[8,16,256]{2,1,0:T(8,128)(2,1)S(1)} %bitcast.16), channel_id=1, source_target_pairs={{0,28},{4,0},{8,4},{12,8},{16,12},{20,16},{24,20},{28,24},{1,29},{... | collective-permute-start | bytes 196616 | tf_op jit(solution)/shard_map/ppermute | solution.py:204
  22.5 1.4 %collective-permute-done.8.rest_6_ = bf16[8,16,256]{2,1,0:T(8,128)(2,1)S(1)} collective-permute-done((bf16[8,16,256]{2,1,0:T(8,128)(2,1)S(1)}, bf16[8,16,256]{2,1,0:T(8,128)(2,1)S(1)}, u32[]{:S(2)}, u32[]{:S(2)}) %collective-permute-start.8) | collective-permute-done | bytes 65568 | tf_op jit(solution)/shard_map/ppermute | solution.py:204
  24.0 1.4 %collective-permute-done.9.rest_7_ = bf16[8,16,256]{2,1,0:T(8,128)(2,1)S(1)} collective-permute-done((bf16[8,16,256]{2,1,0:T(8,128)(2,1)S(1)}, bf16[8,16,256]{2,1,0:T(8,128)(2,1)S(1)}, u32[]{:S(2)}, u32[]{:S(2)}) %collective-permute-start.9) | collective-permute-done | bytes 65568 | tf_op jit(solution)/shard_map/ppermute | solution.py:204
  25.4 10.1 %expectation.1 = (f32[16,64]{1,0:T(8,128)}, bf16[8,8,16,256]{3,2,1,0:T(8,128)(2,1)}) custom-call(s32[8]{0:T(128)S(1)} %compare_select_fusion.slabs_ref, s32[8,8]{1,0:T(8,128)S(1)} %bitcast.18, s32[16,4]{1,0:T(8,128)S(1)} %copy.13.orient_ref, f32[128,128]{1,0:T(8,128)S(1)} %copy-done.2, bf16[256,128]{1,0:T(8,128)(2,1)S(1)} %copy-done.3, ...), custom_call_target="tpu_custom_call" | custom-call | flops 134217728 | bytes 3145728 | tf_op jit(solution)/shard_map/expectation/pallas_call | solution.py:181
  35.4 5.4 %all-to-all-start = ((bf16[8,8,16,256]{3,2,1,0:T(8,128)(2,1)}), bf16[8,8,16,256]{3,2,1,0:T(8,128)(2,1)S(1)}, u32[]{:S(2)}, u32[]{:S(2)}) async-start(bf16[8,8,16,256]{3,2,1,0:T(8,128)(2,1)} %get-tuple-element.4), calls=%async_computation | async-start | bytes 1048576 | tf_op jit(solution)/shard_map/all_to_all | solution.py:226
  40.8 0.1 collective-permute-start
  40.9 1.6 %collective-permute-start.1 = (bf16[128,512]{1,0:T(8,128)(2,1)S(1)}, bf16[128,512]{1,0:T(8,128)(2,1)S(1)}, u32[]{:S(2)}, u32[]{:S(2)}) collective-permute-start(bf16[128,512]{1,0:T(8,128)(2,1)S(1)} %bitcast.21), channel_id=1, source_target_pairs={{0,2},{1,3},{2,0},{3,1},{4,6},{5,7},{6,4},{7,5},{8,10},{9,11},{10,... | collective-permute-start | bytes 393224 | tf_op jit(solution)/shard_map/ppermute | solution.py:204
  42.5 1.4 %collective-permute-start.2 = (bf16[128,512]{1,0:T(8,128)(2,1)S(1)}, bf16[128,512]{1,0:T(8,128)(2,1)S(1)}, u32[]{:S(2)}, u32[]{:S(2)}) collective-permute-start(bf16[128,512]{1,0:T(8,128)(2,1)S(1)} %bitcast.22), channel_id=1, source_target_pairs={{0,3},{1,0},{2,1},{3,2},{4,7},{5,4},{6,5},{7,6},{8,11},{9,8},{10,9... | collective-permute-start | bytes 393224 | tf_op jit(solution)/shard_map/ppermute | solution.py:204
  43.9 8.6 %all-to-all-done = bf16[8,8,16,256]{3,2,1,0:T(8,128)(2,1)S(1)} async-done(((bf16[8,8,16,256]{3,2,1,0:T(8,128)(2,1)}), bf16[8,8,16,256]{3,2,1,0:T(8,128)(2,1)S(1)}, u32[]{:S(2)}, u32[]{:S(2)}) %all-to-all-start) | async-done | bytes 524320 | tf_op jit(solution)/shard_map/all_to_all | solution.py:226
  52.5 0.1 reduce_sum.12
  52.6 0.1 collective-permute-start.10
  52.6 1.6 %collective-permute-start.11 = (bf16[128,256]{1,0:T(8,128)(2,1)S(1)}, bf16[128,256]{1,0:T(8,128)(2,1)S(1)}, u32[]{:S(2)}, u32[]{:S(2)}) collective-permute-start(bf16[128,256]{1,0:T(8,128)(2,1)S(1)} %bitcast.25), channel_id=1, source_target_pairs={{0,2},{1,3},{2,0},{3,1},{4,6},{5,7},{6,4},{7,5},{8,10},{9,11},{10,... | collective-permute-start | bytes 196616 | tf_op jit(solution)/shard_map/ppermute | solution.py:204
  54.2 1.4 %collective-permute-start.12 = (bf16[128,256]{1,0:T(8,128)(2,1)S(1)}, bf16[128,256]{1,0:T(8,128)(2,1)S(1)}, u32[]{:S(2)}, u32[]{:S(2)}) collective-permute-start(bf16[128,256]{1,0:T(8,128)(2,1)S(1)} %bitcast.26), channel_id=1, source_target_pairs={{0,3},{1,0},{2,1},{3,2},{4,7},{5,4},{6,5},{7,6},{8,11},{9,8},{10,9... | collective-permute-start | bytes 196616 | tf_op jit(solution)/shard_map/ppermute | solution.py:204
  55.6 0.8 %collective-permute-done.10 = bf16[128,256]{1,0:T(8,128)(2,1)S(1)} collective-permute-done((bf16[128,256]{1,0:T(8,128)(2,1)S(1)}, bf16[128,256]{1,0:T(8,128)(2,1)S(1)}, u32[]{:S(2)}, u32[]{:S(2)}) %collective-permute-start.10) | collective-permute-done | bytes 65568 | tf_op jit(solution)/shard_map/ppermute | solution.py:204
  56.4 0.8 %collective-permute-done.11 = bf16[128,256]{1,0:T(8,128)(2,1)S(1)} collective-permute-done((bf16[128,256]{1,0:T(8,128)(2,1)S(1)}, bf16[128,256]{1,0:T(8,128)(2,1)S(1)}, u32[]{:S(2)}, u32[]{:S(2)}) %collective-permute-start.11) | collective-permute-done | bytes 65568 | tf_op jit(solution)/shard_map/ppermute | solution.py:204
  57.3 0.2 collective-permute-done.12
  57.5 1.1 %convolution_multiply_fusion = f32[512,256]{1,0:T(8,128)} fusion(bf16[128,512]{1,0:T(8,128)(2,1)S(1)} %collective-permute-done.2, bf16[128,512]{1,0:T(8,128)(2,1)S(1)} %collective-permute-done.1, bf16[128,512]{1,0:T(8,128)(2,1)S(1)} %collective-permute-done, bf16[128,512]{1,0:T(8,128)(2,1)S(1)} %bitcast.23, bf16[128,256]{1,0:T(8,128)(2,1)S(1)} %collective-permute-done.12, ...), kind=kOutput, calls=%fused_computation | convolution fusion | flops 137494528 | bytes 1310720 | tf_op jit(solution)/shard_map/dot_general | solution.py:230
  (23 shorter events, 0.1 us)
Async XLA Ops:
  0.6 1.0 %copy-start = (bf16[512,256]{1,0:T(8,128)(2,1)S(1)}, bf16[512,256]{1,0:T(8,128)(2,1)}, u32[]{:S(2)}) copy-start(bf16[512,256]{1,0:T(8,128)(2,1)} %param.11) | copy-start | bytes 786436
  0.6 24.7 %copy-start.2 = (f32[128,128]{1,0:T(8,128)S(1)}, f32[128,128]{1,0:T(8,128)}, u32[]{:S(2)}) copy-start(f32[128,128]{1,0:T(8,128)} %constant.30.clone.row_ref) | copy-start | bytes 196612
  0.7 24.7 %copy-start.3 = (bf16[256,128]{1,0:T(8,128)(2,1)S(1)}, bf16[256,128]{1,0:T(8,128)(2,1)}, u32[]{:S(2)}) copy-start(bf16[256,128]{1,0:T(8,128)(2,1)} %constant.31.clone.fwd_ref) | copy-start | bytes 196612
  0.7 24.7 %copy-start.4 = (bf16[128,256]{1,0:T(8,128)(2,1)S(1)}, bf16[128,256]{1,0:T(8,128)(2,1)}, u32[]{:S(2)}) copy-start(bf16[128,256]{1,0:T(8,128)(2,1)} %constant.32.clone.back_ref) | copy-start | bytes 196612
  0.7 24.7 %copy-start.7 = (s32[1,8,8]{2,1,0:T(8,128)S(1)}, s32[1,8,8]{2,1,0:T(8,128)}, u32[]{:S(2)}) copy-start(s32[1,8,8]{2,1,0:T(8,128)} %param.13) | copy-start | bytes 772
  2.7 17.0 %collective-permute-start.3 = (bf16[8,16,256]{2,1,0:T(8,128)(2,1)S(1)}, bf16[8,16,256]{2,1,0:T(8,128)(2,1)S(1)}, u32[]{:S(2)}, u32[]{:S(2)}) collective-permute-start(bf16[8,16,256]{2,1,0:T(8,128)(2,1)S(1)} %bitcast.10), channel_id=1, source_target_pairs={{0,4},{4,8},{8,12},{12,16},{16,20},{20,24},{24,28},{28,0},{1,5},{5... | collective-permute-start | bytes 196616 | tf_op jit(solution)/shard_map/ppermute | solution.py:204
  5.7 15.4 %collective-permute-start.4 = (bf16[8,16,256]{2,1,0:T(8,128)(2,1)S(1)}, bf16[8,16,256]{2,1,0:T(8,128)(2,1)S(1)}, u32[]{:S(2)}, u32[]{:S(2)}) collective-permute-start(bf16[8,16,256]{2,1,0:T(8,128)(2,1)S(1)} %bitcast.11), channel_id=1, source_target_pairs={{0,8},{4,12},{8,16},{12,20},{16,24},{20,28},{24,0},{28,4},{1,9},{5... | collective-permute-start | bytes 196616 | tf_op jit(solution)/shard_map/ppermute | solution.py:204
  7.2 15.3 %collective-permute-start.5 = (bf16[8,16,256]{2,1,0:T(8,128)(2,1)S(1)}, bf16[8,16,256]{2,1,0:T(8,128)(2,1)S(1)}, u32[]{:S(2)}, u32[]{:S(2)}) collective-permute-start(bf16[8,16,256]{2,1,0:T(8,128)(2,1)S(1)} %bitcast.12), channel_id=1, source_target_pairs={{0,12},{4,16},{8,20},{12,24},{16,28},{20,0},{24,4},{28,8},{1,13},{... | collective-permute-start | bytes 196616 | tf_op jit(solution)/shard_map/ppermute | solution.py:204
  9.8 12.7 %collective-permute-start.6 = (bf16[8,16,256]{2,1,0:T(8,128)(2,1)S(1)}, bf16[8,16,256]{2,1,0:T(8,128)(2,1)S(1)}, u32[]{:S(2)}, u32[]{:S(2)}) collective-permute-start(bf16[8,16,256]{2,1,0:T(8,128)(2,1)S(1)} %bitcast.13), channel_id=1, source_target_pairs={{0,16},{4,20},{8,24},{12,28},{16,0},{20,4},{24,8},{28,12},{1,17},{... | collective-permute-start | bytes 196616 | tf_op jit(solution)/shard_map/ppermute | solution.py:204
  11.0 11.5 %collective-permute-start.7 = (bf16[8,16,256]{2,1,0:T(8,128)(2,1)S(1)}, bf16[8,16,256]{2,1,0:T(8,128)(2,1)S(1)}, u32[]{:S(2)}, u32[]{:S(2)}) collective-permute-start(bf16[8,16,256]{2,1,0:T(8,128)(2,1)S(1)} %bitcast.14), channel_id=1, source_target_pairs={{0,20},{4,24},{8,28},{12,0},{16,4},{20,8},{24,12},{28,16},{1,21},{... | collective-permute-start | bytes 196616 | tf_op jit(solution)/shard_map/ppermute | solution.py:204
  14.4 1.2 %copy-start.1 = (bf16[1,16,128,256]{3,2,1,0:T(8,128)(2,1)S(1)}, bf16[1,16,128,256]{3,2,1,0:T(8,128)(2,1)}, u32[]{:S(2)}) copy-start(bf16[1,16,128,256]{3,2,1,0:T(8,128)(2,1)} %param.14) | copy-start | bytes 3145732
  15.6 0.8 %copy-start.5 = (f32[128,128]{1,0:T(8,128)S(1)}, f32[128,128]{1,0:T(8,128)}, u32[]{:S(2)}) copy-start(f32[128,128]{1,0:T(8,128)} %constant.28.clone.slope_ref) | copy-start | bytes 196612
  16.5 0.8 %copy-start.6 = (f32[128,128]{1,0:T(8,128)S(1)}, f32[128,128]{1,0:T(8,128)}, u32[]{:S(2)}) copy-start(f32[128,128]{1,0:T(8,128)} %constant.29.clone.offset_ref) | copy-start | bytes 196612
  17.3 0.7 %copy-start.8 = (f32[1,16]{1,0:T(1,128)S(1)}, f32[1,16]{1,0:T(1,128)}, u32[]{:S(2)}) copy-start(f32[1,16]{1,0:T(1,128)} %defocus_ref.1) | copy-start | bytes 196
  19.6 21.2 %copy-start.9 = (bf16[1,8,16,512]{3,2,1,0:T(8,128)(2,1)S(1)}, bf16[1,8,16,512]{3,2,1,0:T(8,128)(2,1)}, u32[]{:S(2)}) copy-start(bf16[1,8,16,512]{3,2,1,0:T(8,128)(2,1)} %param.12) | copy-start | bytes 393220
  19.7 4.3 %collective-permute-start.8 = (bf16[8,16,256]{2,1,0:T(8,128)(2,1)S(1)}, bf16[8,16,256]{2,1,0:T(8,128)(2,1)S(1)}, u32[]{:S(2)}, u32[]{:S(2)}) collective-permute-start(bf16[8,16,256]{2,1,0:T(8,128)(2,1)S(1)} %bitcast.15), channel_id=1, source_target_pairs={{0,24},{4,28},{8,0},{12,4},{16,8},{20,12},{24,16},{28,20},{1,25},{... | collective-permute-start | bytes 196616 | tf_op jit(solution)/shard_map/ppermute | solution.py:204
  21.1 4.3 %collective-permute-start.9 = (bf16[8,16,256]{2,1,0:T(8,128)(2,1)S(1)}, bf16[8,16,256]{2,1,0:T(8,128)(2,1)S(1)}, u32[]{:S(2)}, u32[]{:S(2)}) collective-permute-start(bf16[8,16,256]{2,1,0:T(8,128)(2,1)S(1)} %bitcast.16), channel_id=1, source_target_pairs={{0,28},{4,0},{8,4},{12,8},{16,12},{20,16},{24,20},{28,24},{1,29},{... | collective-permute-start | bytes 196616 | tf_op jit(solution)/shard_map/ppermute | solution.py:204
  35.4 17.1 %all-to-all-start = ((bf16[8,8,16,256]{3,2,1,0:T(8,128)(2,1)}), bf16[8,8,16,256]{3,2,1,0:T(8,128)(2,1)S(1)}, u32[]{:S(2)}, u32[]{:S(2)}) async-start(bf16[8,8,16,256]{3,2,1,0:T(8,128)(2,1)} %get-tuple-element.4), calls=%async_computation | async-start | bytes 1048576 | tf_op jit(solution)/shard_map/all_to_all | solution.py:226
  40.8 13.4 %collective-permute-start = (bf16[128,512]{1,0:T(8,128)(2,1)S(1)}, bf16[128,512]{1,0:T(8,128)(2,1)S(1)}, u32[]{:S(2)}, u32[]{:S(2)}) collective-permute-start(bf16[128,512]{1,0:T(8,128)(2,1)S(1)} %bitcast.20), channel_id=1, source_target_pairs={{0,1},{1,2},{2,3},{3,0},{4,5},{5,6},{6,7},{7,4},{8,9},{9,10},{10,1... | collective-permute-start | bytes 393224 | tf_op jit(solution)/shard_map/ppermute | solution.py:204
  40.9 14.7 %collective-permute-start.1 = (bf16[128,512]{1,0:T(8,128)(2,1)S(1)}, bf16[128,512]{1,0:T(8,128)(2,1)S(1)}, u32[]{:S(2)}, u32[]{:S(2)}) collective-permute-start(bf16[128,512]{1,0:T(8,128)(2,1)S(1)} %bitcast.21), channel_id=1, source_target_pairs={{0,2},{1,3},{2,0},{3,1},{4,6},{5,7},{6,4},{7,5},{8,10},{9,11},{10,... | collective-permute-start | bytes 393224 | tf_op jit(solution)/shard_map/ppermute | solution.py:204
  42.5 13.1 %collective-permute-start.2 = (bf16[128,512]{1,0:T(8,128)(2,1)S(1)}, bf16[128,512]{1,0:T(8,128)(2,1)S(1)}, u32[]{:S(2)}, u32[]{:S(2)}) collective-permute-start(bf16[128,512]{1,0:T(8,128)(2,1)S(1)} %bitcast.22), channel_id=1, source_target_pairs={{0,3},{1,0},{2,1},{3,2},{4,7},{5,4},{6,5},{7,6},{8,11},{9,8},{10,9... | collective-permute-start | bytes 393224 | tf_op jit(solution)/shard_map/ppermute | solution.py:204
  52.6 3.8 %collective-permute-start.10 = (bf16[128,256]{1,0:T(8,128)(2,1)S(1)}, bf16[128,256]{1,0:T(8,128)(2,1)S(1)}, u32[]{:S(2)}, u32[]{:S(2)}) collective-permute-start(bf16[128,256]{1,0:T(8,128)(2,1)S(1)} %bitcast.24), channel_id=1, source_target_pairs={{0,1},{1,2},{2,3},{3,0},{4,5},{5,6},{6,7},{7,4},{8,9},{9,10},{10,1... | collective-permute-start | bytes 196616 | tf_op jit(solution)/shard_map/ppermute | solution.py:204
  52.6 4.6 %collective-permute-start.11 = (bf16[128,256]{1,0:T(8,128)(2,1)S(1)}, bf16[128,256]{1,0:T(8,128)(2,1)S(1)}, u32[]{:S(2)}, u32[]{:S(2)}) collective-permute-start(bf16[128,256]{1,0:T(8,128)(2,1)S(1)} %bitcast.25), channel_id=1, source_target_pairs={{0,2},{1,3},{2,0},{3,1},{4,6},{5,7},{6,4},{7,5},{8,10},{9,11},{10,... | collective-permute-start | bytes 196616 | tf_op jit(solution)/shard_map/ppermute | solution.py:204
  54.2 3.3 %collective-permute-start.12 = (bf16[128,256]{1,0:T(8,128)(2,1)S(1)}, bf16[128,256]{1,0:T(8,128)(2,1)S(1)}, u32[]{:S(2)}, u32[]{:S(2)}) collective-permute-start(bf16[128,256]{1,0:T(8,128)(2,1)S(1)} %bitcast.26), channel_id=1, source_target_pairs={{0,3},{1,0},{2,1},{3,2},{4,7},{5,4},{6,5},{7,6},{8,11},{9,8},{10,9... | collective-permute-start | bytes 196616 | tf_op jit(solution)/shard_map/ppermute | solution.py:204

commit v2 on v1

--- a/solution.py
+++ b/solution.py
@@ -47,15 +47,6 @@
     return row_table, col_fwd, col_back
 
 
-def contrast_tables(fourier):
-    freq = np.arange(fourier) - fourier // 2
-    wave_sq = (freq[:, None] ** 2 + freq[None, :] ** 2) / float(BOX * BOX)
-    slope = wave_length * wave_sq / 2.0
-    offset = -0.25 * aberration * wave_length**3 * wave_sq * wave_sq
-    offset = offset + math.asin(amplitude) / (2.0 * math.pi)
-    return slope.astype(np.float32), offset.astype(np.float32)
-
-
 def sin_turns(turns):
     part = turns - jnp.round(turns)
     folded = jnp.where(part > 0.25, 0.5 - part, jnp.where(part < -0.25, -0.5 - part, part))
@@ -67,36 +58,39 @@
     return x * poly
 
 
-def weigh_images(slope, offset, images, defocus):
-    count, fourier, width = images.shape
-
-    def kernel(defocus_ref, slope_ref, offset_ref, image_ref, u_ref):
-        def one(i, _):
-            ctf = -sin_turns(defocus_ref[0, i] * slope_ref[...] + offset_ref[...])
-            u_ref[i, :, :fourier] = ctf * image_ref[i, :, :fourier].astype(jnp.float32)
-            u_ref[i, :, fourier:] = ctf * image_ref[i, :, fourier:].astype(jnp.float32)
-            return 0
-
-        lax.fori_loop(0, count, one, 0)
+def weigh_images(images, defocus):
+    _, count, fourier, width = images.shape
+
+    def kernel(defocus_ref, image_ref, u_ref):
+        kx = lax.broadcasted_iota(jnp.int32, (fourier, fourier), 0) - fourier // 2
+        ky = lax.broadcasted_iota(jnp.int32, (fourier, fourier), 1) - fourier // 2
+        wave_sq = (kx * kx + ky * ky).astype(jnp.float32) * (1.0 / (BOX * BOX))
+        slope = wave_sq * (0.5 * wave_length)
+        offset = wave_sq * wave_sq * (-0.25 * aberration * wave_length**3)
+        offset = offset + math.asin(amplitude) / (2.0 * math.pi)
+        for i in range(count):
+            ctf = -sin_turns(defocus_ref[0, i] * slope + offset)
+            u_ref[i, :, :fourier] = ctf * image_ref[0, i, :, :fourier].astype(jnp.float32)
+            u_ref[i, :, fourier:] = ctf * image_ref[0, i, :, fourier:].astype(jnp.float32)
 
     return pl.pallas_call(
         kernel,
-        out_shape=jax.ShapeDtypeStruct(images.shape, jnp.float32),
-        in_specs=[pl.BlockSpec(memory_space=pltpu.SMEM)] + [pl.BlockSpec(memory_space=pltpu.VMEM)] * 3,
+        out_shape=jax.ShapeDtypeStruct(images.shape[1:], jnp.float32),
+        in_specs=[pl.BlockSpec(memory_space=pltpu.SMEM), pl.BlockSpec(memory_space=pltpu.VMEM)],
         out_specs=pl.BlockSpec(memory_space=pltpu.VMEM),
         compiler_params=pltpu.CompilerParams(vmem_limit_bytes=24 << 20),
         cost_estimate=pl.CostEstimate(
             flops=30 * count * fourier * fourier, bytes_accessed=6 * count * fourier * width, transcendentals=0
         ),
         name="weigh_images",
-    )(defocus, slope, offset, images)
+    )(defocus, images)
 
 
 def expectation(tables, u, parts, slabs, block_index, orient):
     count, fourier, width = u.shape
     orient_count, block_rows, _ = parts[0].shape
     slab_count = len(parts)
-    picks = orient.shape[1]
+    picks = orient.shape[0]
     row_table, col_fwd, col_back = tables
 
     def kernel(slabs_ref, index_ref, orient_ref, row_ref, fwd_ref, back_ref, u_ref, *rest):
@@ -117,7 +111,7 @@
             imag_u = u_ref[i, :, fourier:]
             products = []
             for k in range(picks):
-                j = orient_ref[i, k]
+                j = orient_ref[k, i]
                 real_p = panel[j, :, :fourier]
                 imag_p = panel[j, :, fourier:]
                 products.append(
@@ -137,7 +131,7 @@
                 score[k, pl.ds(i, 1), :] = jnp.sum(mixed, axis=0, keepdims=True)
             return 0
 
-        lax.fori_loop(0, count, forward, 0)
+        lax.fori_loop(0, count, forward, 0, unroll=True)
 
         squared = []
         for k in range(picks):
@@ -162,14 +156,14 @@
             mixed = [(row_ref[...] * score[k, pl.ds(i, 1), :]).astype(jnp.bfloat16) for k in range(picks)]
             spread = jnp.dot(jnp.concatenate(mixed, axis=0), back_ref[...], preferred_element_type=jnp.float32)
             for k in range(picks):
-                j = orient_ref[i, k]
+                j = orient_ref[k, i]
                 real_e = spread[k * fourier : (k + 1) * fourier, :fourier]
                 imag_e = spread[k * fourier : (k + 1) * fourier, fourier:]
                 total[j, :, :fourier] += real_u * real_e - imag_u * imag_e
                 total[j, :, fourier:] += real_u * imag_e + imag_u * real_e
             return 0
 
-        lax.fori_loop(0, count, backward, 0)
+        lax.fori_loop(0, count, backward, 0, unroll=True)
 
         for slab in range(slab_count):
             for j in range(orient_count):
@@ -204,6 +198,10 @@
         lax.ppermute(value, axis, [(source, (source + step) % size) for source in range(size)])
         for step in range(1, size)
     ]
+
+
+def swap(value, axis, size, flip):
+    return lax.ppermute(value, axis, [(source, source ^ flip) for source in range(size)])
 
 
 def direct(volume, interp, block_index, images, defocus, orient):
@@ -217,12 +215,16 @@
     weigher = interp[0].reshape(orient_count * block_rows, slab_rows)
     partial_value = jnp.dot(weigher, volume, preferred_element_type=jnp.float32).astype(jnp.bfloat16)
     partial_value = partial_value.reshape(orient_count, block_rows, width)
-    parts = [partial_value] + exchange(partial_value, "slab", slab_count)
-    slabs = lax.rem(slab_index - jnp.arange(slab_count, dtype=jnp.int32) + slab_count, slab_count)
+    same_x = [partial_value] + [swap(partial_value, "slab", slab_count, flip) for flip in range(2, slab_count, 2)]
+    other_x = [swap(partial_value, "slab", slab_count, 1)]
+    passed_on = swap(jnp.stack(same_x[1:]), "slab", slab_count, 1)
+    other_x += [passed_on[i] for i in range(slab_count // 2 - 1)]
+    parts = same_x + other_x
+    flips = list(range(0, slab_count, 2)) + list(range(1, slab_count, 2))
+    slabs = jnp.bitwise_xor(slab_index, jnp.array(flips, jnp.int32))
     weighers = [weigher] + exchange(weigher, "img", group_count)
-    slope, offset = contrast_tables(fourier)
-    u = weigh_images(slope, offset, images[0], defocus)
-    weights, rows = expectation(separable_tables(fourier), u, parts, slabs, block_index[0], orient[0])
+    u = weigh_images(images, defocus)
+    weights, rows = expectation(separable_tables(fourier), u, parts, slabs, block_index[0], orient[0].T)
     arrived = lax.all_to_all(rows, "slab", split_axis=0, concat_axis=0, tiled=True)
     back = jnp.sum(arrived.astype(jnp.float32), axis=0).astype(jnp.bfloat16)
     back = back.reshape(orient_count * block_rows, width)
@@ -356,7 +358,8 @@
 def on_device(volume, interp, block_index, images, defocus, orient):
     orient_count, block_rows = interp.shape[1:3]
     gathered = lax.axis_size("slab") * orient_count * block_rows * images.shape[3] * 2
-    plan = direct if gathered <= DIRECT_BYTES else through_owners
+    pairs = lax.axis_size("slab") == 8
+    plan = direct if pairs and gathered <= DIRECT_BYTES else through_owners
     return plan(volume, interp, block_index, images, defocus, orient)
 
 

time: 59.3 us -> 49.6 us (0.84)
  starting transfers between devices: 25.3 us -> 18.1 us
  waiting for transfers between devices: 13.3 us -> 18 us
  Pallas kernels: 11.7 us -> 7.22 us
  local copies, waits for them, and re-layouts: 5.25 us -> 2.86 us
    ppermute x13 -> x6, starting transfers between devices: 19.9 us -> 5.11 us  [exchange(): lax.ppermute(value, axis, [(source, (source + step) % size) for source in...]
    ppermute x0 -> x5, starting transfers between devices: none -> 8.94 us  [swap(): lax.ppermute(value, axis, [(source, source ^ flip) for source in range(si...]
    ppermute x0 -> x5, waiting for transfers between devices: none -> 5.04 us  [swap(): lax.ppermute(value, axis, [(source, source ^ flip) for source in range(si...]
    pallas_call x1, Pallas kernels: 10.1 us -> 5.62 us  [expectation(): pl.pallas_call(kernel, out_shape=(jax.ShapeDtypeStruct((count, picks * NS...]
    unnamed x20, local copies, waits for them, and re-layouts: 4.49 us -> 2.84 us
    all_to_all x1, starting transfers between devices: 5.39 us -> 4.03 us  [direct(): lax.all_to_all(rows, 'slab', split_axis=0, concat_axis=0, tiled=True)]
    ppermute x13 -> x6, waiting for transfers between devices: 4.72 us -> 3.83 us  [exchange(): lax.ppermute(value, axis, [(source, (source + step) % size) for source in...]
    squeeze x1, local copies, waits for them, and re-layouts: 0.76 us -> 0.01 us  [direct(): other_x += [passed_on[i] for i in range(slab_count // 2 - 1)]]
  transfers between devices with their start and end apart: 14 -> 12, of which waited for: 6 -> 5; matrix products, arithmetic and copies ran while one was open for 1% -> 0% of each run, Pallas kernels for 3% -> 3%
where the time goes in v2:
time: 49.6 us; the launch traced here: 49.3 us
  starting transfers between devices  18.1 us (36%)
  waiting for transfers between devices  18 us (36%)
  Pallas kernels  7.22 us (15%)
  local copies, waits for them, and re-layouts  2.86 us (6%)
  matrix products  2.26 us (5%)
  between operations  0.78 us (2%)
    all_to_all x1, waiting for transfers between devices, direct(): lax.all_to_all(rows, 'slab', split_axis=0, concat_axis=0, tiled=True)  9.17 us
    ppermute x5, starting transfers between devices, swap(): lax.ppermute(value, axis, [(source, source ^ flip) for source in range(si...  8.94 us
    pallas_call x1, Pallas kernels, expectation(): pl.pallas_call(kernel, out_shape=(jax.ShapeDtypeStruct((count, picks * NS...  5.62 us
    ppermute x6, starting transfers between devices, exchange(): lax.ppermute(value, axis, [(source, (source + step) % size) for source in...  5.11 us
    ppermute x5, waiting for transfers between devices, swap(): lax.ppermute(value, axis, [(source, source ^ flip) for source in range(si...  5.04 us
    all_to_all x1, starting transfers between devices, direct(): lax.all_to_all(rows, 'slab', split_axis=0, concat_axis=0, tiled=True)  4.03 us
    ppermute x6, waiting for transfers between devices, exchange(): lax.ppermute(value, axis, [(source, (source + step) % size) for source in...  3.83 us
    unnamed x20, local copies, waits for them, and re-layouts  2.84 us
  transfers between devices with their start and end apart: 12, of which 5 were waited for; matrix products, arithmetic and copies ran while one was open for 0% of the time, Pallas kernels for 3%

profile of v2, /device:TPU:0, one launch (start us, length us, event | category | flops | bytes accessed | tf_op | source)
XLA Modules:
  0.0 49.3 jit_solution(10803942999015593622)
XLA Ops:
  0.6 0.0 copy-start
  0.6 0.0 copy-start.9
  0.7 0.9 %copy-done = bf16[512,256]{1,0:T(8,128)(2,1)S(1)} copy-done((bf16[512,256]{1,0:T(8,128)(2,1)S(1)}, bf16[512,256]{1,0:T(8,128)(2,1)}, u32[]{:S(2)}) %copy-start) | copy-done | bytes 262168
  1.6 1.1 %convolution_convert_fusion = bf16[128,256]{1,0:T(8,128)(2,1)S(1)} fusion(bf16[128,512]{1,0:T(8,128)(2,1)} %bitcast.29, bf16[512,256]{1,0:T(8,128)(2,1)S(1)} %copy-done), kind=kOutput, calls=%fused_computation.1 | convolution fusion | flops 33587200 | bytes 458752 | tf_op jit(solution)/shard_map/dot_general | solution.py:216
  2.7 3.1 %collective-permute-start.3 = (bf16[8,16,256]{2,1,0:T(8,128)(2,1)S(1)}, bf16[8,16,256]{2,1,0:T(8,128)(2,1)S(1)}, u32[]{:S(2)}, u32[]{:S(2)}) collective-permute-start(bf16[8,16,256]{2,1,0:T(8,128)(2,1)S(1)} %bitcast.19), channel_id=1, source_target_pairs={{0,8},{4,12},{8,0},{12,4},{16,24},{20,28},{24,16},{28,20},{1,9},{5... | collective-permute-start | bytes 196616 | tf_op jit(solution)/shard_map/ppermute | solution.py:204
  5.8 2.6 %collective-permute-start.4 = (bf16[8,16,256]{2,1,0:T(8,128)(2,1)S(1)}, bf16[8,16,256]{2,1,0:T(8,128)(2,1)S(1)}, u32[]{:S(2)}, u32[]{:S(2)}) collective-permute-start(bf16[8,16,256]{2,1,0:T(8,128)(2,1)S(1)} %bitcast.20), channel_id=1, source_target_pairs={{0,16},{4,20},{8,24},{12,28},{16,0},{20,4},{24,8},{28,12},{1,17},{... | collective-permute-start | bytes 196616 | tf_op jit(solution)/shard_map/ppermute | solution.py:204
  8.4 0.0 collective-permute-start.5
  8.4 1.7 %collective-permute-start.6 = (bf16[8,16,256]{2,1,0:T(8,128)(2,1)S(1)}, bf16[8,16,256]{2,1,0:T(8,128)(2,1)S(1)}, u32[]{:S(2)}, u32[]{:S(2)}) collective-permute-start(bf16[8,16,256]{2,1,0:T(8,128)(2,1)S(1)} %bitcast.22), channel_id=1, source_target_pairs={{0,4},{4,0},{8,12},{12,8},{16,20},{20,16},{24,28},{28,24},{1,5},{5... | collective-permute-start | bytes 196616 | tf_op jit(solution)/shard_map/ppermute | solution.py:204
  10.1 1.2 %copy-done.1 = bf16[1,16,128,256]{3,2,1,0:T(8,128)(2,1)S(1)} copy-done((bf16[1,16,128,256]{3,2,1,0:T(8,128)(2,1)S(1)}, bf16[1,16,128,256]{3,2,1,0:T(8,128)(2,1)}, u32[]{:S(2)}) %copy-start.1) | copy-done | bytes 1048600
  11.4 0.7 %copy-done.7 = f32[1,16]{1,0:T(1,128)S(1)} copy-done((f32[1,16]{1,0:T(1,128)S(1)}, f32[1,16]{1,0:T(1,128)}, u32[]{:S(2)}) %copy-start.7) | copy-done | bytes 88
  12.0 1.6 %weigh_images.1.u_ref = f32[16,128,256]{2,1,0:T(8,128)S(1)} custom-call(f32[1,16]{1,0:T(1,128)S(1)} %copy-done.7, bf16[1,16,128,256]{3,2,1,0:T(8,128)(2,1)S(1)} %copy-done.1), custom_call_target="tpu_custom_call" | custom-call | flops 7864320 | bytes 3145728 | tf_op jit(solution)/shard_map/weigh_images/pallas_call | solution.py:76
  13.6 0.0 collective-permute-done.3.rest_1_
  13.6 0.9 %collective-permute-done.5.rest_3_ = bf16[8,16,256]{2,1,0:T(8,128)(2,1)S(1)} collective-permute-done((bf16[8,16,256]{2,1,0:T(8,128)(2,1)S(1)}, bf16[8,16,256]{2,1,0:T(8,128)(2,1)S(1)}, u32[]{:S(2)}, u32[]{:S(2)}) %collective-permute-start.5) | collective-permute-done | bytes 65568 | tf_op jit(solution)/shard_map/ppermute | solution.py:204
  14.5 1.6 %collective-permute-start.7 = (bf16[3,8,16,256]{3,2,1,0:T(8,128)(2,1)S(1)}, bf16[3,8,16,256]{3,2,1,0:T(8,128)(2,1)S(1)}, u32[]{:S(2)}, u32[]{:S(2)}) collective-permute-start(bf16[3,8,16,256]{3,2,1,0:T(8,128)(2,1)S(1)} %pad_maximum_fusion), channel_id=1, source_target_pairs={{0,4},{4,0},{8,12},{12,8},{16,20},{20,16},{24,28},{28,24},{1,5},{5... | collective-permute-start | bytes 589832 | tf_op jit(solution)/shard_map/ppermute | solution.py:204
  16.1 4.2 %collective-permute-done.7 = bf16[3,8,16,256]{3,2,1,0:T(8,128)(2,1)S(1)} collective-permute-done((bf16[3,8,16,256]{3,2,1,0:T(8,128)(2,1)S(1)}, bf16[3,8,16,256]{3,2,1,0:T(8,128)(2,1)S(1)}, u32[]{:S(2)}, u32[]{:S(2)}) %collective-permute-start.7) | collective-permute-done | bytes 196640 | tf_op jit(solution)/shard_map/ppermute | solution.py:204
  20.3 5.6 %expectation.1 = (f32[16,64]{1,0:T(8,128)}, bf16[8,8,16,256]{3,2,1,0:T(8,128)(2,1)}) custom-call(s32[8]{0:T(128)S(1)} %broadcast_xor_fusion.slabs_ref, s32[8,8]{1,0:T(8,128)S(1)} %bitcast.27, s32[4,16]{1,0:T(4,128)S(1)} %bitcast.28, f32[128,128]{1,0:T(8,128)S(1)} %copy-done.2, bf16[256,128]{1,0:T(8,128)(2,1)S(1)} %copy-done.3, ...), custom_call_target="tpu_custom_call" | custom-call | flops 134217728 | bytes 3145728 | tf_op jit(solution)/shard_map/expectation/pallas_call | solution.py:175
  26.0 4.0 %all-to-all-start = ((bf16[8,8,16,256]{3,2,1,0:T(8,128)(2,1)}), bf16[8,8,16,256]{3,2,1,0:T(8,128)(2,1)S(1)}, u32[]{:S(2)}, u32[]{:S(2)}) async-start(bf16[8,8,16,256]{3,2,1,0:T(8,128)(2,1)} %get-tuple-element.4), calls=%async_computation | async-start | bytes 1048576 | tf_op jit(solution)/shard_map/all_to_all | solution.py:228
  30.0 0.1 collective-permute-start
  30.1 1.6 %collective-permute-start.1 = (bf16[128,512]{1,0:T(8,128)(2,1)S(1)}, bf16[128,512]{1,0:T(8,128)(2,1)S(1)}, u32[]{:S(2)}, u32[]{:S(2)}) collective-permute-start(bf16[128,512]{1,0:T(8,128)(2,1)S(1)} %bitcast.31), channel_id=1, source_target_pairs={{0,2},{1,3},{2,0},{3,1},{4,6},{5,7},{6,4},{7,5},{8,10},{9,11},{10,... | collective-permute-start | bytes 393224 | tf_op jit(solution)/shard_map/ppermute | solution.py:198
  31.7 1.4 %collective-permute-start.2 = (bf16[128,512]{1,0:T(8,128)(2,1)S(1)}, bf16[128,512]{1,0:T(8,128)(2,1)S(1)}, u32[]{:S(2)}, u32[]{:S(2)}) collective-permute-start(bf16[128,512]{1,0:T(8,128)(2,1)S(1)} %bitcast.32), channel_id=1, source_target_pairs={{0,3},{1,0},{2,1},{3,2},{4,7},{5,4},{6,5},{7,6},{8,11},{9,8},{10,9... | collective-permute-start | bytes 393224 | tf_op jit(solution)/shard_map/ppermute | solution.py:198
  33.0 9.2 %all-to-all-done = bf16[8,8,16,256]{3,2,1,0:T(8,128)(2,1)S(1)} async-done(((bf16[8,8,16,256]{3,2,1,0:T(8,128)(2,1)}), bf16[8,8,16,256]{3,2,1,0:T(8,128)(2,1)S(1)}, u32[]{:S(2)}, u32[]{:S(2)}) %all-to-all-start) | async-done | bytes 524320 | tf_op jit(solution)/shard_map/all_to_all | solution.py:228
  42.2 0.1 reduce_sum.12
  42.3 0.1 collective-permute-start.10
  42.4 0.5 %collective-permute-start.8 = (bf16[128,256]{1,0:T(8,128)(2,1)S(1)}, bf16[128,256]{1,0:T(8,128)(2,1)S(1)}, u32[]{:S(2)}, u32[]{:S(2)}) collective-permute-start(bf16[128,256]{1,0:T(8,128)(2,1)S(1)} %bitcast.35), channel_id=1, source_target_pairs={{0,1},{1,2},{2,3},{3,0},{4,5},{5,6},{6,7},{7,4},{8,9},{9,10},{10,1... | collective-permute-start | bytes 196616 | tf_op jit(solution)/shard_map/ppermute | solution.py:198
  42.9 0.0 collective-permute-done
  42.9 1.5 %collective-permute-start.9 = (bf16[128,256]{1,0:T(8,128)(2,1)S(1)}, bf16[128,256]{1,0:T(8,128)(2,1)S(1)}, u32[]{:S(2)}, u32[]{:S(2)}) collective-permute-start(bf16[128,256]{1,0:T(8,128)(2,1)S(1)} %bitcast.36), channel_id=1, source_target_pairs={{0,2},{1,3},{2,0},{3,1},{4,6},{5,7},{6,4},{7,5},{8,10},{9,11},{10,... | collective-permute-start | bytes 196616 | tf_op jit(solution)/shard_map/ppermute | solution.py:198
  44.4 0.0 collective-permute-done.1
  44.4 0.0 collective-permute-done.2
  44.4 0.0 collective-permute-done.10
  44.4 2.4 %collective-permute-done.8 = bf16[128,256]{1,0:T(8,128)(2,1)S(1)} collective-permute-done((bf16[128,256]{1,0:T(8,128)(2,1)S(1)}, bf16[128,256]{1,0:T(8,128)(2,1)S(1)}, u32[]{:S(2)}, u32[]{:S(2)}) %collective-permute-start.8) | collective-permute-done | bytes 65568 | tf_op jit(solution)/shard_map/ppermute | solution.py:198
  46.8 1.4 %collective-permute-done.9 = bf16[128,256]{1,0:T(8,128)(2,1)S(1)} collective-permute-done((bf16[128,256]{1,0:T(8,128)(2,1)S(1)}, bf16[128,256]{1,0:T(8,128)(2,1)S(1)}, u32[]{:S(2)}, u32[]{:S(2)}) %collective-permute-start.9) | collective-permute-done | bytes 65568 | tf_op jit(solution)/shard_map/ppermute | solution.py:198
  48.2 1.1 %convolution_multiply_fusion = f32[512,256]{1,0:T(8,128)} fusion(bf16[128,512]{1,0:T(8,128)(2,1)S(1)} %collective-permute-done.2, bf16[128,512]{1,0:T(8,128)(2,1)S(1)} %collective-permute-done.1, bf16[128,512]{1,0:T(8,128)(2,1)S(1)} %collective-permute-done, bf16[128,512]{1,0:T(8,128)(2,1)S(1)} %bitcast.33, bf16[128,256]{1,0:T(8,128)(2,1)S(1)} %collective-permute-done.10, ...), kind=kOutput, calls=%fused_computation | convolution fusion | flops 137494528 | bytes 1310720 | tf_op jit(solution)/shard_map/dot_general | solution.py:232
  (20 shorter events, 0.1 us)
Async XLA Ops:
  0.6 1.0 %copy-start = (bf16[512,256]{1,0:T(8,128)(2,1)S(1)}, bf16[512,256]{1,0:T(8,128)(2,1)}, u32[]{:S(2)}) copy-start(bf16[512,256]{1,0:T(8,128)(2,1)} %param.10) | copy-start | bytes 786436
  0.6 15.4 %copy-start.9 = (s32[8]{0:T(128)S(1)}, s32[8]{0:T(128)}, u32[]{:S(2)}) copy-start(s32[8]{0:T(128)} %constant.20.clone) | copy-start | bytes 100
  1.6 18.7 %copy-start.2 = (f32[128,128]{1,0:T(8,128)S(1)}, f32[128,128]{1,0:T(8,128)}, u32[]{:S(2)}) copy-start(f32[128,128]{1,0:T(8,128)} %constant.21.clone.row_ref) | copy-start | bytes 196612
  1.6 18.7 %copy-start.3 = (bf16[256,128]{1,0:T(8,128)(2,1)S(1)}, bf16[256,128]{1,0:T(8,128)(2,1)}, u32[]{:S(2)}) copy-start(bf16[256,128]{1,0:T(8,128)(2,1)} %constant.22.clone.fwd_ref) | copy-start | bytes 196612
  1.6 18.7 %copy-start.4 = (bf16[128,256]{1,0:T(8,128)(2,1)S(1)}, bf16[128,256]{1,0:T(8,128)(2,1)}, u32[]{:S(2)}) copy-start(bf16[128,256]{1,0:T(8,128)(2,1)} %constant.23.clone.back_ref) | copy-start | bytes 196612
  1.6 18.7 %copy-start.5 = (s32[1,8,8]{2,1,0:T(8,128)S(1)}, s32[1,8,8]{2,1,0:T(8,128)}, u32[]{:S(2)}) copy-start(s32[1,8,8]{2,1,0:T(8,128)} %param.12) | copy-start | bytes 772
  1.6 18.7 %copy-start.6 = (s32[1,16,4]{1,2,0:T(4,128)S(1)}, s32[1,16,4]{1,2,0:T(4,128)}, u32[]{:S(2)}) copy-start(s32[1,16,4]{1,2,0:T(4,128)} %param.15) | copy-start | bytes 772
  2.7 10.9 %collective-permute-start.3 = (bf16[8,16,256]{2,1,0:T(8,128)(2,1)S(1)}, bf16[8,16,256]{2,1,0:T(8,128)(2,1)S(1)}, u32[]{:S(2)}, u32[]{:S(2)}) collective-permute-start(bf16[8,16,256]{2,1,0:T(8,128)(2,1)S(1)} %bitcast.19), channel_id=1, source_target_pairs={{0,8},{4,12},{8,0},{12,4},{16,24},{20,28},{24,16},{28,20},{1,9},{5... | collective-permute-start | bytes 196616 | tf_op jit(solution)/shard_map/ppermute | solution.py:204
  5.8 7.8 %collective-permute-start.4 = (bf16[8,16,256]{2,1,0:T(8,128)(2,1)S(1)}, bf16[8,16,256]{2,1,0:T(8,128)(2,1)S(1)}, u32[]{:S(2)}, u32[]{:S(2)}) collective-permute-start(bf16[8,16,256]{2,1,0:T(8,128)(2,1)S(1)} %bitcast.20), channel_id=1, source_target_pairs={{0,16},{4,20},{8,24},{12,28},{16,0},{20,4},{24,8},{28,12},{1,17},{... | collective-permute-start | bytes 196616 | tf_op jit(solution)/shard_map/ppermute | solution.py:204
  8.4 6.1 %collective-permute-start.5 = (bf16[8,16,256]{2,1,0:T(8,128)(2,1)S(1)}, bf16[8,16,256]{2,1,0:T(8,128)(2,1)S(1)}, u32[]{:S(2)}, u32[]{:S(2)}) collective-permute-start(bf16[8,16,256]{2,1,0:T(8,128)(2,1)S(1)} %bitcast.21), channel_id=1, source_target_pairs={{0,24},{4,28},{8,16},{12,20},{16,8},{20,12},{24,0},{28,4},{1,25},{... | collective-permute-start | bytes 196616 | tf_op jit(solution)/shard_map/ppermute | solution.py:204
  8.4 11.9 %collective-permute-start.6 = (bf16[8,16,256]{2,1,0:T(8,128)(2,1)S(1)}, bf16[8,16,256]{2,1,0:T(8,128)(2,1)S(1)}, u32[]{:S(2)}, u32[]{:S(2)}) collective-permute-start(bf16[8,16,256]{2,1,0:T(8,128)(2,1)S(1)} %bitcast.22), channel_id=1, source_target_pairs={{0,4},{4,0},{8,12},{12,8},{16,20},{20,16},{24,28},{28,24},{1,5},{5... | collective-permute-start | bytes 196616 | tf_op jit(solution)/shard_map/ppermute | solution.py:204
  10.1 1.2 %copy-start.1 = (bf16[1,16,128,256]{3,2,1,0:T(8,128)(2,1)S(1)}, bf16[1,16,128,256]{3,2,1,0:T(8,128)(2,1)}, u32[]{:S(2)}) copy-start(bf16[1,16,128,256]{3,2,1,0:T(8,128)(2,1)} %image_ref.1) | copy-start | bytes 3145732
  11.4 0.7 %copy-start.7 = (f32[1,16]{1,0:T(1,128)S(1)}, f32[1,16]{1,0:T(1,128)}, u32[]{:S(2)}) copy-start(f32[1,16]{1,0:T(1,128)} %defocus_ref.1) | copy-start | bytes 196
  14.5 5.7 %collective-permute-start.7 = (bf16[3,8,16,256]{3,2,1,0:T(8,128)(2,1)S(1)}, bf16[3,8,16,256]{3,2,1,0:T(8,128)(2,1)S(1)}, u32[]{:S(2)}, u32[]{:S(2)}) collective-permute-start(bf16[3,8,16,256]{3,2,1,0:T(8,128)(2,1)S(1)} %pad_maximum_fusion), channel_id=1, source_target_pairs={{0,4},{4,0},{8,12},{12,8},{16,20},{20,16},{24,28},{28,24},{1,5},{5... | collective-permute-start | bytes 589832 | tf_op jit(solution)/shard_map/ppermute | solution.py:204
  16.1 13.9 %copy-start.8 = (bf16[1,8,16,512]{3,2,1,0:T(8,128)(2,1)S(1)}, bf16[1,8,16,512]{3,2,1,0:T(8,128)(2,1)}, u32[]{:S(2)}) copy-start(bf16[1,8,16,512]{3,2,1,0:T(8,128)(2,1)} %param.11) | copy-start | bytes 393220
  26.0 16.3 %all-to-all-start = ((bf16[8,8,16,256]{3,2,1,0:T(8,128)(2,1)}), bf16[8,8,16,256]{3,2,1,0:T(8,128)(2,1)S(1)}, u32[]{:S(2)}, u32[]{:S(2)}) async-start(bf16[8,8,16,256]{3,2,1,0:T(8,128)(2,1)} %get-tuple-element.4), calls=%async_computation | async-start | bytes 1048576 | tf_op jit(solution)/shard_map/all_to_all | solution.py:228
  30.0 12.9 %collective-permute-start = (bf16[128,512]{1,0:T(8,128)(2,1)S(1)}, bf16[128,512]{1,0:T(8,128)(2,1)S(1)}, u32[]{:S(2)}, u32[]{:S(2)}) collective-permute-start(bf16[128,512]{1,0:T(8,128)(2,1)S(1)} %bitcast.30), channel_id=1, source_target_pairs={{0,1},{1,2},{2,3},{3,0},{4,5},{5,6},{6,7},{7,4},{8,9},{9,10},{10,1... | collective-permute-start | bytes 393224 | tf_op jit(solution)/shard_map/ppermute | solution.py:198
  30.1 14.3 %collective-permute-start.1 = (bf16[128,512]{1,0:T(8,128)(2,1)S(1)}, bf16[128,512]{1,0:T(8,128)(2,1)S(1)}, u32[]{:S(2)}, u32[]{:S(2)}) collective-permute-start(bf16[128,512]{1,0:T(8,128)(2,1)S(1)} %bitcast.31), channel_id=1, source_target_pairs={{0,2},{1,3},{2,0},{3,1},{4,6},{5,7},{6,4},{7,5},{8,10},{9,11},{10,... | collective-permute-start | bytes 393224 | tf_op jit(solution)/shard_map/ppermute | solution.py:198
  31.7 12.7 %collective-permute-start.2 = (bf16[128,512]{1,0:T(8,128)(2,1)S(1)}, bf16[128,512]{1,0:T(8,128)(2,1)S(1)}, u32[]{:S(2)}, u32[]{:S(2)}) collective-permute-start(bf16[128,512]{1,0:T(8,128)(2,1)S(1)} %bitcast.32), channel_id=1, source_target_pairs={{0,3},{1,0},{2,1},{3,2},{4,7},{5,4},{6,5},{7,6},{8,11},{9,8},{10,9... | collective-permute-start | bytes 393224 | tf_op jit(solution)/shard_map/ppermute | solution.py:198
  42.3 2.1 %collective-permute-start.10 = (bf16[128,256]{1,0:T(8,128)(2,1)S(1)}, bf16[128,256]{1,0:T(8,128)(2,1)S(1)}, u32[]{:S(2)}, u32[]{:S(2)}) collective-permute-start(bf16[128,256]{1,0:T(8,128)(2,1)S(1)} %bitcast.34), channel_id=1, source_target_pairs={{0,3},{1,0},{2,1},{3,2},{4,7},{5,4},{6,5},{7,6},{8,11},{9,8},{10,9... | collective-permute-start | bytes 196616 | tf_op jit(solution)/shard_map/ppermute | solution.py:198
  42.4 4.4 %collective-permute-start.8 = (bf16[128,256]{1,0:T(8,128)(2,1)S(1)}, bf16[128,256]{1,0:T(8,128)(2,1)S(1)}, u32[]{:S(2)}, u32[]{:S(2)}) collective-permute-start(bf16[128,256]{1,0:T(8,128)(2,1)S(1)} %bitcast.35), channel_id=1, source_target_pairs={{0,1},{1,2},{2,3},{3,0},{4,5},{5,6},{6,7},{7,4},{8,9},{9,10},{10,1... | collective-permute-start | bytes 196616 | tf_op jit(solution)/shard_map/ppermute | solution.py:198
  42.9 5.3 %collective-permute-start.9 = (bf16[128,256]{1,0:T(8,128)(2,1)S(1)}, bf16[128,256]{1,0:T(8,128)(2,1)S(1)}, u32[]{:S(2)}, u32[]{:S(2)}) collective-permute-start(bf16[128,256]{1,0:T(8,128)(2,1)S(1)} %bitcast.36), channel_id=1, source_target_pairs={{0,2},{1,3},{2,0},{3,1},{4,6},{5,7},{6,4},{7,5},{8,10},{9,11},{10,... | collective-permute-start | bytes 196616 | tf_op jit(solution)/shard_map/ppermute | solution.py:198

commit v3 on v2

--- a/solution.py
+++ b/solution.py
@@ -16,6 +16,9 @@
 amplitude = 0.1
 grid_side = 4
 LANES = 128
+VMEM_LIMIT = 32 << 20
+SMEM = pl.BlockSpec(memory_space=pltpu.SMEM)
+VMEM = pl.BlockSpec(memory_space=pltpu.VMEM)
 DIRECT_BYTES = 4 << 20
 
 
@@ -75,10 +78,10 @@
 
     return pl.pallas_call(
         kernel,
-        out_shape=jax.ShapeDtypeStruct(images.shape[1:], jnp.float32),
-        in_specs=[pl.BlockSpec(memory_space=pltpu.SMEM), pl.BlockSpec(memory_space=pltpu.VMEM)],
-        out_specs=pl.BlockSpec(memory_space=pltpu.VMEM),
-        compiler_params=pltpu.CompilerParams(vmem_limit_bytes=24 << 20),
+        out_shape=pltpu.VMEM(images.shape[1:], jnp.float32),
+        in_specs=[SMEM, VMEM],
+        out_specs=VMEM,
+        compiler_params=pltpu.CompilerParams(vmem_limit_bytes=VMEM_LIMIT),
         cost_estimate=pl.CostEstimate(
             flops=30 * count * fourier * fourier, bytes_accessed=6 * count * fourier * width, transcendentals=0
         ),
@@ -86,34 +89,29 @@
     )(defocus, images)
 
 
-def expectation(tables, u, parts, slabs, block_index, orient):
-    count, fourier, width = u.shape
-    orient_count, block_rows, _ = parts[0].shape
-    slab_count = len(parts)
-    picks = orient.shape[0]
-    row_table, col_fwd, col_back = tables
-
-    def kernel(slabs_ref, index_ref, orient_ref, row_ref, fwd_ref, back_ref, u_ref, *rest):
-        part_refs = rest[:slab_count]
-        weights_ref, rows_ref, panel, total, score = rest[slab_count:]
-        panel[...] = jnp.zeros_like(panel)
-        for part in range(slab_count):
-            slab = slabs_ref[part]
-            for j in range(orient_count):
-                where = pl.ds(pl.multiple_of(index_ref[j, slab] * block_rows, block_rows), block_rows)
-                panel[j, where, :] += part_refs[part][j].astype(jnp.float32)
-        for j in range(orient_count):
-            panel[j] = panel[j].astype(jnp.bfloat16).astype(jnp.float32)
-        total[...] = jnp.zeros_like(total)
-
-        def forward(i, _):
-            real_u = u_ref[i, :, :fourier]
-            imag_u = u_ref[i, :, fourier:]
-            products = []
-            for k in range(picks):
-                j = orient_ref[k, i]
-                real_p = panel[j, :, :fourier]
-                imag_p = panel[j, :, fourier:]
+class Reach:
+    def __init__(self, me_ref, index_ref, block_rows):
+        self.me, self.index, self.block_rows = me_ref[0], index_ref, block_rows
+
+    def __call__(self, j, flip):
+        block = self.index[j, jnp.bitwise_xor(self.me, flip)]
+        return pl.ds(pl.multiple_of(block * self.block_rows, self.block_rows), self.block_rows)
+
+
+def add_up_scores(reach, flips, orient_ref, row_ref, fwd_ref, u_ref, part_refs, store):
+    count, fourier = u_ref.shape[0], u_ref.shape[1]
+    picks = orient_ref.shape[0]
+    rows = reach.block_rows
+    for i in range(count):
+        products, row_parts = [], []
+        for k in range(picks):
+            j = orient_ref[k, i]
+            for flip, part_ref in zip(flips, part_refs):
+                where = reach(j, flip)
+                real_u = u_ref[i, where, :fourier]
+                imag_u = u_ref[i, where, fourier:]
+                real_p = part_ref[j, :, :fourier].astype(jnp.float32)
+                imag_p = part_ref[j, :, fourier:].astype(jnp.float32)
                 products.append(
                     jnp.concatenate(
                         [
@@ -123,19 +121,88 @@
                         axis=1,
                     )
                 )
-            by_row = jnp.dot(
-                jnp.concatenate(products, axis=0), fwd_ref[...], preferred_element_type=jnp.float32
-            )
-            for k in range(picks):
-                mixed = by_row[k * fourier : (k + 1) * fourier] * row_ref[...]
-                score[k, pl.ds(i, 1), :] = jnp.sum(mixed, axis=0, keepdims=True)
-            return 0
-
-        lax.fori_loop(0, count, forward, 0, unroll=True)
-
+                row_parts.append(row_ref[where, :])
+        by_row = jnp.dot(jnp.concatenate(products, axis=0), fwd_ref[...], preferred_element_type=jnp.float32)
+        for k in range(picks):
+            mixed = 0.0
+            for s in range(len(flips)):
+                at = k * len(flips) + s
+                mixed = mixed + by_row[at * rows : (at + 1) * rows] * row_parts[at]
+            store(k, i, jnp.sum(mixed, axis=0, keepdims=True))
+
+
+def add_up_slices(reach, flips, orient_ref, row_ref, back_ref, u_ref, rounded_ref, total):
+    count, fourier = u_ref.shape[0], u_ref.shape[1]
+    picks = orient_ref.shape[0]
+    rows = reach.block_rows
+    total[...] = jnp.zeros_like(total)
+    for i in range(count):
+        mixed = []
+        for k in range(picks):
+            j = orient_ref[k, i]
+            weight = rounded_ref[k, i : i + 1, :]
+            for flip in flips:
+                mixed.append((row_ref[reach(j, flip), :] * weight).astype(jnp.bfloat16))
+        spread = jnp.dot(jnp.concatenate(mixed, axis=0), back_ref[...], preferred_element_type=jnp.float32)
+        for k in range(picks):
+            j = orient_ref[k, i]
+            for s, flip in enumerate(flips):
+                where = reach(j, flip)
+                at = (k * len(flips) + s) * rows
+                real_u = u_ref[i, where, :fourier]
+                imag_u = u_ref[i, where, fourier:]
+                real_e = spread[at : at + rows, :fourier]
+                imag_e = spread[at : at + rows, fourier:]
+                total[s, j, :, :fourier] += real_u * real_e - imag_u * imag_e
+                total[s, j, :, fourier:] += real_u * imag_e + imag_u * real_e
+
+
+def first_scores(me, block_index, orient, tables, u, parts, flips):
+    count, fourier, width = u.shape
+    picks = orient.shape[0]
+    block_rows = parts[0].shape[1]
+
+    def kernel(me_ref, index_ref, orient_ref, row_ref, fwd_ref, u_ref, *rest):
+        part_refs, score_ref = rest[:-1], rest[-1]
+        reach = Reach(me_ref, index_ref, block_rows)
+
+        def store(k, i, value):
+            score_ref[k, i : i + 1, :] = value
+
+        add_up_scores(reach, flips, orient_ref, row_ref, fwd_ref, u_ref, part_refs, store)
+
+    return pl.pallas_call(
+        kernel,
+        out_shape=pltpu.VMEM((picks, count, LANES), jnp.float32),
+        in_specs=[SMEM] * 3 + [VMEM] * (3 + len(parts)),
+        out_specs=VMEM,
+        compiler_params=pltpu.CompilerParams(vmem_limit_bytes=VMEM_LIMIT),
+        cost_estimate=pl.CostEstimate(
+            flops=len(parts) * count * picks * block_rows * width * LANES * 2,
+            bytes_accessed=4 * count * fourier * width,
+            transcendentals=0,
+        ),
+        name="first_scores",
+    )(me, block_index, orient, *tables[:2], u, *parts)
+
+
+def expectation(me, block_index, orient, tables, u, parts, flips, scores, out_flips):
+    count, fourier, width = u.shape
+    picks = orient.shape[0]
+    orient_count, block_rows, _ = parts[0].shape
+
+    def kernel(me_ref, index_ref, orient_ref, row_ref, fwd_ref, back_ref, u_ref, score_ref, *rest):
+        part_refs = rest[: len(parts)]
+        weights_ref, rounded_ref, rows_ref, total = rest[len(parts) :]
+        reach = Reach(me_ref, index_ref, block_rows)
+
+        def store(k, i, value):
+            rounded_ref[k, i : i + 1, :] = value
+
+        add_up_scores(reach, flips, orient_ref, row_ref, fwd_ref, u_ref, part_refs, store)
         squared = []
         for k in range(picks):
-            value = score[k]
+            value = rounded_ref[k] + score_ref[k]
             value = value + pltpu.roll(value, 2 * NS, 1)
             value = value + pltpu.roll(value, NS, 1)
             value = value * (1.0 / fourier)
@@ -147,95 +214,122 @@
         for k in range(picks):
             value = squared[k] * scale
             merged = jnp.where(lane == k, value, merged)
-            score[k] = value.astype(jnp.bfloat16).astype(jnp.float32)
-        weights_ref[...] = merged[:, : picks * NS]
-
-        def backward(i, _):
-            real_u = u_ref[i, :, :fourier]
-            imag_u = u_ref[i, :, fourier:]
-            mixed = [(row_ref[...] * score[k, pl.ds(i, 1), :]).astype(jnp.bfloat16) for k in range(picks)]
-            spread = jnp.dot(jnp.concatenate(mixed, axis=0), back_ref[...], preferred_element_type=jnp.float32)
-            for k in range(picks):
-                j = orient_ref[k, i]
-                real_e = spread[k * fourier : (k + 1) * fourier, :fourier]
-                imag_e = spread[k * fourier : (k + 1) * fourier, fourier:]
-                total[j, :, :fourier] += real_u * real_e - imag_u * imag_e
-                total[j, :, fourier:] += real_u * imag_e + imag_u * real_e
-            return 0
-
-        lax.fori_loop(0, count, backward, 0, unroll=True)
-
-        for slab in range(slab_count):
-            for j in range(orient_count):
-                where = pl.ds(pl.multiple_of(index_ref[j, slab] * block_rows, block_rows), block_rows)
-                rows_ref[slab, j] = total[j, where, :].astype(jnp.bfloat16)
-
-    smem = pl.BlockSpec(memory_space=pltpu.SMEM)
-    vmem = pl.BlockSpec(memory_space=pltpu.VMEM)
+            rounded_ref[k] = value.astype(jnp.bfloat16).astype(jnp.float32)
+        weights_ref[0] = merged[:, : picks * NS]
+        add_up_slices(reach, out_flips, orient_ref, row_ref, back_ref, u_ref, rounded_ref, total)
+        rows_ref[...] = total[...].astype(jnp.bfloat16)
+
     return pl.pallas_call(
         kernel,
         out_shape=(
-            jax.ShapeDtypeStruct((count, picks * NS), jnp.float32),
-            jax.ShapeDtypeStruct((slab_count, orient_count, block_rows, width), jnp.bfloat16),
-        ),
-        in_specs=[smem] * 3 + [vmem] * (4 + slab_count),
-        out_specs=(vmem, vmem),
-        scratch_shapes=[
-            pltpu.VMEM((orient_count, fourier, width), jnp.float32),
-            pltpu.VMEM((orient_count, fourier, width), jnp.float32),
+            pltpu.VMEM((1, count, picks * NS), jnp.float32),
             pltpu.VMEM((picks, count, LANES), jnp.float32),
-        ],
-        compiler_params=pltpu.CompilerParams(vmem_limit_bytes=32 << 20),
+            pltpu.VMEM((len(out_flips), orient_count, block_rows, width), jnp.bfloat16),
+        ),
+        in_specs=[SMEM] * 3 + [VMEM] * (5 + len(parts)),
+        out_specs=(VMEM,) * 3,
+        scratch_shapes=[pltpu.VMEM((len(out_flips), orient_count, block_rows, width), jnp.float32)],
+        compiler_params=pltpu.CompilerParams(vmem_limit_bytes=VMEM_LIMIT),
         cost_estimate=pl.CostEstimate(
-            flops=64 * count * picks * fourier * width, bytes_accessed=6 * count * fourier * width, transcendentals=0
+            flops=(len(parts) + len(out_flips)) * count * picks * block_rows * width * LANES * 2,
+            bytes_accessed=4 * count * fourier * width,
+            transcendentals=0,
         ),
         name="expectation",
-    )(slabs, block_index, orient, row_table, col_fwd, col_back, u, *parts)
-
-
-def exchange(value, axis, size):
-    return [
-        lax.ppermute(value, axis, [(source, (source + step) % size) for source in range(size)])
-        for step in range(1, size)
-    ]
+    )(me, block_index, orient, *tables, u, scores, *parts)
+
+
+def last_slices(me, block_index, orient, tables, u, rounded, block_rows, out_flips):
+    count, fourier, width = u.shape
+    picks = orient.shape[0]
+    orient_count = block_index.shape[0]
+
+    def kernel(me_ref, index_ref, orient_ref, row_ref, back_ref, u_ref, rounded_ref, rows_ref, total):
+        reach = Reach(me_ref, index_ref, block_rows)
+        add_up_slices(reach, out_flips, orient_ref, row_ref, back_ref, u_ref, rounded_ref, total)
+        rows_ref[...] = total[...].astype(jnp.bfloat16)
+
+    return pl.pallas_call(
+        kernel,
+        out_shape=pltpu.VMEM((len(out_flips), orient_count, block_rows, width), jnp.bfloat16),
+        in_specs=[SMEM] * 3 + [VMEM] * 4,
+        out_specs=VMEM,
+        scratch_shapes=[pltpu.VMEM((len(out_flips), orient_count, block_rows, width), jnp.float32)],
+        compiler_params=pltpu.CompilerParams(vmem_limit_bytes=VMEM_LIMIT),
+        cost_estimate=pl.CostEstimate(
+            flops=len(out_flips) * count * picks * block_rows * width * LANES * 2,
+            bytes_accessed=4 * count * fourier * width,
+            transcendentals=0,
+        ),
+        name="last_slices",
+    )(me, block_index, orient, tables[0], tables[2], u, rounded)
 
 
 def swap(value, axis, size, flip):
     return lax.ppermute(value, axis, [(source, source ^ flip) for source in range(size)])
+
+
+def together(*values):
+    return sum(value.astype(jnp.float32) for value in values).astype(jnp.bfloat16)
 
 
 def direct(volume, interp, block_index, images, defocus, orient):
     slab_count = lax.axis_size("slab")
     group_count = lax.axis_size("img")
-    slab_index = lax.axis_index("slab")
     orient_count, block_rows, slab_rows = interp.shape[1:]
-    fourier = images.shape[2]
-    width = images.shape[3]
+    fourier, width = images.shape[2:]
     image_count = images.shape[1] * slab_count
+    near, far, other, side = 2, 4, 6, 1
+
+    def to(value, flip):
+        return swap(value, "slab", slab_count, flip)
+
     weigher = interp[0].reshape(orient_count * block_rows, slab_rows)
-    partial_value = jnp.dot(weigher, volume, preferred_element_type=jnp.float32).astype(jnp.bfloat16)
-    partial_value = partial_value.reshape(orient_count, block_rows, width)
-    same_x = [partial_value] + [swap(partial_value, "slab", slab_count, flip) for flip in range(2, slab_count, 2)]
-    other_x = [swap(partial_value, "slab", slab_count, 1)]
-    passed_on = swap(jnp.stack(same_x[1:]), "slab", slab_count, 1)
-    other_x += [passed_on[i] for i in range(slab_count // 2 - 1)]
-    parts = same_x + other_x
-    flips = list(range(0, slab_count, 2)) + list(range(1, slab_count, 2))
-    slabs = jnp.bitwise_xor(slab_index, jnp.array(flips, jnp.int32))
-    weighers = [weigher] + exchange(weigher, "img", group_count)
+    own = jnp.dot(weigher, volume, preferred_element_type=jnp.float32).astype(jnp.bfloat16)
+    own = own.reshape(orient_count, block_rows, width)
+    from_other, from_far, from_near, from_side = (to(own, flip) for flip in (other, far, near, side))
+    from_near_side = to(from_near, side)
     u = weigh_images(images, defocus)
-    weights, rows = expectation(separable_tables(fourier), u, parts, slabs, block_index[0], orient[0].T)
-    arrived = lax.all_to_all(rows, "slab", split_axis=0, concat_axis=0, tiled=True)
-    back = jnp.sum(arrived.astype(jnp.float32), axis=0).astype(jnp.bfloat16)
-    back = back.reshape(orient_count * block_rows, width)
-    backs = [back] + exchange(back, "img", group_count)
+    from_far, u = lax.optimization_barrier((from_far, u))
+    from_other, _ = lax.optimization_barrier((from_other, from_far))
+    from_far_side, from_other_side = to(from_far, side), to(from_other, side)
+
+    common = lax.axis_index("slab").astype(jnp.int32).reshape(1), block_index[0], orient[0].T, separable_tables(fourier), u
+    scores = first_scores(*common, [own, from_near, from_far, from_other, from_side, from_near_side], (0, near, far, other, side, near + side))
+    late_weigher, scores = lax.optimization_barrier((weigher, scores))
+    weigher_across = swap(late_weigher, "img", group_count, 2)
+    weights, rounded, side_rows = expectation(
+        *common,
+        [from_far_side, from_other_side],
+        (far + side, other + side),
+        scores,
+        (other + side, far + side, near + side, side),
+    )
+    first = to(side_rows[0], side)
+    rest = to(side_rows[1:], side)
+    weigher_across, rounded = lax.optimization_barrier((weigher_across, rounded))
+    rows = last_slices(*common, rounded, block_rows, (other, far, near, 0))
+    back = together(
+        rows[3],
+        rest[2],
+        to(together(rows[0], first), other),
+        to(together(rows[1], rest[0]), far),
+        to(together(rows[2], rest[1]), near),
+    ).reshape(orient_count * block_rows, width)
+
+    def all_groups(value):
+        across = swap(value, "img", group_count, 2)
+        return [value, swap(value, "img", group_count, 1), across, swap(across, "img", group_count, 1)]
+
+    weighers = [weigher, swap(weigher, "img", group_count, 1), weigher_across, swap(weigher_across, "img", group_count, 1)]
+    backs = all_groups(back)
     update = lax.dot_general(
         jnp.concatenate(weighers, axis=0),
         jnp.concatenate(backs, axis=0),
         (((0,), (0,)), ((), ())),
         preferred_element_type=jnp.float32,
     )
-    return update / math.sqrt(image_count), weights[None]
+    return update / math.sqrt(image_count), weights
 
 
 def phase_tables(fourier, shifts, box):
@@ -358,7 +452,7 @@
 def on_device(volume, interp, block_index, images, defocus, orient):
     orient_count, block_rows = interp.shape[1:3]
     gathered = lax.axis_size("slab") * orient_count * block_rows * images.shape[3] * 2
-    pairs = lax.axis_size("slab") == 8
+    pairs = lax.axis_size("slab") == 8 and lax.axis_size("img") == 4
     plan = direct if pairs and gathered <= DIRECT_BYTES else through_owners
     return plan(volume, interp, block_index, images, defocus, orient)
 

time: 49.6 us -> 44.4 us (0.90)
  waiting for transfers between devices: 18 us -> 7.53 us
  starting transfers between devices: 18.1 us -> 21.6 us
  Pallas kernels: 7.22 us -> 8.58 us
  local copies, waits for them, and re-layouts: 2.86 us -> 3.44 us
    ppermute x5 -> x18, starting transfers between devices: 8.94 us -> 21.6 us  [swap(): lax.ppermute(value, axis, [(source, source ^ flip) for source in range(si...]
    all_to_all x1 -> x0, waiting for transfers between devices: 9.17 us -> none  [direct(): lax.all_to_all(rows, 'slab', split_axis=0, concat_axis=0, tiled=True)]
    ppermute x6 -> x0, starting transfers between devices: 5.11 us -> none  [exchange(): lax.ppermute(value, axis, [(source, (source + step) % size) for source in...]
    all_to_all x1 -> x0, starting transfers between devices: 4.03 us -> none  [direct(): lax.all_to_all(rows, 'slab', split_axis=0, concat_axis=0, tiled=True)]
    ppermute x6 -> x0, waiting for transfers between devices: 3.83 us -> none  [exchange(): lax.ppermute(value, axis, [(source, (source + step) % size) for source in...]
    ppermute x5 -> x18, waiting for transfers between devices: 5.04 us -> 7.53 us  [swap(): lax.ppermute(value, axis, [(source, source ^ flip) for source in range(si...]
    pallas_call x2 -> x4, Pallas kernels: 7.22 us -> 8.58 us  [the longest x1 2.81 us: expectation(): pl.pallas_call(kernel, out_shape=(pltpu.VMEM((1, count, picks * NS), jnp....]
    unnamed x20 -> x19, local copies, waits for them, and re-layouts: 2.84 us -> 3.42 us
  transfers between devices with their start and end apart: 12 -> 18, of which waited for: 5 -> 6; matrix products, arithmetic and copies ran while one was open for 0% -> 2% of each run, Pallas kernels for 3% -> 19%
where the time goes in v3:
time: 44.4 us; the launch traced here: 44.2 us
  starting transfers between devices  21.6 us (49%)
  Pallas kernels  8.58 us (19%)
  waiting for transfers between devices  7.53 us (17%)
  local copies, waits for them, and re-layouts  3.44 us (8%)
  matrix products  2.22 us (5%)
  between operations  0.8 us (2%)
    ppermute x18, starting transfers between devices, swap(): lax.ppermute(value, axis, [(source, source ^ flip) for source in range(si...  21.6 us
    ppermute x18, waiting for transfers between devices, swap(): lax.ppermute(value, axis, [(source, source ^ flip) for source in range(si...  7.53 us
    unnamed x19, local copies, waits for them, and re-layouts  3.42 us
    pallas_call x1, Pallas kernels, expectation(): pl.pallas_call(kernel, out_shape=(pltpu.VMEM((1, count, picks * NS), jnp....  2.81 us
    pallas_call x1, Pallas kernels, first_scores(): pl.pallas_call(kernel, out_shape=pltpu.VMEM((picks, count, LANES), jnp.fl...  2.28 us
    pallas_call x1, Pallas kernels, last_slices(): pl.pallas_call(kernel, out_shape=pltpu.VMEM((len(out_flips), orient_count...  1.9 us
    pallas_call x1, Pallas kernels, weigh_images(): pl.pallas_call(kernel, out_shape=pltpu.VMEM(images.shape[1:], jnp.float32...  1.6 us
    dot_general x1, matrix products, direct(): lax.dot_general(jnp.concatenate(weighers, axis=0), jnp.concatenate(backs,...  1.13 us
  transfers between devices with their start and end apart: 18, of which 6 were waited for; matrix products, arithmetic and copies ran while one was open for 2% of the time, Pallas kernels for 19%

profile of v3, /device:TPU:0, one launch (start us, length us, event | category | flops | bytes accessed | tf_op | source)
XLA Modules:
  0.0 44.2 jit_solution(18059564497299891741)
XLA Ops:
  0.6 0.0 copy-start
  0.6 0.0 copy-start.2
  0.7 0.9 %copy-done = bf16[512,256]{1,0:T(8,128)(2,1)S(1)} copy-done((bf16[512,256]{1,0:T(8,128)(2,1)S(1)}, bf16[512,256]{1,0:T(8,128)(2,1)}, u32[]{:S(2)}) %copy-start) | copy-done | bytes 262168
  1.6 1.1 %convolution_convert_fusion = bf16[128,256]{1,0:T(8,128)(2,1)S(1)} fusion(bf16[128,512]{1,0:T(8,128)(2,1)} %bitcast.40, bf16[512,256]{1,0:T(8,128)(2,1)S(1)} %copy-done), kind=kOutput, calls=%fused_computation.1 | convolution fusion | flops 33587200 | bytes 458752 | tf_op jit(solution)/shard_map/dot_general | solution.py:288
  2.7 3.1 %collective-permute-start.2 = (bf16[8,16,256]{2,1,0:T(8,128)(2,1)S(1)}, bf16[8,16,256]{2,1,0:T(8,128)(2,1)S(1)}, u32[]{:S(2)}, u32[]{:S(2)}) collective-permute-start(bf16[8,16,256]{2,1,0:T(8,128)(2,1)S(1)} %bitcast.29), channel_id=1, source_target_pairs={{0,8},{4,12},{8,0},{12,4},{16,24},{20,28},{24,16},{28,20},{1,9},{5... | collective-permute-start | bytes 196616 | tf_op jit(solution)/shard_map/ppermute | solution.py:269
  5.8 2.6 %collective-permute-start.1 = (bf16[8,16,256]{2,1,0:T(8,128)(2,1)S(1)}, bf16[8,16,256]{2,1,0:T(8,128)(2,1)S(1)}, u32[]{:S(2)}, u32[]{:S(2)}) collective-permute-start(bf16[8,16,256]{2,1,0:T(8,128)(2,1)S(1)} %bitcast.30), channel_id=1, source_target_pairs={{0,16},{4,20},{8,24},{12,28},{16,0},{20,4},{24,8},{28,12},{1,17},{... | collective-permute-start | bytes 196616 | tf_op jit(solution)/shard_map/ppermute | solution.py:269
  8.4 1.7 %collective-permute-start.4 = (bf16[8,16,256]{2,1,0:T(8,128)(2,1)S(1)}, bf16[8,16,256]{2,1,0:T(8,128)(2,1)S(1)}, u32[]{:S(2)}, u32[]{:S(2)}) collective-permute-start(bf16[8,16,256]{2,1,0:T(8,128)(2,1)S(1)} %bitcast.32), channel_id=1, source_target_pairs={{0,4},{4,0},{8,12},{12,8},{16,20},{20,16},{24,28},{28,24},{1,5},{5... | collective-permute-start | bytes 196616 | tf_op jit(solution)/shard_map/ppermute | solution.py:269
  10.1 0.3 collective-permute-start.5
  10.4 1.2 %copy-done.1 = bf16[1,16,128,256]{3,2,1,0:T(8,128)(2,1)S(1)} copy-done((bf16[1,16,128,256]{3,2,1,0:T(8,128)(2,1)S(1)}, bf16[1,16,128,256]{3,2,1,0:T(8,128)(2,1)}, u32[]{:S(2)}) %copy-start.1) | copy-done | bytes 1048600
  11.6 0.7 %copy-done.7 = f32[1,16]{1,0:T(1,128)S(1)} copy-done((f32[1,16]{1,0:T(1,128)S(1)}, f32[1,16]{1,0:T(1,128)}, u32[]{:S(2)}) %copy-start.7) | copy-done | bytes 88
  12.3 1.6 %weigh_images.1.u_ref = f32[16,128,256]{2,1,0:T(8,128)S(1)} custom-call(f32[1,16]{1,0:T(1,128)S(1)} %copy-done.7, bf16[1,16,128,256]{3,2,1,0:T(8,128)(2,1)S(1)} %copy-done.1), custom_call_target="tpu_custom_call" | custom-call | flops 7864320 | bytes 3145728 | tf_op jit(solution)/shard_map/weigh_images/pallas_call | solution.py:79
  13.9 0.5 %collective-permute-done.3.rest_3_ = bf16[8,16,256]{2,1,0:T(8,128)(2,1)S(1)} collective-permute-done((bf16[8,16,256]{2,1,0:T(8,128)(2,1)S(1)}, bf16[8,16,256]{2,1,0:T(8,128)(2,1)S(1)}, u32[]{:S(2)}, u32[]{:S(2)}) %collective-permute-start.3) | collective-permute-done | bytes 65568 | tf_op jit(solution)/shard_map/ppermute | solution.py:269
  14.4 1.5 %collective-permute-start.8 = (bf16[8,16,256]{2,1,0:T(8,128)(2,1)S(1)}, bf16[8,16,256]{2,1,0:T(8,128)(2,1)S(1)}, u32[]{:S(2)}, u32[]{:S(2)}) collective-permute-start(bf16[8,16,256]{2,1,0:T(8,128)(2,1)S(1)} %collective-permute-done.3.rest_3_), channel_id=1, source_target_pairs={{0,4},{4,0},{8,12},{12,8},{16,20},{20,16},{24,28},{28,24},{1,5},{5... | collective-permute-start | bytes 196616 | tf_op jit(solution)/shard_map/ppermute | solution.py:269
  15.9 0.5 %collective-permute-start.7 = (bf16[8,16,256]{2,1,0:T(8,128)(2,1)S(1)}, bf16[8,16,256]{2,1,0:T(8,128)(2,1)S(1)}, u32[]{:S(2)}, u32[]{:S(2)}) collective-permute-start(bf16[8,16,256]{2,1,0:T(8,128)(2,1)S(1)} %collective-permute-done.1.rest_2_), channel_id=1, source_target_pairs={{0,4},{4,0},{8,12},{12,8},{16,20},{20,16},{24,28},{28,24},{1,5},{5... | collective-permute-start | bytes 196616 | tf_op jit(solution)/shard_map/ppermute | solution.py:269
  16.5 2.3 %first_scores.1.score_ref = f32[4,16,128]{2,1,0:T(8,128)S(1)} custom-call(s32[1]{0:T(128)} %bitcast.1.me_ref, s32[8,8]{1,0:T(8,128)S(1)} %bitcast.34, s32[4,16]{1,0:T(4,128)S(1)} %bitcast.37, f32[128,128]{1,0:T(8,128)S(1)} %copy-done.2, bf16[256,128]{1,0:T(8,128)(2,1)S(1)} %copy-done.4, f32[16,128,256]{2,1,0:T(8,128)S(1)} %weigh_images.1.u_ref, ...), custom_call_target="tpu_custom_call" | custom-call | flops 402653184 | bytes 2097152 | tf_op jit(solution)/shard_map/first_scores/pallas_call | solution.py:174
  18.8 1.6 %collective-permute-start.6 = (bf16[128,512]{1,0:T(8,128)(2,1)S(1)}, bf16[128,512]{1,0:T(8,128)(2,1)S(1)}, u32[]{:S(2)}, u32[]{:S(2)}) collective-permute-start(bf16[128,512]{1,0:T(8,128)(2,1)S(1)} %bitcast.41), channel_id=1, source_target_pairs={{0,2},{1,3},{2,0},{3,1},{4,6},{5,7},{6,4},{7,5},{8,10},{9,11},{10,... | collective-permute-start | bytes 393224 | tf_op jit(solution)/shard_map/ppermute | solution.py:269
  20.4 2.8 %expectation.1 = (f32[1,16,64]{2,1,0:T(8,128)S(1)}, f32[4,16,128]{2,1,0:T(8,128)S(1)}, bf16[4,8,16,256]{3,2,1,0:T(8,128)(2,1)S(1)}) custom-call(s32[1]{0:T(128)} %bitcast.1.me_ref, s32[8,8]{1,0:T(8,128)S(1)} %bitcast.35, s32[4,16]{1,0:T(4,128)S(1)} %bitcast.38, f32[128,128]{1,0:T(8,128)S(1)} %copy-done.2, bf16[256,128]{1,0:T(8,128)(2,1)S(1)} %copy-done.4, ...), custom_call_target="tpu_custom_call" | custom-call | flops 402653184 | bytes 2097152 | tf_op jit(solution)/shard_map/expectation/pallas_call | solution.py:222
  23.2 1.5 %collective-permute-start.11 = (bf16[8,16,256]{2,1,0:T(8,128)(2,1)S(1)}, bf16[8,16,256]{2,1,0:T(8,128)(2,1)S(1)}, u32[]{:S(2)}, u32[]{:S(2)}) collective-permute-start(bf16[8,16,256]{2,1,0:T(8,128)(2,1)S(1)} %slice_bitcast_fusion.1), channel_id=1, source_target_pairs={{0,4},{4,0},{8,12},{12,8},{16,20},{20,16},{24,28},{28,24},{1,5},{5... | collective-permute-start | bytes 196616 | tf_op jit(solution)/shard_map/ppermute | solution.py:269
  24.8 0.6 %collective-permute-start.10 = (bf16[3,8,16,256]{3,2,1,0:T(8,128)(2,1)S(1)}, bf16[3,8,16,256]{3,2,1,0:T(8,128)(2,1)S(1)}, u32[]{:S(2)}, u32[]{:S(2)}) collective-permute-start(bf16[3,8,16,256]{3,2,1,0:T(8,128)(2,1)S(1)} %slice.28), channel_id=1, source_target_pairs={{0,4},{4,0},{8,12},{12,8},{16,20},{20,16},{24,28},{28,24},{1,5},{5... | collective-permute-start | bytes 589832 | tf_op jit(solution)/shard_map/ppermute | solution.py:269
  25.4 1.9 %last_slices.1 = bf16[4,8,16,256]{3,2,1,0:T(8,128)(2,1)S(1)} custom-call(s32[1]{0:T(128)} %bitcast.1.me_ref, s32[8,8]{1,0:T(8,128)S(1)} %bitcast.36, s32[4,16]{1,0:T(4,128)S(1)} %bitcast.39, f32[128,128]{1,0:T(8,128)S(1)} %copy-done.2, bf16[128,256]{1,0:T(8,128)(2,1)S(1)} %copy-done.3, f32[16,128,256]{2,1,0:T(8,128)S(1)} %weigh_images.1.u_ref, ...), custom_call_target="tpu_custom_call" | custom-call | flops 268435456 | bytes 2097152 | tf_op jit(solution)/shard_map/last_slices/pallas_call | solution.py:252
  27.3 0.2 collective-permute-done.11
  27.6 3.5 %collective-permute-start.12 = (bf16[8,16,256]{2,1,0:T(8,128)(2,1)S(1)}, bf16[8,16,256]{2,1,0:T(8,128)(2,1)S(1)}, u32[]{:S(2)}, u32[]{:S(2)}) collective-permute-start(bf16[8,16,256]{2,1,0:T(8,128)(2,1)S(1)} %fusion.14), channel_id=1, source_target_pairs={{0,24},{4,28},{8,16},{12,20},{16,8},{20,12},{24,0},{28,4},{1,25},{... | collective-permute-start | bytes 196616 | tf_op jit(solution)/shard_map/ppermute | solution.py:269
  31.1 1.1 %collective-permute-start.13 = (bf16[8,16,256]{2,1,0:T(8,128)(2,1)S(1)}, bf16[8,16,256]{2,1,0:T(8,128)(2,1)S(1)}, u32[]{:S(2)}, u32[]{:S(2)}) collective-permute-start(bf16[8,16,256]{2,1,0:T(8,128)(2,1)S(1)} %get-tuple-element.22), channel_id=1, source_target_pairs={{0,16},{4,20},{8,24},{12,28},{16,0},{20,4},{24,8},{28,12},{1,17},{... | collective-permute-start | bytes 196616 | tf_op jit(solution)/shard_map/ppermute | solution.py:269
  32.2 2.4 %collective-permute-start.14 = (bf16[8,16,256]{2,1,0:T(8,128)(2,1)S(1)}, bf16[8,16,256]{2,1,0:T(8,128)(2,1)S(1)}, u32[]{:S(2)}, u32[]{:S(2)}) collective-permute-start(bf16[8,16,256]{2,1,0:T(8,128)(2,1)S(1)} %get-tuple-element.23), channel_id=1, source_target_pairs={{0,8},{4,12},{8,0},{12,4},{16,24},{20,28},{24,16},{28,20},{1,9},{5... | collective-permute-start | bytes 196616 | tf_op jit(solution)/shard_map/ppermute | solution.py:269
  34.6 0.5 %collective-permute-start.9 = (bf16[128,512]{1,0:T(8,128)(2,1)S(1)}, bf16[128,512]{1,0:T(8,128)(2,1)S(1)}, u32[]{:S(2)}, u32[]{:S(2)}) collective-permute-start(bf16[128,512]{1,0:T(8,128)(2,1)S(1)} %collective-permute-done.6), channel_id=1, source_target_pairs={{0,1},{1,0},{2,3},{3,2},{4,5},{5,4},{6,7},{7,6},{8,9},{9,8},{10,11... | collective-permute-start | bytes 393224 | tf_op jit(solution)/shard_map/ppermute | solution.py:269
  35.1 2.0 %collective-permute-done.13 = bf16[8,16,256]{2,1,0:T(8,128)(2,1)S(1)} collective-permute-done((bf16[8,16,256]{2,1,0:T(8,128)(2,1)S(1)}, bf16[8,16,256]{2,1,0:T(8,128)(2,1)S(1)}, u32[]{:S(2)}, u32[]{:S(2)}) %collective-permute-start.13) | collective-permute-done | bytes 65568 | tf_op jit(solution)/shard_map/ppermute | solution.py:269
  37.1 0.4 collective-permute-done.14
  37.5 0.6 %collective-permute-start.16 = (bf16[128,256]{1,0:T(8,128)(2,1)S(1)}, bf16[128,256]{1,0:T(8,128)(2,1)S(1)}, u32[]{:S(2)}, u32[]{:S(2)}) collective-permute-start(bf16[128,256]{1,0:T(8,128)(2,1)S(1)} %bitcast.44), channel_id=1, source_target_pairs={{0,2},{1,3},{2,0},{3,1},{4,6},{5,7},{6,4},{7,5},{8,10},{9,11},{10,... | collective-permute-start | bytes 196616 | tf_op jit(solution)/shard_map/ppermute | solution.py:269
  38.2 3.7 %collective-permute-done.16 = bf16[128,256]{1,0:T(8,128)(2,1)S(1)} collective-permute-done((bf16[128,256]{1,0:T(8,128)(2,1)S(1)}, bf16[128,256]{1,0:T(8,128)(2,1)S(1)}, u32[]{:S(2)}, u32[]{:S(2)}) %collective-permute-start.16) | collective-permute-done | bytes 65568 | tf_op jit(solution)/shard_map/ppermute | solution.py:269
  41.9 0.6 %copy.11 = f32[1,16,64]{2,1,0:T(8,128)} copy(f32[1,16,64]{2,1,0:T(8,128)S(1)} %get-tuple-element.25) | data formatting | bytes 8192
  42.5 0.6 %collective-permute-done.17 = bf16[128,256]{1,0:T(8,128)(2,1)S(1)} collective-permute-done((bf16[128,256]{1,0:T(8,128)(2,1)S(1)}, bf16[128,256]{1,0:T(8,128)(2,1)S(1)}, u32[]{:S(2)}, u32[]{:S(2)}) %collective-permute-start.17) | collective-permute-done | bytes 65568 | tf_op jit(solution)/shard_map/ppermute | solution.py:269
  43.1 1.1 %convolution_multiply_fusion = f32[512,256]{1,0:T(8,128)} fusion(bf16[128,512]{1,0:T(8,128)(2,1)S(1)} %collective-permute-done.9, bf16[128,512]{1,0:T(8,128)(2,1)S(1)} %collective-permute-done.6, bf16[128,512]{1,0:T(8,128)(2,1)S(1)} %collective-permute-done, bf16[128,512]{1,0:T(8,128)(2,1)S(1)} %bitcast.43, bf16[128,256]{1,0:T(8,128)(2,1)S(1)} %collective-permute-done.17, ...), kind=kOutput, calls=%fused_computation | convolution fusion | flops 137494528 | bytes 1310720 | tf_op jit(solution)/shard_map/dot_general | solution.py:326
  (34 shorter events, 0.2 us)
Async XLA Ops:
  0.6 1.0 %copy-start = (bf16[512,256]{1,0:T(8,128)(2,1)S(1)}, bf16[512,256]{1,0:T(8,128)(2,1)}, u32[]{:S(2)}) copy-start(bf16[512,256]{1,0:T(8,128)(2,1)} %param.9) | copy-start | bytes 786436
  0.6 15.8 %copy-start.2 = (f32[128,128]{1,0:T(8,128)S(1)}, f32[128,128]{1,0:T(8,128)}, u32[]{:S(2)}) copy-start(f32[128,128]{1,0:T(8,128)} %constant.15.clone.row_ref) | copy-start | bytes 196612
  0.7 15.8 %copy-start.4 = (bf16[256,128]{1,0:T(8,128)(2,1)S(1)}, bf16[256,128]{1,0:T(8,128)(2,1)}, u32[]{:S(2)}) copy-start(bf16[256,128]{1,0:T(8,128)(2,1)} %constant.16.clone.fwd_ref) | copy-start | bytes 196612
  0.7 15.8 %copy-start.5 = (s32[1,8,8]{2,1,0:T(8,128)S(1)}, s32[1,8,8]{2,1,0:T(8,128)}, u32[]{:S(2)}) copy-start(s32[1,8,8]{2,1,0:T(8,128)} %param.11) | copy-start | bytes 772
  0.7 15.8 %copy-start.6 = (s32[1,16,4]{1,2,0:T(4,128)S(1)}, s32[1,16,4]{1,2,0:T(4,128)}, u32[]{:S(2)}) copy-start(s32[1,16,4]{1,2,0:T(4,128)} %param.14) | copy-start | bytes 772
  2.7 7.4 %collective-permute-start.2 = (bf16[8,16,256]{2,1,0:T(8,128)(2,1)S(1)}, bf16[8,16,256]{2,1,0:T(8,128)(2,1)S(1)}, u32[]{:S(2)}, u32[]{:S(2)}) collective-permute-start(bf16[8,16,256]{2,1,0:T(8,128)(2,1)S(1)} %bitcast.29), channel_id=1, source_target_pairs={{0,8},{4,12},{8,0},{12,4},{16,24},{20,28},{24,16},{28,20},{1,9},{5... | collective-permute-start | bytes 196616 | tf_op jit(solution)/shard_map/ppermute | solution.py:269
  5.8 8.1 %collective-permute-start.1 = (bf16[8,16,256]{2,1,0:T(8,128)(2,1)S(1)}, bf16[8,16,256]{2,1,0:T(8,128)(2,1)S(1)}, u32[]{:S(2)}, u32[]{:S(2)}) collective-permute-start(bf16[8,16,256]{2,1,0:T(8,128)(2,1)S(1)} %bitcast.30), channel_id=1, source_target_pairs={{0,16},{4,20},{8,24},{12,28},{16,0},{20,4},{24,8},{28,12},{1,17},{... | collective-permute-start | bytes 196616 | tf_op jit(solution)/shard_map/ppermute | solution.py:269
  8.4 6.1 %collective-permute-start.3 = (bf16[8,16,256]{2,1,0:T(8,128)(2,1)S(1)}, bf16[8,16,256]{2,1,0:T(8,128)(2,1)S(1)}, u32[]{:S(2)}, u32[]{:S(2)}) collective-permute-start(bf16[8,16,256]{2,1,0:T(8,128)(2,1)S(1)} %bitcast.31), channel_id=1, source_target_pairs={{0,24},{4,28},{8,16},{12,20},{16,8},{20,12},{24,0},{28,4},{1,25},{... | collective-permute-start | bytes 196616 | tf_op jit(solution)/shard_map/ppermute | solution.py:269
  8.4 8.1 %collective-permute-start.4 = (bf16[8,16,256]{2,1,0:T(8,128)(2,1)S(1)}, bf16[8,16,256]{2,1,0:T(8,128)(2,1)S(1)}, u32[]{:S(2)}, u32[]{:S(2)}) collective-permute-start(bf16[8,16,256]{2,1,0:T(8,128)(2,1)S(1)} %bitcast.32), channel_id=1, source_target_pairs={{0,4},{4,0},{8,12},{12,8},{16,20},{20,16},{24,28},{28,24},{1,5},{5... | collective-permute-start | bytes 196616 | tf_op jit(solution)/shard_map/ppermute | solution.py:269
  10.1 6.4 %collective-permute-start.5 = (bf16[8,16,256]{2,1,0:T(8,128)(2,1)S(1)}, bf16[8,16,256]{2,1,0:T(8,128)(2,1)S(1)}, u32[]{:S(2)}, u32[]{:S(2)}) collective-permute-start(bf16[8,16,256]{2,1,0:T(8,128)(2,1)S(1)} %collective-permute-done.2.rest_1_), channel_id=1, source_target_pairs={{0,4},{4,0},{8,12},{12,8},{16,20},{20,16},{24,28},{28,24},{1,5},{5... | collective-permute-start | bytes 196616 | tf_op jit(solution)/shard_map/ppermute | solution.py:269
  10.4 1.2 %copy-start.1 = (bf16[1,16,128,256]{3,2,1,0:T(8,128)(2,1)S(1)}, bf16[1,16,128,256]{3,2,1,0:T(8,128)(2,1)}, u32[]{:S(2)}) copy-start(bf16[1,16,128,256]{3,2,1,0:T(8,128)(2,1)} %image_ref.1) | copy-start | bytes 3145732
  11.6 0.7 %copy-start.7 = (f32[1,16]{1,0:T(1,128)S(1)}, f32[1,16]{1,0:T(1,128)}, u32[]{:S(2)}) copy-start(f32[1,16]{1,0:T(1,128)} %defocus_ref.1) | copy-start | bytes 196
  13.9 4.9 %copy-start.8 = (bf16[1,8,16,512]{3,2,1,0:T(8,128)(2,1)S(1)}, bf16[1,8,16,512]{3,2,1,0:T(8,128)(2,1)}, u32[]{:S(2)}) copy-start(bf16[1,8,16,512]{3,2,1,0:T(8,128)(2,1)} %param.10) | copy-start | bytes 393220
  13.9 6.5 %copy-start.3 = (bf16[128,256]{1,0:T(8,128)(2,1)S(1)}, bf16[128,256]{1,0:T(8,128)(2,1)}, u32[]{:S(2)}) copy-start(bf16[128,256]{1,0:T(8,128)(2,1)} %constant.17.clone.back_ref) | copy-start | bytes 196612
  14.4 5.9 %collective-permute-start.8 = (bf16[8,16,256]{2,1,0:T(8,128)(2,1)S(1)}, bf16[8,16,256]{2,1,0:T(8,128)(2,1)S(1)}, u32[]{:S(2)}, u32[]{:S(2)}) collective-permute-start(bf16[8,16,256]{2,1,0:T(8,128)(2,1)S(1)} %collective-permute-done.3.rest_3_), channel_id=1, source_target_pairs={{0,4},{4,0},{8,12},{12,8},{16,20},{20,16},{24,28},{28,24},{1,5},{5... | collective-permute-start | bytes 196616 | tf_op jit(solution)/shard_map/ppermute | solution.py:269
  15.9 4.5 %collective-permute-start.7 = (bf16[8,16,256]{2,1,0:T(8,128)(2,1)S(1)}, bf16[8,16,256]{2,1,0:T(8,128)(2,1)S(1)}, u32[]{:S(2)}, u32[]{:S(2)}) collective-permute-start(bf16[8,16,256]{2,1,0:T(8,128)(2,1)S(1)} %collective-permute-done.1.rest_2_), channel_id=1, source_target_pairs={{0,4},{4,0},{8,12},{12,8},{16,20},{20,16},{24,28},{28,24},{1,5},{5... | collective-permute-start | bytes 196616 | tf_op jit(solution)/shard_map/ppermute | solution.py:269
  18.8 6.6 %collective-permute-start.6 = (bf16[128,512]{1,0:T(8,128)(2,1)S(1)}, bf16[128,512]{1,0:T(8,128)(2,1)S(1)}, u32[]{:S(2)}, u32[]{:S(2)}) collective-permute-start(bf16[128,512]{1,0:T(8,128)(2,1)S(1)} %bitcast.41), channel_id=1, source_target_pairs={{0,2},{1,3},{2,0},{3,1},{4,6},{5,7},{6,4},{7,5},{8,10},{9,11},{10,... | collective-permute-start | bytes 393224 | tf_op jit(solution)/shard_map/ppermute | solution.py:269
  23.2 4.3 %collective-permute-start.11 = (bf16[8,16,256]{2,1,0:T(8,128)(2,1)S(1)}, bf16[8,16,256]{2,1,0:T(8,128)(2,1)S(1)}, u32[]{:S(2)}, u32[]{:S(2)}) collective-permute-start(bf16[8,16,256]{2,1,0:T(8,128)(2,1)S(1)} %slice_bitcast_fusion.1), channel_id=1, source_target_pairs={{0,4},{4,0},{8,12},{12,8},{16,20},{20,16},{24,28},{28,24},{1,5},{5... | collective-permute-start | bytes 196616 | tf_op jit(solution)/shard_map/ppermute | solution.py:269
  24.8 6.3 %collective-permute-start.10 = (bf16[3,8,16,256]{3,2,1,0:T(8,128)(2,1)S(1)}, bf16[3,8,16,256]{3,2,1,0:T(8,128)(2,1)S(1)}, u32[]{:S(2)}, u32[]{:S(2)}) collective-permute-start(bf16[3,8,16,256]{3,2,1,0:T(8,128)(2,1)S(1)} %slice.28), channel_id=1, source_target_pairs={{0,4},{4,0},{8,12},{12,8},{16,20},{20,16},{24,28},{28,24},{1,5},{5... | collective-permute-start | bytes 589832 | tf_op jit(solution)/shard_map/ppermute | solution.py:269
  27.6 7.5 %collective-permute-start.12 = (bf16[8,16,256]{2,1,0:T(8,128)(2,1)S(1)}, bf16[8,16,256]{2,1,0:T(8,128)(2,1)S(1)}, u32[]{:S(2)}, u32[]{:S(2)}) collective-permute-start(bf16[8,16,256]{2,1,0:T(8,128)(2,1)S(1)} %fusion.14), channel_id=1, source_target_pairs={{0,24},{4,28},{8,16},{12,20},{16,8},{20,12},{24,0},{28,4},{1,25},{... | collective-permute-start | bytes 196616 | tf_op jit(solution)/shard_map/ppermute | solution.py:269
  31.1 6.0 %collective-permute-start.13 = (bf16[8,16,256]{2,1,0:T(8,128)(2,1)S(1)}, bf16[8,16,256]{2,1,0:T(8,128)(2,1)S(1)}, u32[]{:S(2)}, u32[]{:S(2)}) collective-permute-start(bf16[8,16,256]{2,1,0:T(8,128)(2,1)S(1)} %get-tuple-element.22), channel_id=1, source_target_pairs={{0,16},{4,20},{8,24},{12,28},{16,0},{20,4},{24,8},{28,12},{1,17},{... | collective-permute-start | bytes 196616 | tf_op jit(solution)/shard_map/ppermute | solution.py:269
  32.2 5.3 %collective-permute-start.14 = (bf16[8,16,256]{2,1,0:T(8,128)(2,1)S(1)}, bf16[8,16,256]{2,1,0:T(8,128)(2,1)S(1)}, u32[]{:S(2)}, u32[]{:S(2)}) collective-permute-start(bf16[8,16,256]{2,1,0:T(8,128)(2,1)S(1)} %get-tuple-element.23), channel_id=1, source_target_pairs={{0,8},{4,12},{8,0},{12,4},{16,24},{20,28},{24,16},{28,20},{1,9},{5... | collective-permute-start | bytes 196616 | tf_op jit(solution)/shard_map/ppermute | solution.py:269
  34.6 7.9 %collective-permute-start = (bf16[128,512]{1,0:T(8,128)(2,1)S(1)}, bf16[128,512]{1,0:T(8,128)(2,1)S(1)}, u32[]{:S(2)}, u32[]{:S(2)}) collective-permute-start(bf16[128,512]{1,0:T(8,128)(2,1)S(1)} %bitcast.42), channel_id=1, source_target_pairs={{0,1},{1,0},{2,3},{3,2},{4,5},{5,4},{6,7},{7,6},{8,9},{9,8},{10,11... | collective-permute-start | bytes 393224 | tf_op jit(solution)/shard_map/ppermute | solution.py:269
  34.6 7.9 %collective-permute-start.9 = (bf16[128,512]{1,0:T(8,128)(2,1)S(1)}, bf16[128,512]{1,0:T(8,128)(2,1)S(1)}, u32[]{:S(2)}, u32[]{:S(2)}) collective-permute-start(bf16[128,512]{1,0:T(8,128)(2,1)S(1)} %collective-permute-done.6), channel_id=1, source_target_pairs={{0,1},{1,0},{2,3},{3,2},{4,5},{5,4},{6,7},{7,6},{8,9},{9,8},{10,11... | collective-permute-start | bytes 393224 | tf_op jit(solution)/shard_map/ppermute | solution.py:269
  37.5 4.3 %collective-permute-start.16 = (bf16[128,256]{1,0:T(8,128)(2,1)S(1)}, bf16[128,256]{1,0:T(8,128)(2,1)S(1)}, u32[]{:S(2)}, u32[]{:S(2)}) collective-permute-start(bf16[128,256]{1,0:T(8,128)(2,1)S(1)} %bitcast.44), channel_id=1, source_target_pairs={{0,2},{1,3},{2,0},{3,1},{4,6},{5,7},{6,4},{7,5},{8,10},{9,11},{10,... | collective-permute-start | bytes 196616 | tf_op jit(solution)/shard_map/ppermute | solution.py:269
  38.1 4.3 %collective-permute-start.15 = (bf16[128,256]{1,0:T(8,128)(2,1)S(1)}, bf16[128,256]{1,0:T(8,128)(2,1)S(1)}, u32[]{:S(2)}, u32[]{:S(2)}) collective-permute-start(bf16[128,256]{1,0:T(8,128)(2,1)S(1)} %bitcast.45), channel_id=1, source_target_pairs={{0,1},{1,0},{2,3},{3,2},{4,5},{5,4},{6,7},{7,6},{8,9},{9,8},{10,11... | collective-permute-start | bytes 196616 | tf_op jit(solution)/shard_map/ppermute | solution.py:269
  41.9 1.3 %collective-permute-start.17 = (bf16[128,256]{1,0:T(8,128)(2,1)S(1)}, bf16[128,256]{1,0:T(8,128)(2,1)S(1)}, u32[]{:S(2)}, u32[]{:S(2)}) collective-permute-start(bf16[128,256]{1,0:T(8,128)(2,1)S(1)} %collective-permute-done.16), channel_id=1, source_target_pairs={{0,1},{1,0},{2,3},{3,2},{4,5},{5,4},{6,7},{7,6},{8,9},{9,8},{10,11... | collective-permute-start | bytes 196616 | tf_op jit(solution)/shard_map/ppermute | solution.py:269

commit v4 on v3

--- a/solution.py
+++ b/solution.py
@@ -290,9 +290,8 @@
     from_other, from_far, from_near, from_side = (to(own, flip) for flip in (other, far, near, side))
     from_near_side = to(from_near, side)
     u = weigh_images(images, defocus)
-    from_far, u = lax.optimization_barrier((from_far, u))
-    from_other, _ = lax.optimization_barrier((from_other, from_far))
-    from_far_side, from_other_side = to(from_far, side), to(from_other, side)
+    from_far, from_other, u, from_side, from_near_side = lax.optimization_barrier((from_far, from_other, u, from_side, from_near_side))
+    from_far_side, from_other_side = to(jnp.stack([from_far, from_other]), side)
 
     common = lax.axis_index("slab").astype(jnp.int32).reshape(1), block_index[0], orient[0].T, separable_tables(fourier), u
     scores = first_scores(*common, [own, from_near, from_far, from_other, from_side, from_near_side], (0, near, far, other, side, near + side))

time: 44.4 us -> 43.6 us (0.982)
  waiting for transfers between devices: 7.53 us -> 6.61 us
    ppermute x18 -> x17, waiting for transfers between devices: 7.53 us -> 6.61 us  [swap(): lax.ppermute(value, axis, [(source, source ^ flip) for source in range(si...]
    ppermute x18 -> x17, starting transfers between devices: 21.6 us -> 21.6 us  [swap(): lax.ppermute(value, axis, [(source, source ^ flip) for source in range(si...]
  transfers between devices with their start and end apart: 18 -> 17, of which waited for: 6 -> 6; matrix products, arithmetic and copies ran while one was open for 2% -> 2% of each run, Pallas kernels for 19% -> 20%
where the time goes in v4:
time: 43.6 us; the launch traced here: 43.4 us
  starting transfers between devices  21.6 us (50%)
  Pallas kernels  8.58 us (20%)
  waiting for transfers between devices  6.61 us (15%)
  local copies, waits for them, and re-layouts  3.45 us (8%)
  matrix products  2.22 us (5%)
  between operations  0.8 us (2%)
    ppermute x17, starting transfers between devices, swap(): lax.ppermute(value, axis, [(source, source ^ flip) for source in range(si...  21.6 us
    ppermute x17, waiting for transfers between devices, swap(): lax.ppermute(value, axis, [(source, source ^ flip) for source in range(si...  6.61 us
    unnamed x19, local copies, waits for them, and re-layouts  3.42 us
    pallas_call x1, Pallas kernels, expectation(): pl.pallas_call(kernel, out_shape=(pltpu.VMEM((1, count, picks * NS), jnp....  2.81 us
    pallas_call x1, Pallas kernels, first_scores(): pl.pallas_call(kernel, out_shape=pltpu.VMEM((picks, count, LANES), jnp.fl...  2.28 us
    pallas_call x1, Pallas kernels, last_slices(): pl.pallas_call(kernel, out_shape=pltpu.VMEM((len(out_flips), orient_count...  1.89 us
    pallas_call x1, Pallas kernels, weigh_images(): pl.pallas_call(kernel, out_shape=pltpu.VMEM(images.shape[1:], jnp.float32...  1.6 us
    dot_general x1, matrix products, direct(): lax.dot_general(jnp.concatenate(weighers, axis=0), jnp.concatenate(backs,...  1.13 us
  transfers between devices with their start and end apart: 17, of which 6 were waited for; matrix products, arithmetic and copies ran while one was open for 2% of the time, Pallas kernels for 20%

profile of v4, /device:TPU:0, one launch (start us, length us, event | category | flops | bytes accessed | tf_op | source)
XLA Modules:
  0.0 43.4 jit_solution(16778557468459240090)
XLA Ops:
  0.6 0.0 copy-start
  0.6 0.0 copy-start.2
  0.7 0.0 copy-start.4
  0.7 0.9 %copy-done = bf16[512,256]{1,0:T(8,128)(2,1)S(1)} copy-done((bf16[512,256]{1,0:T(8,128)(2,1)S(1)}, bf16[512,256]{1,0:T(8,128)(2,1)}, u32[]{:S(2)}) %copy-start) | copy-done | bytes 262168
  1.6 1.1 %convolution_convert_fusion = bf16[128,256]{1,0:T(8,128)(2,1)S(1)} fusion(bf16[128,512]{1,0:T(8,128)(2,1)} %bitcast.48, bf16[512,256]{1,0:T(8,128)(2,1)S(1)} %copy-done), kind=kOutput, calls=%fused_computation.1 | convolution fusion | flops 33587200 | bytes 458752 | tf_op jit(solution)/shard_map/dot_general | solution.py:288
  2.7 3.1 %collective-permute-start.4 = (bf16[8,16,256]{2,1,0:T(8,128)(2,1)S(1)}, bf16[8,16,256]{2,1,0:T(8,128)(2,1)S(1)}, u32[]{:S(2)}, u32[]{:S(2)}) collective-permute-start(bf16[8,16,256]{2,1,0:T(8,128)(2,1)S(1)} %bitcast.35), channel_id=1, source_target_pairs={{0,8},{4,12},{8,0},{12,4},{16,24},{20,28},{24,16},{28,20},{1,9},{5... | collective-permute-start | bytes 196616 | tf_op jit(solution)/shard_map/ppermute | solution.py:269
  5.8 2.6 %collective-permute-start.1 = (bf16[8,16,256]{2,1,0:T(8,128)(2,1)S(1)}, bf16[8,16,256]{2,1,0:T(8,128)(2,1)S(1)}, u32[]{:S(2)}, u32[]{:S(2)}) collective-permute-start(bf16[8,16,256]{2,1,0:T(8,128)(2,1)S(1)} %bitcast.36), channel_id=1, source_target_pairs={{0,16},{4,20},{8,24},{12,28},{16,0},{20,4},{24,8},{28,12},{1,17},{... | collective-permute-start | bytes 196616 | tf_op jit(solution)/shard_map/ppermute | solution.py:269
  8.4 1.7 %collective-permute-start.3 = (bf16[8,16,256]{2,1,0:T(8,128)(2,1)S(1)}, bf16[8,16,256]{2,1,0:T(8,128)(2,1)S(1)}, u32[]{:S(2)}, u32[]{:S(2)}) collective-permute-start(bf16[8,16,256]{2,1,0:T(8,128)(2,1)S(1)} %bitcast.38), channel_id=1, source_target_pairs={{0,4},{4,0},{8,12},{12,8},{16,20},{20,16},{24,28},{28,24},{1,5},{5... | collective-permute-start | bytes 196616 | tf_op jit(solution)/shard_map/ppermute | solution.py:269
  10.1 0.3 collective-permute-start.5
  10.4 1.2 %copy-done.1 = bf16[1,16,128,256]{3,2,1,0:T(8,128)(2,1)S(1)} copy-done((bf16[1,16,128,256]{3,2,1,0:T(8,128)(2,1)S(1)}, bf16[1,16,128,256]{3,2,1,0:T(8,128)(2,1)}, u32[]{:S(2)}) %copy-start.1) | copy-done | bytes 1048600
  11.6 0.7 %copy-done.7 = f32[1,16]{1,0:T(1,128)S(1)} copy-done((f32[1,16]{1,0:T(1,128)S(1)}, f32[1,16]{1,0:T(1,128)}, u32[]{:S(2)}) %copy-start.7) | copy-done | bytes 88
  12.3 1.6 %weigh_images.1.u_ref = f32[16,128,256]{2,1,0:T(8,128)S(1)} custom-call(f32[1,16]{1,0:T(1,128)S(1)} %copy-done.7, bf16[1,16,128,256]{3,2,1,0:T(8,128)(2,1)S(1)} %copy-done.1), custom_call_target="tpu_custom_call" | custom-call | flops 7864320 | bytes 3145728 | tf_op jit(solution)/shard_map/weigh_images/pallas_call | solution.py:79
  13.9 0.5 %collective-permute-done.2.rest_3_ = bf16[8,16,256]{2,1,0:T(8,128)(2,1)S(1)} collective-permute-done((bf16[8,16,256]{2,1,0:T(8,128)(2,1)S(1)}, bf16[8,16,256]{2,1,0:T(8,128)(2,1)S(1)}, u32[]{:S(2)}, u32[]{:S(2)}) %collective-permute-start.2) | collective-permute-done | bytes 65568 | tf_op jit(solution)/shard_map/ppermute | solution.py:269
  14.5 1.6 %collective-permute-start.7 = (bf16[2,8,16,256]{3,2,1,0:T(8,128)(2,1)S(1)}, bf16[2,8,16,256]{3,2,1,0:T(8,128)(2,1)S(1)}, u32[]{:S(2)}, u32[]{:S(2)}) collective-permute-start(bf16[2,8,16,256]{3,2,1,0:T(8,128)(2,1)S(1)} %pad_maximum_fusion), channel_id=1, source_target_pairs={{0,4},{4,0},{8,12},{12,8},{16,20},{20,16},{24,28},{28,24},{1,5},{5... | collective-permute-start | bytes 393224 | tf_op jit(solution)/shard_map/ppermute | solution.py:269
  16.0 2.3 %first_scores.1.score_ref = f32[4,16,128]{2,1,0:T(8,128)S(1)} custom-call(s32[1]{0:T(128)} %bitcast.1.me_ref, s32[8,8]{1,0:T(8,128)S(1)} %bitcast.42, s32[4,16]{1,0:T(4,128)S(1)} %bitcast.45, f32[128,128]{1,0:T(8,128)S(1)} %copy-done.2, bf16[256,128]{1,0:T(8,128)(2,1)S(1)} %copy-done.4, f32[16,128,256]{2,1,0:T(8,128)S(1)} %weigh_images.1.u_ref, ...), custom_call_target="tpu_custom_call" | custom-call | flops 402653184 | bytes 2097152 | tf_op jit(solution)/shard_map/first_scores/pallas_call | solution.py:174
  18.3 1.6 %collective-permute-start.6 = (bf16[128,512]{1,0:T(8,128)(2,1)S(1)}, bf16[128,512]{1,0:T(8,128)(2,1)S(1)}, u32[]{:S(2)}, u32[]{:S(2)}) collective-permute-start(bf16[128,512]{1,0:T(8,128)(2,1)S(1)} %bitcast.49), channel_id=1, source_target_pairs={{0,2},{1,3},{2,0},{3,1},{4,6},{5,7},{6,4},{7,5},{8,10},{9,11},{10,... | collective-permute-start | bytes 393224 | tf_op jit(solution)/shard_map/ppermute | solution.py:269
  19.9 2.8 %expectation.1 = (f32[1,16,64]{2,1,0:T(8,128)S(1)}, f32[4,16,128]{2,1,0:T(8,128)S(1)}, bf16[4,8,16,256]{3,2,1,0:T(8,128)(2,1)S(1)}) custom-call(s32[1]{0:T(128)} %bitcast.1.me_ref, s32[8,8]{1,0:T(8,128)S(1)} %bitcast.43, s32[4,16]{1,0:T(4,128)S(1)} %bitcast.46, f32[128,128]{1,0:T(8,128)S(1)} %copy-done.2, bf16[256,128]{1,0:T(8,128)(2,1)S(1)} %copy-done.4, ...), custom_call_target="tpu_custom_call" | custom-call | flops 402653184 | bytes 2097152 | tf_op jit(solution)/shard_map/expectation/pallas_call | solution.py:222
  22.8 1.1 %collective-permute-start.10 = (bf16[8,16,256]{2,1,0:T(8,128)(2,1)S(1)}, bf16[8,16,256]{2,1,0:T(8,128)(2,1)S(1)}, u32[]{:S(2)}, u32[]{:S(2)}) collective-permute-start(bf16[8,16,256]{2,1,0:T(8,128)(2,1)S(1)} %slice_bitcast_fusion.3), channel_id=1, source_target_pairs={{0,4},{4,0},{8,12},{12,8},{16,20},{20,16},{24,28},{28,24},{1,5},{5... | collective-permute-start | bytes 196616 | tf_op jit(solution)/shard_map/ppermute | solution.py:269
  23.9 1.0 %collective-permute-start.9 = (bf16[3,8,16,256]{3,2,1,0:T(8,128)(2,1)S(1)}, bf16[3,8,16,256]{3,2,1,0:T(8,128)(2,1)S(1)}, u32[]{:S(2)}, u32[]{:S(2)}) collective-permute-start(bf16[3,8,16,256]{3,2,1,0:T(8,128)(2,1)S(1)} %slice.28), channel_id=1, source_target_pairs={{0,4},{4,0},{8,12},{12,8},{16,20},{20,16},{24,28},{28,24},{1,5},{5... | collective-permute-start | bytes 589832 | tf_op jit(solution)/shard_map/ppermute | solution.py:269
  25.0 1.9 %last_slices.1 = bf16[4,8,16,256]{3,2,1,0:T(8,128)(2,1)S(1)} custom-call(s32[1]{0:T(128)} %bitcast.1.me_ref, s32[8,8]{1,0:T(8,128)S(1)} %bitcast.44, s32[4,16]{1,0:T(4,128)S(1)} %bitcast.47, f32[128,128]{1,0:T(8,128)S(1)} %copy-done.2, bf16[128,256]{1,0:T(8,128)(2,1)S(1)} %copy-done.3, f32[16,128,256]{2,1,0:T(8,128)S(1)} %weigh_images.1.u_ref, ...), custom_call_target="tpu_custom_call" | custom-call | flops 268435456 | bytes 2097152 | tf_op jit(solution)/shard_map/last_slices/pallas_call | solution.py:252
  26.9 0.2 collective-permute-done.10
  27.1 3.4 %collective-permute-start.11 = (bf16[8,16,256]{2,1,0:T(8,128)(2,1)S(1)}, bf16[8,16,256]{2,1,0:T(8,128)(2,1)S(1)}, u32[]{:S(2)}, u32[]{:S(2)}) collective-permute-start(bf16[8,16,256]{2,1,0:T(8,128)(2,1)S(1)} %fusion.14), channel_id=1, source_target_pairs={{0,24},{4,28},{8,16},{12,20},{16,8},{20,12},{24,0},{28,4},{1,25},{... | collective-permute-start | bytes 196616 | tf_op jit(solution)/shard_map/ppermute | solution.py:269
  30.6 0.8 %collective-permute-start.12 = (bf16[8,16,256]{2,1,0:T(8,128)(2,1)S(1)}, bf16[8,16,256]{2,1,0:T(8,128)(2,1)S(1)}, u32[]{:S(2)}, u32[]{:S(2)}) collective-permute-start(bf16[8,16,256]{2,1,0:T(8,128)(2,1)S(1)} %get-tuple-element.26), channel_id=1, source_target_pairs={{0,16},{4,20},{8,24},{12,28},{16,0},{20,4},{24,8},{28,12},{1,17},{... | collective-permute-start | bytes 196616 | tf_op jit(solution)/shard_map/ppermute | solution.py:269
  31.4 2.3 %collective-permute-start.13 = (bf16[8,16,256]{2,1,0:T(8,128)(2,1)S(1)}, bf16[8,16,256]{2,1,0:T(8,128)(2,1)S(1)}, u32[]{:S(2)}, u32[]{:S(2)}) collective-permute-start(bf16[8,16,256]{2,1,0:T(8,128)(2,1)S(1)} %get-tuple-element.27), channel_id=1, source_target_pairs={{0,8},{4,12},{8,0},{12,4},{16,24},{20,28},{24,16},{28,20},{1,9},{5... | collective-permute-start | bytes 196616 | tf_op jit(solution)/shard_map/ppermute | solution.py:269
  33.7 0.5 %collective-permute-start.8 = (bf16[128,512]{1,0:T(8,128)(2,1)S(1)}, bf16[128,512]{1,0:T(8,128)(2,1)S(1)}, u32[]{:S(2)}, u32[]{:S(2)}) collective-permute-start(bf16[128,512]{1,0:T(8,128)(2,1)S(1)} %collective-permute-done.6), channel_id=1, source_target_pairs={{0,1},{1,0},{2,3},{3,2},{4,5},{5,4},{6,7},{7,6},{8,9},{9,8},{10,11... | collective-permute-start | bytes 393224 | tf_op jit(solution)/shard_map/ppermute | solution.py:269
  34.2 2.0 %collective-permute-done.12 = bf16[8,16,256]{2,1,0:T(8,128)(2,1)S(1)} collective-permute-done((bf16[8,16,256]{2,1,0:T(8,128)(2,1)S(1)}, bf16[8,16,256]{2,1,0:T(8,128)(2,1)S(1)}, u32[]{:S(2)}, u32[]{:S(2)}) %collective-permute-start.12) | collective-permute-done | bytes 65568 | tf_op jit(solution)/shard_map/ppermute | solution.py:269
  36.2 0.4 %collective-permute-done.13 = bf16[8,16,256]{2,1,0:T(8,128)(2,1)S(1)} collective-permute-done((bf16[8,16,256]{2,1,0:T(8,128)(2,1)S(1)}, bf16[8,16,256]{2,1,0:T(8,128)(2,1)S(1)}, u32[]{:S(2)}, u32[]{:S(2)}) %collective-permute-start.13) | collective-permute-done | bytes 65568 | tf_op jit(solution)/shard_map/ppermute | solution.py:269
  36.6 1.6 %collective-permute-start.15 = (bf16[128,256]{1,0:T(8,128)(2,1)S(1)}, bf16[128,256]{1,0:T(8,128)(2,1)S(1)}, u32[]{:S(2)}, u32[]{:S(2)}) collective-permute-start(bf16[128,256]{1,0:T(8,128)(2,1)S(1)} %bitcast.52), channel_id=1, source_target_pairs={{0,2},{1,3},{2,0},{3,1},{4,6},{5,7},{6,4},{7,5},{8,10},{9,11},{10,... | collective-permute-start | bytes 196616 | tf_op jit(solution)/shard_map/ppermute | solution.py:269
  38.2 2.8 %collective-permute-done.15 = bf16[128,256]{1,0:T(8,128)(2,1)S(1)} collective-permute-done((bf16[128,256]{1,0:T(8,128)(2,1)S(1)}, bf16[128,256]{1,0:T(8,128)(2,1)S(1)}, u32[]{:S(2)}, u32[]{:S(2)}) %collective-permute-start.15) | collective-permute-done | bytes 65568 | tf_op jit(solution)/shard_map/ppermute | solution.py:269
  41.0 0.6 %copy.11 = f32[1,16,64]{2,1,0:T(8,128)} copy(f32[1,16,64]{2,1,0:T(8,128)S(1)} %get-tuple-element.31) | data formatting | bytes 8192
  41.6 0.6 %collective-permute-done.16 = bf16[128,256]{1,0:T(8,128)(2,1)S(1)} collective-permute-done((bf16[128,256]{1,0:T(8,128)(2,1)S(1)}, bf16[128,256]{1,0:T(8,128)(2,1)S(1)}, u32[]{:S(2)}, u32[]{:S(2)}) %collective-permute-start.16) | collective-permute-done | bytes 65568 | tf_op jit(solution)/shard_map/ppermute | solution.py:269
  42.2 1.1 %convolution_multiply_fusion = f32[512,256]{1,0:T(8,128)} fusion(bf16[128,512]{1,0:T(8,128)(2,1)S(1)} %collective-permute-done.8, bf16[128,512]{1,0:T(8,128)(2,1)S(1)} %collective-permute-done.6, bf16[128,512]{1,0:T(8,128)(2,1)S(1)} %collective-permute-done, bf16[128,512]{1,0:T(8,128)(2,1)S(1)} %bitcast.51, bf16[128,256]{1,0:T(8,128)(2,1)S(1)} %collective-permute-done.16, ...), kind=kOutput, calls=%fused_computation | convolution fusion | flops 137494528 | bytes 1310720 | tf_op jit(solution)/shard_map/dot_general | solution.py:325
  (34 shorter events, 0.2 us)
Async XLA Ops:
  0.6 1.0 %copy-start = (bf16[512,256]{1,0:T(8,128)(2,1)S(1)}, bf16[512,256]{1,0:T(8,128)(2,1)}, u32[]{:S(2)}) copy-start(bf16[512,256]{1,0:T(8,128)(2,1)} %param.9) | copy-start | bytes 786436
  0.6 15.4 %copy-start.2 = (f32[128,128]{1,0:T(8,128)S(1)}, f32[128,128]{1,0:T(8,128)}, u32[]{:S(2)}) copy-start(f32[128,128]{1,0:T(8,128)} %constant.15.clone.row_ref) | copy-start | bytes 196612
  0.7 15.4 %copy-start.4 = (bf16[256,128]{1,0:T(8,128)(2,1)S(1)}, bf16[256,128]{1,0:T(8,128)(2,1)}, u32[]{:S(2)}) copy-start(bf16[256,128]{1,0:T(8,128)(2,1)} %constant.16.clone.fwd_ref) | copy-start | bytes 196612
  0.7 15.4 %copy-start.5 = (s32[1,8,8]{2,1,0:T(8,128)S(1)}, s32[1,8,8]{2,1,0:T(8,128)}, u32[]{:S(2)}) copy-start(s32[1,8,8]{2,1,0:T(8,128)} %param.11) | copy-start | bytes 772
  0.7 15.4 %copy-start.6 = (s32[1,16,4]{1,2,0:T(4,128)S(1)}, s32[1,16,4]{1,2,0:T(4,128)}, u32[]{:S(2)}) copy-start(s32[1,16,4]{1,2,0:T(4,128)} %param.14) | copy-start | bytes 772
  2.7 7.4 %collective-permute-start.4 = (bf16[8,16,256]{2,1,0:T(8,128)(2,1)S(1)}, bf16[8,16,256]{2,1,0:T(8,128)(2,1)S(1)}, u32[]{:S(2)}, u32[]{:S(2)}) collective-permute-start(bf16[8,16,256]{2,1,0:T(8,128)(2,1)S(1)} %bitcast.35), channel_id=1, source_target_pairs={{0,8},{4,12},{8,0},{12,4},{16,24},{20,28},{24,16},{28,20},{1,9},{5... | collective-permute-start | bytes 196616 | tf_op jit(solution)/shard_map/ppermute | solution.py:269
  5.8 8.1 %collective-permute-start.1 = (bf16[8,16,256]{2,1,0:T(8,128)(2,1)S(1)}, bf16[8,16,256]{2,1,0:T(8,128)(2,1)S(1)}, u32[]{:S(2)}, u32[]{:S(2)}) collective-permute-start(bf16[8,16,256]{2,1,0:T(8,128)(2,1)S(1)} %bitcast.36), channel_id=1, source_target_pairs={{0,16},{4,20},{8,24},{12,28},{16,0},{20,4},{24,8},{28,12},{1,17},{... | collective-permute-start | bytes 196616 | tf_op jit(solution)/shard_map/ppermute | solution.py:269
  8.4 6.1 %collective-permute-start.2 = (bf16[8,16,256]{2,1,0:T(8,128)(2,1)S(1)}, bf16[8,16,256]{2,1,0:T(8,128)(2,1)S(1)}, u32[]{:S(2)}, u32[]{:S(2)}) collective-permute-start(bf16[8,16,256]{2,1,0:T(8,128)(2,1)S(1)} %bitcast.37), channel_id=1, source_target_pairs={{0,24},{4,28},{8,16},{12,20},{16,8},{20,12},{24,0},{28,4},{1,25},{... | collective-permute-start | bytes 196616 | tf_op jit(solution)/shard_map/ppermute | solution.py:269
  8.4 6.1 %collective-permute-start.3 = (bf16[8,16,256]{2,1,0:T(8,128)(2,1)S(1)}, bf16[8,16,256]{2,1,0:T(8,128)(2,1)S(1)}, u32[]{:S(2)}, u32[]{:S(2)}) collective-permute-start(bf16[8,16,256]{2,1,0:T(8,128)(2,1)S(1)} %bitcast.38), channel_id=1, source_target_pairs={{0,4},{4,0},{8,12},{12,8},{16,20},{20,16},{24,28},{28,24},{1,5},{5... | collective-permute-start | bytes 196616 | tf_op jit(solution)/shard_map/ppermute | solution.py:269
  10.1 4.4 %collective-permute-start.5 = (bf16[8,16,256]{2,1,0:T(8,128)(2,1)S(1)}, bf16[8,16,256]{2,1,0:T(8,128)(2,1)S(1)}, u32[]{:S(2)}, u32[]{:S(2)}) collective-permute-start(bf16[8,16,256]{2,1,0:T(8,128)(2,1)S(1)} %collective-permute-done.4.rest_1_), channel_id=1, source_target_pairs={{0,4},{4,0},{8,12},{12,8},{16,20},{20,16},{24,28},{28,24},{1,5},{5... | collective-permute-start | bytes 196616 | tf_op jit(solution)/shard_map/ppermute | solution.py:269
  10.4 1.2 %copy-start.1 = (bf16[1,16,128,256]{3,2,1,0:T(8,128)(2,1)S(1)}, bf16[1,16,128,256]{3,2,1,0:T(8,128)(2,1)}, u32[]{:S(2)}) copy-start(bf16[1,16,128,256]{3,2,1,0:T(8,128)(2,1)} %image_ref.1) | copy-start | bytes 3145732
  11.6 0.7 %copy-start.7 = (f32[1,16]{1,0:T(1,128)S(1)}, f32[1,16]{1,0:T(1,128)}, u32[]{:S(2)}) copy-start(f32[1,16]{1,0:T(1,128)} %defocus_ref.1) | copy-start | bytes 196
  13.9 4.4 %copy-start.8 = (bf16[1,8,16,512]{3,2,1,0:T(8,128)(2,1)S(1)}, bf16[1,8,16,512]{3,2,1,0:T(8,128)(2,1)}, u32[]{:S(2)}) copy-start(bf16[1,8,16,512]{3,2,1,0:T(8,128)(2,1)} %param.10) | copy-start | bytes 393220
  13.9 6.0 %copy-start.3 = (bf16[128,256]{1,0:T(8,128)(2,1)S(1)}, bf16[128,256]{1,0:T(8,128)(2,1)}, u32[]{:S(2)}) copy-start(bf16[128,256]{1,0:T(8,128)(2,1)} %constant.17.clone.back_ref) | copy-start | bytes 196612
  14.5 5.5 %collective-permute-start.7 = (bf16[2,8,16,256]{3,2,1,0:T(8,128)(2,1)S(1)}, bf16[2,8,16,256]{3,2,1,0:T(8,128)(2,1)S(1)}, u32[]{:S(2)}, u32[]{:S(2)}) collective-permute-start(bf16[2,8,16,256]{3,2,1,0:T(8,128)(2,1)S(1)} %pad_maximum_fusion), channel_id=1, source_target_pairs={{0,4},{4,0},{8,12},{12,8},{16,20},{20,16},{24,28},{28,24},{1,5},{5... | collective-permute-start | bytes 393224 | tf_op jit(solution)/shard_map/ppermute | solution.py:269
  18.3 5.6 %collective-permute-start.6 = (bf16[128,512]{1,0:T(8,128)(2,1)S(1)}, bf16[128,512]{1,0:T(8,128)(2,1)S(1)}, u32[]{:S(2)}, u32[]{:S(2)}) collective-permute-start(bf16[128,512]{1,0:T(8,128)(2,1)S(1)} %bitcast.49), channel_id=1, source_target_pairs={{0,2},{1,3},{2,0},{3,1},{4,6},{5,7},{6,4},{7,5},{8,10},{9,11},{10,... | collective-permute-start | bytes 393224 | tf_op jit(solution)/shard_map/ppermute | solution.py:269
  22.8 4.3 %collective-permute-start.10 = (bf16[8,16,256]{2,1,0:T(8,128)(2,1)S(1)}, bf16[8,16,256]{2,1,0:T(8,128)(2,1)S(1)}, u32[]{:S(2)}, u32[]{:S(2)}) collective-permute-start(bf16[8,16,256]{2,1,0:T(8,128)(2,1)S(1)} %slice_bitcast_fusion.3), channel_id=1, source_target_pairs={{0,4},{4,0},{8,12},{12,8},{16,20},{20,16},{24,28},{28,24},{1,5},{5... | collective-permute-start | bytes 196616 | tf_op jit(solution)/shard_map/ppermute | solution.py:269
  23.9 6.6 %collective-permute-start.9 = (bf16[3,8,16,256]{3,2,1,0:T(8,128)(2,1)S(1)}, bf16[3,8,16,256]{3,2,1,0:T(8,128)(2,1)S(1)}, u32[]{:S(2)}, u32[]{:S(2)}) collective-permute-start(bf16[3,8,16,256]{3,2,1,0:T(8,128)(2,1)S(1)} %slice.28), channel_id=1, source_target_pairs={{0,4},{4,0},{8,12},{12,8},{16,20},{20,16},{24,28},{28,24},{1,5},{5... | collective-permute-start | bytes 589832 | tf_op jit(solution)/shard_map/ppermute | solution.py:269
  27.1 7.1 %collective-permute-start.11 = (bf16[8,16,256]{2,1,0:T(8,128)(2,1)S(1)}, bf16[8,16,256]{2,1,0:T(8,128)(2,1)S(1)}, u32[]{:S(2)}, u32[]{:S(2)}) collective-permute-start(bf16[8,16,256]{2,1,0:T(8,128)(2,1)S(1)} %fusion.14), channel_id=1, source_target_pairs={{0,24},{4,28},{8,16},{12,20},{16,8},{20,12},{24,0},{28,4},{1,25},{... | collective-permute-start | bytes 196616 | tf_op jit(solution)/shard_map/ppermute | solution.py:269
  30.6 5.6 %collective-permute-start.12 = (bf16[8,16,256]{2,1,0:T(8,128)(2,1)S(1)}, bf16[8,16,256]{2,1,0:T(8,128)(2,1)S(1)}, u32[]{:S(2)}, u32[]{:S(2)}) collective-permute-start(bf16[8,16,256]{2,1,0:T(8,128)(2,1)S(1)} %get-tuple-element.26), channel_id=1, source_target_pairs={{0,16},{4,20},{8,24},{12,28},{16,0},{20,4},{24,8},{28,12},{1,17},{... | collective-permute-start | bytes 196616 | tf_op jit(solution)/shard_map/ppermute | solution.py:269
  31.4 5.2 %collective-permute-start.13 = (bf16[8,16,256]{2,1,0:T(8,128)(2,1)S(1)}, bf16[8,16,256]{2,1,0:T(8,128)(2,1)S(1)}, u32[]{:S(2)}, u32[]{:S(2)}) collective-permute-start(bf16[8,16,256]{2,1,0:T(8,128)(2,1)S(1)} %get-tuple-element.27), channel_id=1, source_target_pairs={{0,8},{4,12},{8,0},{12,4},{16,24},{20,28},{24,16},{28,20},{1,9},{5... | collective-permute-start | bytes 196616 | tf_op jit(solution)/shard_map/ppermute | solution.py:269
  33.7 7.9 %collective-permute-start = (bf16[128,512]{1,0:T(8,128)(2,1)S(1)}, bf16[128,512]{1,0:T(8,128)(2,1)S(1)}, u32[]{:S(2)}, u32[]{:S(2)}) collective-permute-start(bf16[128,512]{1,0:T(8,128)(2,1)S(1)} %bitcast.50), channel_id=1, source_target_pairs={{0,1},{1,0},{2,3},{3,2},{4,5},{5,4},{6,7},{7,6},{8,9},{9,8},{10,11... | collective-permute-start | bytes 393224 | tf_op jit(solution)/shard_map/ppermute | solution.py:269
  33.7 7.9 %collective-permute-start.8 = (bf16[128,512]{1,0:T(8,128)(2,1)S(1)}, bf16[128,512]{1,0:T(8,128)(2,1)S(1)}, u32[]{:S(2)}, u32[]{:S(2)}) collective-permute-start(bf16[128,512]{1,0:T(8,128)(2,1)S(1)} %collective-permute-done.6), channel_id=1, source_target_pairs={{0,1},{1,0},{2,3},{3,2},{4,5},{5,4},{6,7},{7,6},{8,9},{9,8},{10,11... | collective-permute-start | bytes 393224 | tf_op jit(solution)/shard_map/ppermute | solution.py:269
  36.6 4.3 %collective-permute-start.15 = (bf16[128,256]{1,0:T(8,128)(2,1)S(1)}, bf16[128,256]{1,0:T(8,128)(2,1)S(1)}, u32[]{:S(2)}, u32[]{:S(2)}) collective-permute-start(bf16[128,256]{1,0:T(8,128)(2,1)S(1)} %bitcast.52), channel_id=1, source_target_pairs={{0,2},{1,3},{2,0},{3,1},{4,6},{5,7},{6,4},{7,5},{8,10},{9,11},{10,... | collective-permute-start | bytes 196616 | tf_op jit(solution)/shard_map/ppermute | solution.py:269
  38.2 3.4 %collective-permute-start.14 = (bf16[128,256]{1,0:T(8,128)(2,1)S(1)}, bf16[128,256]{1,0:T(8,128)(2,1)S(1)}, u32[]{:S(2)}, u32[]{:S(2)}) collective-permute-start(bf16[128,256]{1,0:T(8,128)(2,1)S(1)} %bitcast.53), channel_id=1, source_target_pairs={{0,1},{1,0},{2,3},{3,2},{4,5},{5,4},{6,7},{7,6},{8,9},{9,8},{10,11... | collective-permute-start | bytes 196616 | tf_op jit(solution)/shard_map/ppermute | solution.py:269
  41.0 1.3 %collective-permute-start.16 = (bf16[128,256]{1,0:T(8,128)(2,1)S(1)}, bf16[128,256]{1,0:T(8,128)(2,1)S(1)}, u32[]{:S(2)}, u32[]{:S(2)}) collective-permute-start(bf16[128,256]{1,0:T(8,128)(2,1)S(1)} %collective-permute-done.15), channel_id=1, source_target_pairs={{0,1},{1,0},{2,3},{3,2},{4,5},{5,4},{6,7},{7,6},{8,9},{9,8},{10,11... | collective-permute-start | bytes 196616 | tf_op jit(solution)/shard_map/ppermute | solution.py:269

commit v5 on v4

--- a/solution.py
+++ b/solution.py
@@ -89,25 +89,28 @@
     )(defocus, images)
 
 
-class Reach:
-    def __init__(self, me_ref, index_ref, block_rows):
-        self.me, self.index, self.block_rows = me_ref[0], index_ref, block_rows
-
-    def __call__(self, j, flip):
-        block = self.index[j, jnp.bitwise_xor(self.me, flip)]
-        return pl.ds(pl.multiple_of(block * self.block_rows, self.block_rows), self.block_rows)
-
-
-def add_up_scores(reach, flips, orient_ref, row_ref, fwd_ref, u_ref, part_refs, store):
+class Places:
+    def __init__(self, first_ref, orient_ref, block_rows):
+        self.first_ref, self.orient_ref, self.block_rows = first_ref, orient_ref, block_rows
+        self.picks = orient_ref.shape[0]
+
+    def rows(self, i, k, flip):
+        first = self.first_ref[self.orient_ref[k, i], flip]
+        return pl.ds(pl.multiple_of(first, self.block_rows), self.block_rows)
+
+    def orientation(self, i, k):
+        return self.orient_ref[k, i]
+
+
+def add_up_scores(places, flips, row_ref, fwd_ref, u_ref, part_refs, store):
     count, fourier = u_ref.shape[0], u_ref.shape[1]
-    picks = orient_ref.shape[0]
-    rows = reach.block_rows
+    picks, rows = places.picks, places.block_rows
     for i in range(count):
         products, row_parts = [], []
         for k in range(picks):
-            j = orient_ref[k, i]
+            j = places.orientation(i, k)
             for flip, part_ref in zip(flips, part_refs):
-                where = reach(j, flip)
+                where = places.rows(i, k, flip)
                 real_u = u_ref[i, where, :fourier]
                 imag_u = u_ref[i, where, fourier:]
                 real_p = part_ref[j, :, :fourier].astype(jnp.float32)
@@ -131,23 +134,22 @@
             store(k, i, jnp.sum(mixed, axis=0, keepdims=True))
 
 
-def add_up_slices(reach, flips, orient_ref, row_ref, back_ref, u_ref, rounded_ref, total):
+def add_up_slices(places, flips, row_ref, back_ref, u_ref, rounded_ref, total):
     count, fourier = u_ref.shape[0], u_ref.shape[1]
-    picks = orient_ref.shape[0]
-    rows = reach.block_rows
+    picks, rows = places.picks, places.block_rows
     total[...] = jnp.zeros_like(total)
     for i in range(count):
         mixed = []
         for k in range(picks):
-            j = orient_ref[k, i]
+            j = places.orientation(i, k)
             weight = rounded_ref[k, i : i + 1, :]
             for flip in flips:
-                mixed.append((row_ref[reach(j, flip), :] * weight).astype(jnp.bfloat16))
+                mixed.append((row_ref[places.rows(i, k, flip), :] * weight).astype(jnp.bfloat16))
         spread = jnp.dot(jnp.concatenate(mixed, axis=0), back_ref[...], preferred_element_type=jnp.float32)
         for k in range(picks):
-            j = orient_ref[k, i]
+            j = places.orientation(i, k)
             for s, flip in enumerate(flips):
-                where = reach(j, flip)
+                where = places.rows(i, k, flip)
                 at = (k * len(flips) + s) * rows
                 real_u = u_ref[i, where, :fourier]
                 imag_u = u_ref[i, where, fourier:]
@@ -160,22 +162,33 @@
 def first_scores(me, block_index, orient, tables, u, parts, flips):
     count, fourier, width = u.shape
     picks = orient.shape[0]
+    orient_count, slab_count = block_index.shape
     block_rows = parts[0].shape[1]
 
     def kernel(me_ref, index_ref, orient_ref, row_ref, fwd_ref, u_ref, *rest):
-        part_refs, score_ref = rest[:-1], rest[-1]
-        reach = Reach(me_ref, index_ref, block_rows)
+        part_refs, (score_ref, first_out, orient_out) = rest[:-3], rest[-3:]
+        for j in range(orient_count):
+            for flip in range(slab_count):
+                first_out[j, flip] = index_ref[j, jnp.bitwise_xor(me_ref[0], flip)] * block_rows
+        for i in range(count):
+            for k in range(picks):
+                orient_out[k, i] = orient_ref[k, i]
+        places = Places(first_out, orient_out, block_rows)
 
         def store(k, i, value):
             score_ref[k, i : i + 1, :] = value
 
-        add_up_scores(reach, flips, orient_ref, row_ref, fwd_ref, u_ref, part_refs, store)
+        add_up_scores(places, flips, row_ref, fwd_ref, u_ref, part_refs, store)
 
     return pl.pallas_call(
         kernel,
-        out_shape=pltpu.VMEM((picks, count, LANES), jnp.float32),
+        out_shape=(
+            pltpu.VMEM((picks, count, LANES), jnp.float32),
+            pltpu.SMEM(block_index.shape, jnp.int32),
+            pltpu.SMEM(orient.shape, jnp.int32),
+        ),
         in_specs=[SMEM] * 3 + [VMEM] * (3 + len(parts)),
-        out_specs=VMEM,
+        out_specs=(VMEM, SMEM, SMEM),
         compiler_params=pltpu.CompilerParams(vmem_limit_bytes=VMEM_LIMIT),
         cost_estimate=pl.CostEstimate(
             flops=len(parts) * count * picks * block_rows * width * LANES * 2,
@@ -186,20 +199,20 @@
     )(me, block_index, orient, *tables[:2], u, *parts)
 
 
-def expectation(me, block_index, orient, tables, u, parts, flips, scores, out_flips):
+def expectation(first, orient, tables, u, parts, flips, scores, out_flips):
     count, fourier, width = u.shape
     picks = orient.shape[0]
     orient_count, block_rows, _ = parts[0].shape
 
-    def kernel(me_ref, index_ref, orient_ref, row_ref, fwd_ref, back_ref, u_ref, score_ref, *rest):
+    def kernel(first_ref, orient_ref, row_ref, fwd_ref, back_ref, u_ref, score_ref, *rest):
         part_refs = rest[: len(parts)]
         weights_ref, rounded_ref, rows_ref, total = rest[len(parts) :]
-        reach = Reach(me_ref, index_ref, block_rows)
+        places = Places(first_ref, orient_ref, block_rows)
 
         def store(k, i, value):
             rounded_ref[k, i : i + 1, :] = value
 
-        add_up_scores(reach, flips, orient_ref, row_ref, fwd_ref, u_ref, part_refs, store)
+        add_up_scores(places, flips, row_ref, fwd_ref, u_ref, part_refs, store)
         squared = []
         for k in range(picks):
             value = rounded_ref[k] + score_ref[k]
@@ -216,7 +229,7 @@
             merged = jnp.where(lane == k, value, merged)
             rounded_ref[k] = value.astype(jnp.bfloat16).astype(jnp.float32)
         weights_ref[0] = merged[:, : picks * NS]
-        add_up_slices(reach, out_flips, orient_ref, row_ref, back_ref, u_ref, rounded_ref, total)
+        add_up_slices(places, out_flips, row_ref, back_ref, u_ref, rounded_ref, total)
         rows_ref[...] = total[...].astype(jnp.bfloat16)
 
     return pl.pallas_call(
@@ -226,7 +239,7 @@
             pltpu.VMEM((picks, count, LANES), jnp.float32),
             pltpu.VMEM((len(out_flips), orient_count, block_rows, width), jnp.bfloat16),
         ),
-        in_specs=[SMEM] * 3 + [VMEM] * (5 + len(parts)),
+        in_specs=[SMEM] * 2 + [VMEM] * (5 + len(parts)),
         out_specs=(VMEM,) * 3,
         scratch_shapes=[pltpu.VMEM((len(out_flips), orient_count, block_rows, width), jnp.float32)],
         compiler_params=pltpu.CompilerParams(vmem_limit_bytes=VMEM_LIMIT),
@@ -236,23 +249,22 @@
             transcendentals=0,
         ),
         name="expectation",
-    )(me, block_index, orient, *tables, u, scores, *parts)
-
-
-def last_slices(me, block_index, orient, tables, u, rounded, block_rows, out_flips):
+    )(first, orient, *tables, u, scores, *parts)
+
+
+def more_slices(first, orient, tables, u, rounded, block_rows, out_flips):
     count, fourier, width = u.shape
-    picks = orient.shape[0]
-    orient_count = block_index.shape[0]
-
-    def kernel(me_ref, index_ref, orient_ref, row_ref, back_ref, u_ref, rounded_ref, rows_ref, total):
-        reach = Reach(me_ref, index_ref, block_rows)
-        add_up_slices(reach, out_flips, orient_ref, row_ref, back_ref, u_ref, rounded_ref, total)
+    picks, orient_count = orient.shape[0], first.shape[0]
+
+    def kernel(first_ref, orient_ref, row_ref, back_ref, u_ref, rounded_ref, rows_ref, total):
+        places = Places(first_ref, orient_ref, block_rows)
+        add_up_slices(places, out_flips, row_ref, back_ref, u_ref, rounded_ref, total)
         rows_ref[...] = total[...].astype(jnp.bfloat16)
 
     return pl.pallas_call(
         kernel,
         out_shape=pltpu.VMEM((len(out_flips), orient_count, block_rows, width), jnp.bfloat16),
-        in_specs=[SMEM] * 3 + [VMEM] * 4,
+        in_specs=[SMEM] * 2 + [VMEM] * 4,
         out_specs=VMEM,
         scratch_shapes=[pltpu.VMEM((len(out_flips), orient_count, block_rows, width), jnp.float32)],
         compiler_params=pltpu.CompilerParams(vmem_limit_bytes=VMEM_LIMIT),
@@ -261,8 +273,8 @@
             bytes_accessed=4 * count * fourier * width,
             transcendentals=0,
         ),
-        name="last_slices",
-    )(me, block_index, orient, tables[0], tables[2], u, rounded)
+        name="more_slices",
+    )(first, orient, tables[0], tables[2], u, rounded)
 
 
 def swap(value, axis, size, flip):
@@ -289,29 +301,31 @@
     own = own.reshape(orient_count, block_rows, width)
     from_other, from_far, from_near, from_side = (to(own, flip) for flip in (other, far, near, side))
     from_near_side = to(from_near, side)
+    me = lax.axis_index("slab").astype(jnp.int32).reshape(1)
     u = weigh_images(images, defocus)
     from_far, from_other, u, from_side, from_near_side = lax.optimization_barrier((from_far, from_other, u, from_side, from_near_side))
     from_far_side, from_other_side = to(jnp.stack([from_far, from_other]), side)
 
-    common = lax.axis_index("slab").astype(jnp.int32).reshape(1), block_index[0], orient[0].T, separable_tables(fourier), u
-    scores = first_scores(*common, [own, from_near, from_far, from_other, from_side, from_near_side], (0, near, far, other, side, near + side))
+    tables = separable_tables(fourier)
+    scores, first, choice = first_scores(me, block_index[0], orient[0].T, tables, u, [own, from_near, from_far, from_other, from_side, from_near_side], (0, near, far, other, side, near + side))
     late_weigher, scores = lax.optimization_barrier((weigher, scores))
     weigher_across = swap(late_weigher, "img", group_count, 2)
+    common = first, choice, tables, u
     weights, rounded, side_rows = expectation(
         *common,
         [from_far_side, from_other_side],
         (far + side, other + side),
         scores,
-        (other + side, far + side, near + side, side),
-    )
-    first = to(side_rows[0], side)
-    rest = to(side_rows[1:], side)
-    weigher_across, rounded = lax.optimization_barrier((weigher_across, rounded))
-    rows = last_slices(*common, rounded, block_rows, (other, far, near, 0))
+        (other + side,),
+    )
+    sent_first = to(side_rows[0], side)
+    rest = to(more_slices(*common, rounded, block_rows, (far + side, near + side, side)), side)
+    weigher_across, sent_first = lax.optimization_barrier((weigher_across, sent_first))
+    rows = more_slices(*common, rounded, block_rows, (other, far, near, 0))
     back = together(
         rows[3],
         rest[2],
-        to(together(rows[0], first), other),
+        to(together(rows[0], sent_first), other),
         to(together(rows[1], rest[0]), far),
         to(together(rows[2], rest[1]), near),
     ).reshape(orient_count * block_rows, width)

time: 43.6 us -> 42.6 us (0.977)
  Pallas kernels: 8.58 us -> 7.1 us
  starting transfers between devices: 21.6 us -> 22.5 us
    pallas_call x1, Pallas kernels: 2.81 us -> 1.29 us  [expectation(): pl.pallas_call(kernel, out_shape=(pltpu.VMEM((1, count, picks * NS), jnp....]
    ppermute x17, starting transfers between devices: 21.6 us -> 22.5 us  [swap(): lax.ppermute(value, axis, [(source, source ^ flip) for source in range(si...]
    pallas_call x2 -> x3, Pallas kernels: 4.17 us -> 4.21 us  [the longest x1 2.14 us: first_scores(): pl.pallas_call(kernel, out_shape=(pltpu.VMEM((picks, count, LANES), jnp.f...]
  transfers between devices with their start and end apart: 17 -> 17, of which waited for: 6 -> 6; matrix products, arithmetic and copies ran while one was open for 2% -> 2% of each run, Pallas kernels for 20% -> 17%
where the time goes in v5:
time: 42.6 us; the launch traced here: 42.4 us
  starting transfers between devices  22.5 us (53%)
  Pallas kernels  7.1 us (17%)
  waiting for transfers between devices  6.23 us (15%)
  local copies, waits for them, and re-layouts  3.43 us (8%)
  matrix products  2.22 us (5%)
  between operations  0.8 us (2%)
    ppermute x17, starting transfers between devices, swap(): lax.ppermute(value, axis, [(source, source ^ flip) for source in range(si...  22.5 us
    ppermute x17, waiting for transfers between devices, swap(): lax.ppermute(value, axis, [(source, source ^ flip) for source in range(si...  6.23 us
    unnamed x19, local copies, waits for them, and re-layouts  3.42 us
    pallas_call x1, Pallas kernels, first_scores(): pl.pallas_call(kernel, out_shape=(pltpu.VMEM((picks, count, LANES), jnp.f...  2.14 us
    pallas_call x2, Pallas kernels, more_slices(): pl.pallas_call(kernel, out_shape=pltpu.VMEM((len(out_flips), orient_count...  2.07 us
    pallas_call x1, Pallas kernels, weigh_images(): pl.pallas_call(kernel, out_shape=pltpu.VMEM(images.shape[1:], jnp.float32...  1.6 us
    pallas_call x1, Pallas kernels, expectation(): pl.pallas_call(kernel, out_shape=(pltpu.VMEM((1, count, picks * NS), jnp....  1.29 us
    dot_general x1, matrix products, direct(): lax.dot_general(jnp.concatenate(weighers, axis=0), jnp.concatenate(backs,...  1.13 us
  transfers between devices with their start and end apart: 17, of which 6 were waited for; matrix products, arithmetic and copies ran while one was open for 2% of the time, Pallas kernels for 17%

profile of v5, /device:TPU:0, one launch (start us, length us, event | category | flops | bytes accessed | tf_op | source)
XLA Modules:
  0.0 42.4 jit_solution(12336722264755774634)
XLA Ops:
  0.6 0.0 copy-start
  0.6 0.0 copy-start.1
  0.7 0.9 %copy-done = bf16[512,256]{1,0:T(8,128)(2,1)S(1)} copy-done((bf16[512,256]{1,0:T(8,128)(2,1)S(1)}, bf16[512,256]{1,0:T(8,128)(2,1)}, u32[]{:S(2)}) %copy-start) | copy-done | bytes 262168
  1.6 1.1 %convolution_convert_fusion = bf16[128,256]{1,0:T(8,128)(2,1)S(1)} fusion(bf16[128,512]{1,0:T(8,128)(2,1)} %bitcast.44, bf16[512,256]{1,0:T(8,128)(2,1)S(1)} %copy-done), kind=kOutput, calls=%fused_computation.1 | convolution fusion | flops 33587200 | bytes 458752 | tf_op jit(solution)/shard_map/dot_general | solution.py:300
  2.7 3.1 %collective-permute-start.4 = (bf16[8,16,256]{2,1,0:T(8,128)(2,1)S(1)}, bf16[8,16,256]{2,1,0:T(8,128)(2,1)S(1)}, u32[]{:S(2)}, u32[]{:S(2)}) collective-permute-start(bf16[8,16,256]{2,1,0:T(8,128)(2,1)S(1)} %bitcast.34), channel_id=1, source_target_pairs={{0,8},{4,12},{8,0},{12,4},{16,24},{20,28},{24,16},{28,20},{1,9},{5... | collective-permute-start | bytes 196616 | tf_op jit(solution)/shard_map/ppermute | solution.py:281
  5.8 2.6 %collective-permute-start.1 = (bf16[8,16,256]{2,1,0:T(8,128)(2,1)S(1)}, bf16[8,16,256]{2,1,0:T(8,128)(2,1)S(1)}, u32[]{:S(2)}, u32[]{:S(2)}) collective-permute-start(bf16[8,16,256]{2,1,0:T(8,128)(2,1)S(1)} %bitcast.35), channel_id=1, source_target_pairs={{0,16},{4,20},{8,24},{12,28},{16,0},{20,4},{24,8},{28,12},{1,17},{... | collective-permute-start | bytes 196616 | tf_op jit(solution)/shard_map/ppermute | solution.py:281
  8.4 1.7 %collective-permute-start.3 = (bf16[8,16,256]{2,1,0:T(8,128)(2,1)S(1)}, bf16[8,16,256]{2,1,0:T(8,128)(2,1)S(1)}, u32[]{:S(2)}, u32[]{:S(2)}) collective-permute-start(bf16[8,16,256]{2,1,0:T(8,128)(2,1)S(1)} %bitcast.37), channel_id=1, source_target_pairs={{0,4},{4,0},{8,12},{12,8},{16,20},{20,16},{24,28},{28,24},{1,5},{5... | collective-permute-start | bytes 196616 | tf_op jit(solution)/shard_map/ppermute | solution.py:281
  10.1 0.3 collective-permute-start.5
  10.4 1.2 %copy-done.2 = bf16[1,16,128,256]{3,2,1,0:T(8,128)(2,1)S(1)} copy-done((bf16[1,16,128,256]{3,2,1,0:T(8,128)(2,1)S(1)}, bf16[1,16,128,256]{3,2,1,0:T(8,128)(2,1)}, u32[]{:S(2)}) %copy-start.2) | copy-done | bytes 1048600
  11.6 0.7 %copy-done.7 = f32[1,16]{1,0:T(1,128)S(1)} copy-done((f32[1,16]{1,0:T(1,128)S(1)}, f32[1,16]{1,0:T(1,128)}, u32[]{:S(2)}) %copy-start.7) | copy-done | bytes 88
  12.3 1.6 %weigh_images.1.u_ref = f32[16,128,256]{2,1,0:T(8,128)S(1)} custom-call(f32[1,16]{1,0:T(1,128)S(1)} %copy-done.7, bf16[1,16,128,256]{3,2,1,0:T(8,128)(2,1)S(1)} %copy-done.2), custom_call_target="tpu_custom_call" | custom-call | flops 7864320 | bytes 3145728 | tf_op jit(solution)/shard_map/weigh_images/pallas_call | solution.py:79
  13.9 0.5 %collective-permute-done.2.rest_3_ = bf16[8,16,256]{2,1,0:T(8,128)(2,1)S(1)} collective-permute-done((bf16[8,16,256]{2,1,0:T(8,128)(2,1)S(1)}, bf16[8,16,256]{2,1,0:T(8,128)(2,1)S(1)}, u32[]{:S(2)}, u32[]{:S(2)}) %collective-permute-start.2) | collective-permute-done | bytes 65568 | tf_op jit(solution)/shard_map/ppermute | solution.py:281
  14.5 1.6 %collective-permute-start.7 = (bf16[2,8,16,256]{3,2,1,0:T(8,128)(2,1)S(1)}, bf16[2,8,16,256]{3,2,1,0:T(8,128)(2,1)S(1)}, u32[]{:S(2)}, u32[]{:S(2)}) collective-permute-start(bf16[2,8,16,256]{3,2,1,0:T(8,128)(2,1)S(1)} %pad_maximum_fusion), channel_id=1, source_target_pairs={{0,4},{4,0},{8,12},{12,8},{16,20},{20,16},{24,28},{28,24},{1,5},{5... | collective-permute-start | bytes 393224 | tf_op jit(solution)/shard_map/ppermute | solution.py:281
  16.0 2.1 %first_scores.1 = (f32[4,16,128]{2,1,0:T(8,128)S(1)}, s32[8,8]{1,0:T(8,128)S(4)}, s32[4,16]{1,0:T(4,128)S(4)}) custom-call(s32[1]{0:T(128)} %bitcast.1.me_ref, s32[8,8]{1,0:T(8,128)S(1)} %bitcast.41, s32[4,16]{1,0:T(4,128)S(1)} %bitcast.42, f32[128,128]{1,0:T(8,128)S(1)} %copy-done.1, bf16[256,128]{1,0:T(8,128)(2,1)S(1)} %copy-done.4, ...), custom_call_target="tpu_custom_call" | custom-call | flops 402653184 | bytes 2097152 | tf_op jit(solution)/shard_map/first_scores/pallas_call | solution.py:183
  18.2 1.6 %collective-permute-start.6 = (bf16[128,512]{1,0:T(8,128)(2,1)S(1)}, bf16[128,512]{1,0:T(8,128)(2,1)S(1)}, u32[]{:S(2)}, u32[]{:S(2)}) collective-permute-start(bf16[128,512]{1,0:T(8,128)(2,1)S(1)} %bitcast.45), channel_id=1, source_target_pairs={{0,2},{1,3},{2,0},{3,1},{4,6},{5,7},{6,4},{7,5},{8,10},{9,11},{10,... | collective-permute-start | bytes 393224 | tf_op jit(solution)/shard_map/ppermute | solution.py:281
  19.8 1.3 %expectation.1 = (f32[1,16,64]{2,1,0:T(8,128)S(1)}, f32[4,16,128]{2,1,0:T(8,128)S(1)}, bf16[1,8,16,256]{3,2,1,0:T(8,128)(2,1)S(1)}) custom-call(s32[8,8]{1,0:T(8,128)S(4)} %get-tuple-element.24.first_ref, s32[4,16]{1,0:T(4,128)S(4)} %get-tuple-element.25.orient_ref, f32[128,128]{1,0:T(8,128)S(1)} %copy-done.1, bf16[256,128]{1,0:T(8,128)(2,1)S(1)} %copy-done.4, ...), custom_call_target="tpu_custom_call" | custom-call | flops 201326592 | bytes 2097152 | tf_op jit(solution)/shard_map/expectation/pallas_call | solution.py:235
  21.1 1.3 %collective-permute-start.8 = (bf16[8,16,256]{2,1,0:T(8,128)(2,1)S(1)}, bf16[8,16,256]{2,1,0:T(8,128)(2,1)S(1)}, u32[]{:S(2)}, u32[]{:S(2)}) collective-permute-start(bf16[8,16,256]{2,1,0:T(8,128)(2,1)S(1)} %bitcast.43), channel_id=1, source_target_pairs={{0,4},{4,0},{8,12},{12,8},{16,20},{20,16},{24,28},{28,24},{1,5},{5... | collective-permute-start | bytes 196616 | tf_op jit(solution)/shard_map/ppermute | solution.py:281
  22.4 0.9 %more_slices.3 = bf16[3,8,16,256]{3,2,1,0:T(8,128)(2,1)S(1)} custom-call(s32[8,8]{1,0:T(8,128)S(4)} %get-tuple-element.24.first_ref, s32[4,16]{1,0:T(4,128)S(4)} %get-tuple-element.25.orient_ref, f32[128,128]{1,0:T(8,128)S(1)} %copy-done.1, bf16[128,256]{1,0:T(8,128)(2,1)S(1)} %copy-done.3, f32[16,128,256]{2,1,0:T(8,128)S(1)} %weigh_images.1.u_ref, ...), custom_call_target="tpu_custom_call" | custom-call | flops 201326592 | bytes 2097152 | tf_op jit(solution)/shard_map/more_slices/pallas_call | solution.py:264
  23.3 0.9 %collective-permute-start.10 = (bf16[3,8,16,256]{3,2,1,0:T(8,128)(2,1)S(1)}, bf16[3,8,16,256]{3,2,1,0:T(8,128)(2,1)S(1)}, u32[]{:S(2)}, u32[]{:S(2)}) collective-permute-start(bf16[3,8,16,256]{3,2,1,0:T(8,128)(2,1)S(1)} %more_slices.3), channel_id=1, source_target_pairs={{0,4},{4,0},{8,12},{12,8},{16,20},{20,16},{24,28},{28,24},{1,5},{5... | collective-permute-start | bytes 589832 | tf_op jit(solution)/shard_map/ppermute | solution.py:281
  24.2 1.2 %more_slices.2 = bf16[4,8,16,256]{3,2,1,0:T(8,128)(2,1)S(1)} custom-call(s32[8,8]{1,0:T(8,128)S(4)} %get-tuple-element.24.first_ref, s32[4,16]{1,0:T(4,128)S(4)} %get-tuple-element.25.orient_ref, f32[128,128]{1,0:T(8,128)S(1)} %copy-done.1, bf16[128,256]{1,0:T(8,128)(2,1)S(1)} %copy-done.3, f32[16,128,256]{2,1,0:T(8,128)S(1)} %weigh_images.1.u_ref, ...), custom_call_target="tpu_custom_call" | custom-call | flops 268435456 | bytes 2097152 | tf_op jit(solution)/shard_map/more_slices/pallas_call | solution.py:264
  25.3 0.2 collective-permute-done.8
  25.6 3.6 %collective-permute-start.11 = (bf16[8,16,256]{2,1,0:T(8,128)(2,1)S(1)}, bf16[8,16,256]{2,1,0:T(8,128)(2,1)S(1)}, u32[]{:S(2)}, u32[]{:S(2)}) collective-permute-start(bf16[8,16,256]{2,1,0:T(8,128)(2,1)S(1)} %fusion.14), channel_id=1, source_target_pairs={{0,24},{4,28},{8,16},{12,20},{16,8},{20,12},{24,0},{28,4},{1,25},{... | collective-permute-start | bytes 196616 | tf_op jit(solution)/shard_map/ppermute | solution.py:281
  29.2 1.5 %collective-permute-start.12 = (bf16[8,16,256]{2,1,0:T(8,128)(2,1)S(1)}, bf16[8,16,256]{2,1,0:T(8,128)(2,1)S(1)}, u32[]{:S(2)}, u32[]{:S(2)}) collective-permute-start(bf16[8,16,256]{2,1,0:T(8,128)(2,1)S(1)} %get-tuple-element.32), channel_id=1, source_target_pairs={{0,16},{4,20},{8,24},{12,28},{16,0},{20,4},{24,8},{28,12},{1,17},{... | collective-permute-start | bytes 196616 | tf_op jit(solution)/shard_map/ppermute | solution.py:281
  30.7 2.3 %collective-permute-start.13 = (bf16[8,16,256]{2,1,0:T(8,128)(2,1)S(1)}, bf16[8,16,256]{2,1,0:T(8,128)(2,1)S(1)}, u32[]{:S(2)}, u32[]{:S(2)}) collective-permute-start(bf16[8,16,256]{2,1,0:T(8,128)(2,1)S(1)} %get-tuple-element.33), channel_id=1, source_target_pairs={{0,8},{4,12},{8,0},{12,4},{16,24},{20,28},{24,16},{28,20},{1,9},{5... | collective-permute-start | bytes 196616 | tf_op jit(solution)/shard_map/ppermute | solution.py:281
  33.0 0.5 %collective-permute-start.9 = (bf16[128,512]{1,0:T(8,128)(2,1)S(1)}, bf16[128,512]{1,0:T(8,128)(2,1)S(1)}, u32[]{:S(2)}, u32[]{:S(2)}) collective-permute-start(bf16[128,512]{1,0:T(8,128)(2,1)S(1)} %collective-permute-done.6), channel_id=1, source_target_pairs={{0,1},{1,0},{2,3},{3,2},{4,5},{5,4},{6,7},{7,6},{8,9},{9,8},{10,11... | collective-permute-start | bytes 393224 | tf_op jit(solution)/shard_map/ppermute | solution.py:281
  33.5 1.7 %collective-permute-done.12 = bf16[8,16,256]{2,1,0:T(8,128)(2,1)S(1)} collective-permute-done((bf16[8,16,256]{2,1,0:T(8,128)(2,1)S(1)}, bf16[8,16,256]{2,1,0:T(8,128)(2,1)S(1)}, u32[]{:S(2)}, u32[]{:S(2)}) %collective-permute-start.12) | collective-permute-done | bytes 65568 | tf_op jit(solution)/shard_map/ppermute | solution.py:281
  35.3 0.4 collective-permute-done.13
  35.7 1.6 %collective-permute-start.15 = (bf16[128,256]{1,0:T(8,128)(2,1)S(1)}, bf16[128,256]{1,0:T(8,128)(2,1)S(1)}, u32[]{:S(2)}, u32[]{:S(2)}) collective-permute-start(bf16[128,256]{1,0:T(8,128)(2,1)S(1)} %bitcast.48), channel_id=1, source_target_pairs={{0,2},{1,3},{2,0},{3,1},{4,6},{5,7},{6,4},{7,5},{8,10},{9,11},{10,... | collective-permute-start | bytes 196616 | tf_op jit(solution)/shard_map/ppermute | solution.py:281
  37.2 2.7 %collective-permute-done.15 = bf16[128,256]{1,0:T(8,128)(2,1)S(1)} collective-permute-done((bf16[128,256]{1,0:T(8,128)(2,1)S(1)}, bf16[128,256]{1,0:T(8,128)(2,1)S(1)}, u32[]{:S(2)}, u32[]{:S(2)}) %collective-permute-start.15) | collective-permute-done | bytes 65568 | tf_op jit(solution)/shard_map/ppermute | solution.py:281
  40.0 0.6 %copy.11 = f32[1,16,64]{2,1,0:T(8,128)} copy(f32[1,16,64]{2,1,0:T(8,128)S(1)} %get-tuple-element.37) | data formatting | bytes 8192
  40.6 0.6 %collective-permute-done.16 = bf16[128,256]{1,0:T(8,128)(2,1)S(1)} collective-permute-done((bf16[128,256]{1,0:T(8,128)(2,1)S(1)}, bf16[128,256]{1,0:T(8,128)(2,1)S(1)}, u32[]{:S(2)}, u32[]{:S(2)}) %collective-permute-start.16) | collective-permute-done | bytes 65568 | tf_op jit(solution)/shard_map/ppermute | solution.py:281
  41.2 1.1 %convolution_multiply_fusion = f32[512,256]{1,0:T(8,128)} fusion(bf16[128,512]{1,0:T(8,128)(2,1)S(1)} %collective-permute-done.9, bf16[128,512]{1,0:T(8,128)(2,1)S(1)} %collective-permute-done.6, bf16[128,512]{1,0:T(8,128)(2,1)S(1)} %collective-permute-done, bf16[128,512]{1,0:T(8,128)(2,1)S(1)} %bitcast.47, bf16[128,256]{1,0:T(8,128)(2,1)S(1)} %collective-permute-done.16, ...), kind=kOutput, calls=%fused_computation | convolution fusion | flops 137494528 | bytes 1310720 | tf_op jit(solution)/shard_map/dot_general | solution.py:339
  (33 shorter events, 0.2 us)
Async XLA Ops:
  0.6 1.0 %copy-start = (bf16[512,256]{1,0:T(8,128)(2,1)S(1)}, bf16[512,256]{1,0:T(8,128)(2,1)}, u32[]{:S(2)}) copy-start(bf16[512,256]{1,0:T(8,128)(2,1)} %param.9) | copy-start | bytes 786436
  0.6 15.4 %copy-start.1 = (f32[128,128]{1,0:T(8,128)S(1)}, f32[128,128]{1,0:T(8,128)}, u32[]{:S(2)}) copy-start(f32[128,128]{1,0:T(8,128)} %constant.15.clone.row_ref) | copy-start | bytes 196612
  0.7 15.4 %copy-start.4 = (bf16[256,128]{1,0:T(8,128)(2,1)S(1)}, bf16[256,128]{1,0:T(8,128)(2,1)}, u32[]{:S(2)}) copy-start(bf16[256,128]{1,0:T(8,128)(2,1)} %constant.16.clone.fwd_ref) | copy-start | bytes 196612
  0.7 15.4 %copy-start.5 = (s32[1,8,8]{2,1,0:T(8,128)S(1)}, s32[1,8,8]{2,1,0:T(8,128)}, u32[]{:S(2)}) copy-start(s32[1,8,8]{2,1,0:T(8,128)} %param.11) | copy-start | bytes 772
  0.7 15.4 %copy-start.6 = (s32[1,16,4]{1,2,0:T(4,128)S(1)}, s32[1,16,4]{1,2,0:T(4,128)}, u32[]{:S(2)}) copy-start(s32[1,16,4]{1,2,0:T(4,128)} %param.14) | copy-start | bytes 772
  2.7 7.4 %collective-permute-start.4 = (bf16[8,16,256]{2,1,0:T(8,128)(2,1)S(1)}, bf16[8,16,256]{2,1,0:T(8,128)(2,1)S(1)}, u32[]{:S(2)}, u32[]{:S(2)}) collective-permute-start(bf16[8,16,256]{2,1,0:T(8,128)(2,1)S(1)} %bitcast.34), channel_id=1, source_target_pairs={{0,8},{4,12},{8,0},{12,4},{16,24},{20,28},{24,16},{28,20},{1,9},{5... | collective-permute-start | bytes 196616 | tf_op jit(solution)/shard_map/ppermute | solution.py:281
  5.8 8.1 %collective-permute-start.1 = (bf16[8,16,256]{2,1,0:T(8,128)(2,1)S(1)}, bf16[8,16,256]{2,1,0:T(8,128)(2,1)S(1)}, u32[]{:S(2)}, u32[]{:S(2)}) collective-permute-start(bf16[8,16,256]{2,1,0:T(8,128)(2,1)S(1)} %bitcast.35), channel_id=1, source_target_pairs={{0,16},{4,20},{8,24},{12,28},{16,0},{20,4},{24,8},{28,12},{1,17},{... | collective-permute-start | bytes 196616 | tf_op jit(solution)/shard_map/ppermute | solution.py:281
  8.4 6.1 %collective-permute-start.2 = (bf16[8,16,256]{2,1,0:T(8,128)(2,1)S(1)}, bf16[8,16,256]{2,1,0:T(8,128)(2,1)S(1)}, u32[]{:S(2)}, u32[]{:S(2)}) collective-permute-start(bf16[8,16,256]{2,1,0:T(8,128)(2,1)S(1)} %bitcast.36), channel_id=1, source_target_pairs={{0,24},{4,28},{8,16},{12,20},{16,8},{20,12},{24,0},{28,4},{1,25},{... | collective-permute-start | bytes 196616 | tf_op jit(solution)/shard_map/ppermute | solution.py:281
  8.4 6.1 %collective-permute-start.3 = (bf16[8,16,256]{2,1,0:T(8,128)(2,1)S(1)}, bf16[8,16,256]{2,1,0:T(8,128)(2,1)S(1)}, u32[]{:S(2)}, u32[]{:S(2)}) collective-permute-start(bf16[8,16,256]{2,1,0:T(8,128)(2,1)S(1)} %bitcast.37), channel_id=1, source_target_pairs={{0,4},{4,0},{8,12},{12,8},{16,20},{20,16},{24,28},{28,24},{1,5},{5... | collective-permute-start | bytes 196616 | tf_op jit(solution)/shard_map/ppermute | solution.py:281
  10.1 4.4 %collective-permute-start.5 = (bf16[8,16,256]{2,1,0:T(8,128)(2,1)S(1)}, bf16[8,16,256]{2,1,0:T(8,128)(2,1)S(1)}, u32[]{:S(2)}, u32[]{:S(2)}) collective-permute-start(bf16[8,16,256]{2,1,0:T(8,128)(2,1)S(1)} %collective-permute-done.4.rest_1_), channel_id=1, source_target_pairs={{0,4},{4,0},{8,12},{12,8},{16,20},{20,16},{24,28},{28,24},{1,5},{5... | collective-permute-start | bytes 196616 | tf_op jit(solution)/shard_map/ppermute | solution.py:281
  10.4 1.2 %copy-start.2 = (bf16[1,16,128,256]{3,2,1,0:T(8,128)(2,1)S(1)}, bf16[1,16,128,256]{3,2,1,0:T(8,128)(2,1)}, u32[]{:S(2)}) copy-start(bf16[1,16,128,256]{3,2,1,0:T(8,128)(2,1)} %image_ref.1) | copy-start | bytes 3145732
  11.6 0.7 %copy-start.7 = (f32[1,16]{1,0:T(1,128)S(1)}, f32[1,16]{1,0:T(1,128)}, u32[]{:S(2)}) copy-start(f32[1,16]{1,0:T(1,128)} %defocus_ref.1) | copy-start | bytes 196
  13.9 4.3 %copy-start.8 = (bf16[1,8,16,512]{3,2,1,0:T(8,128)(2,1)S(1)}, bf16[1,8,16,512]{3,2,1,0:T(8,128)(2,1)}, u32[]{:S(2)}) copy-start(bf16[1,8,16,512]{3,2,1,0:T(8,128)(2,1)} %param.10) | copy-start | bytes 393220
  13.9 5.9 %copy-start.3 = (bf16[128,256]{1,0:T(8,128)(2,1)S(1)}, bf16[128,256]{1,0:T(8,128)(2,1)}, u32[]{:S(2)}) copy-start(bf16[128,256]{1,0:T(8,128)(2,1)} %constant.17.clone.back_ref) | copy-start | bytes 196612
  14.5 5.3 %collective-permute-start.7 = (bf16[2,8,16,256]{3,2,1,0:T(8,128)(2,1)S(1)}, bf16[2,8,16,256]{3,2,1,0:T(8,128)(2,1)S(1)}, u32[]{:S(2)}, u32[]{:S(2)}) collective-permute-start(bf16[2,8,16,256]{3,2,1,0:T(8,128)(2,1)S(1)} %pad_maximum_fusion), channel_id=1, source_target_pairs={{0,4},{4,0},{8,12},{12,8},{16,20},{20,16},{24,28},{28,24},{1,5},{5... | collective-permute-start | bytes 393224 | tf_op jit(solution)/shard_map/ppermute | solution.py:281
  18.2 7.1 %collective-permute-start.6 = (bf16[128,512]{1,0:T(8,128)(2,1)S(1)}, bf16[128,512]{1,0:T(8,128)(2,1)S(1)}, u32[]{:S(2)}, u32[]{:S(2)}) collective-permute-start(bf16[128,512]{1,0:T(8,128)(2,1)S(1)} %bitcast.45), channel_id=1, source_target_pairs={{0,2},{1,3},{2,0},{3,1},{4,6},{5,7},{6,4},{7,5},{8,10},{9,11},{10,... | collective-permute-start | bytes 393224 | tf_op jit(solution)/shard_map/ppermute | solution.py:281
  21.1 4.5 %collective-permute-start.8 = (bf16[8,16,256]{2,1,0:T(8,128)(2,1)S(1)}, bf16[8,16,256]{2,1,0:T(8,128)(2,1)S(1)}, u32[]{:S(2)}, u32[]{:S(2)}) collective-permute-start(bf16[8,16,256]{2,1,0:T(8,128)(2,1)S(1)} %bitcast.43), channel_id=1, source_target_pairs={{0,4},{4,0},{8,12},{12,8},{16,20},{20,16},{24,28},{28,24},{1,5},{5... | collective-permute-start | bytes 196616 | tf_op jit(solution)/shard_map/ppermute | solution.py:281
  23.3 5.9 %collective-permute-start.10 = (bf16[3,8,16,256]{3,2,1,0:T(8,128)(2,1)S(1)}, bf16[3,8,16,256]{3,2,1,0:T(8,128)(2,1)S(1)}, u32[]{:S(2)}, u32[]{:S(2)}) collective-permute-start(bf16[3,8,16,256]{3,2,1,0:T(8,128)(2,1)S(1)} %more_slices.3), channel_id=1, source_target_pairs={{0,4},{4,0},{8,12},{12,8},{16,20},{20,16},{24,28},{28,24},{1,5},{5... | collective-permute-start | bytes 589832 | tf_op jit(solution)/shard_map/ppermute | solution.py:281
  25.6 7.9 %collective-permute-start.11 = (bf16[8,16,256]{2,1,0:T(8,128)(2,1)S(1)}, bf16[8,16,256]{2,1,0:T(8,128)(2,1)S(1)}, u32[]{:S(2)}, u32[]{:S(2)}) collective-permute-start(bf16[8,16,256]{2,1,0:T(8,128)(2,1)S(1)} %fusion.14), channel_id=1, source_target_pairs={{0,24},{4,28},{8,16},{12,20},{16,8},{20,12},{24,0},{28,4},{1,25},{... | collective-permute-start | bytes 196616 | tf_op jit(solution)/shard_map/ppermute | solution.py:281
  29.2 6.0 %collective-permute-start.12 = (bf16[8,16,256]{2,1,0:T(8,128)(2,1)S(1)}, bf16[8,16,256]{2,1,0:T(8,128)(2,1)S(1)}, u32[]{:S(2)}, u32[]{:S(2)}) collective-permute-start(bf16[8,16,256]{2,1,0:T(8,128)(2,1)S(1)} %get-tuple-element.32), channel_id=1, source_target_pairs={{0,16},{4,20},{8,24},{12,28},{16,0},{20,4},{24,8},{28,12},{1,17},{... | collective-permute-start | bytes 196616 | tf_op jit(solution)/shard_map/ppermute | solution.py:281
  30.7 4.9 %collective-permute-start.13 = (bf16[8,16,256]{2,1,0:T(8,128)(2,1)S(1)}, bf16[8,16,256]{2,1,0:T(8,128)(2,1)S(1)}, u32[]{:S(2)}, u32[]{:S(2)}) collective-permute-start(bf16[8,16,256]{2,1,0:T(8,128)(2,1)S(1)} %get-tuple-element.33), channel_id=1, source_target_pairs={{0,8},{4,12},{8,0},{12,4},{16,24},{20,28},{24,16},{28,20},{1,9},{5... | collective-permute-start | bytes 196616 | tf_op jit(solution)/shard_map/ppermute | solution.py:281
  33.0 7.6 %collective-permute-start = (bf16[128,512]{1,0:T(8,128)(2,1)S(1)}, bf16[128,512]{1,0:T(8,128)(2,1)S(1)}, u32[]{:S(2)}, u32[]{:S(2)}) collective-permute-start(bf16[128,512]{1,0:T(8,128)(2,1)S(1)} %bitcast.46), channel_id=1, source_target_pairs={{0,1},{1,0},{2,3},{3,2},{4,5},{5,4},{6,7},{7,6},{8,9},{9,8},{10,11... | collective-permute-start | bytes 393224 | tf_op jit(solution)/shard_map/ppermute | solution.py:281
  33.0 7.6 %collective-permute-start.9 = (bf16[128,512]{1,0:T(8,128)(2,1)S(1)}, bf16[128,512]{1,0:T(8,128)(2,1)S(1)}, u32[]{:S(2)}, u32[]{:S(2)}) collective-permute-start(bf16[128,512]{1,0:T(8,128)(2,1)S(1)} %collective-permute-done.6), channel_id=1, source_target_pairs={{0,1},{1,0},{2,3},{3,2},{4,5},{5,4},{6,7},{7,6},{8,9},{9,8},{10,11... | collective-permute-start | bytes 393224 | tf_op jit(solution)/shard_map/ppermute | solution.py:281
  35.7 4.3 %collective-permute-start.15 = (bf16[128,256]{1,0:T(8,128)(2,1)S(1)}, bf16[128,256]{1,0:T(8,128)(2,1)S(1)}, u32[]{:S(2)}, u32[]{:S(2)}) collective-permute-start(bf16[128,256]{1,0:T(8,128)(2,1)S(1)} %bitcast.48), channel_id=1, source_target_pairs={{0,2},{1,3},{2,0},{3,1},{4,6},{5,7},{6,4},{7,5},{8,10},{9,11},{10,... | collective-permute-start | bytes 196616 | tf_op jit(solution)/shard_map/ppermute | solution.py:281
  37.2 3.4 %collective-permute-start.14 = (bf16[128,256]{1,0:T(8,128)(2,1)S(1)}, bf16[128,256]{1,0:T(8,128)(2,1)S(1)}, u32[]{:S(2)}, u32[]{:S(2)}) collective-permute-start(bf16[128,256]{1,0:T(8,128)(2,1)S(1)} %bitcast.49), channel_id=1, source_target_pairs={{0,1},{1,0},{2,3},{3,2},{4,5},{5,4},{6,7},{7,6},{8,9},{9,8},{10,11... | collective-permute-start | bytes 196616 | tf_op jit(solution)/shard_map/ppermute | solution.py:281
  40.0 1.3 %collective-permute-start.16 = (bf16[128,256]{1,0:T(8,128)(2,1)S(1)}, bf16[128,256]{1,0:T(8,128)(2,1)S(1)}, u32[]{:S(2)}, u32[]{:S(2)}) collective-permute-start(bf16[128,256]{1,0:T(8,128)(2,1)S(1)} %collective-permute-done.15), channel_id=1, source_target_pairs={{0,1},{1,0},{2,3},{3,2},{4,5},{5,4},{6,7},{7,6},{8,9},{9,8},{10,11... | collective-permute-start | bytes 196616 | tf_op jit(solution)/shard_map/ppermute | solution.py:281

commit v6 on v5

--- a/solution.py
+++ b/solution.py
@@ -16,6 +16,7 @@
 amplitude = 0.1
 grid_side = 4
 LANES = 128
+IMAGE_MOVES = 4
 VMEM_LIMIT = 32 << 20
 SMEM = pl.BlockSpec(memory_space=pltpu.SMEM)
 VMEM = pl.BlockSpec(memory_space=pltpu.VMEM)
@@ -64,29 +65,44 @@
 def weigh_images(images, defocus):
     _, count, fourier, width = images.shape
 
-    def kernel(defocus_ref, image_ref, u_ref):
+    def kernel(defocus_hbm, image_hbm, u_ref, defocus_ref, image_ref, defocus_sem, image_sems):
+        moves = [pltpu.make_async_copy(defocus_hbm, defocus_ref, defocus_sem)]
+        for part in range(IMAGE_MOVES):
+            some = pl.ds(part * (count // IMAGE_MOVES), count // IMAGE_MOVES)
+            moves.append(pltpu.make_async_copy(image_hbm.at[0, some], image_ref.at[some], image_sems.at[part]))
+        for move in moves:
+            move.start()
         kx = lax.broadcasted_iota(jnp.int32, (fourier, fourier), 0) - fourier // 2
         ky = lax.broadcasted_iota(jnp.int32, (fourier, fourier), 1) - fourier // 2
         wave_sq = (kx * kx + ky * ky).astype(jnp.float32) * (1.0 / (BOX * BOX))
         slope = wave_sq * (0.5 * wave_length)
         offset = wave_sq * wave_sq * (-0.25 * aberration * wave_length**3)
         offset = offset + math.asin(amplitude) / (2.0 * math.pi)
+        moves[0].wait()
         for i in range(count):
+            if i % (count // IMAGE_MOVES) == 0:
+                moves[1 + i // (count // IMAGE_MOVES)].wait()
             ctf = -sin_turns(defocus_ref[0, i] * slope + offset)
-            u_ref[i, :, :fourier] = ctf * image_ref[0, i, :, :fourier].astype(jnp.float32)
-            u_ref[i, :, fourier:] = ctf * image_ref[0, i, :, fourier:].astype(jnp.float32)
+            u_ref[i, :, :fourier] = ctf * image_ref[i, :, :fourier].astype(jnp.float32)
+            u_ref[i, :, fourier:] = ctf * image_ref[i, :, fourier:].astype(jnp.float32)
 
     return pl.pallas_call(
         kernel,
         out_shape=pltpu.VMEM(images.shape[1:], jnp.float32),
-        in_specs=[SMEM, VMEM],
+        in_specs=[pl.BlockSpec(memory_space=pltpu.HBM)] * 2,
         out_specs=VMEM,
+        scratch_shapes=[
+            pltpu.SMEM(defocus.shape, defocus.dtype),
+            pltpu.VMEM(images.shape[1:], images.dtype),
+            pltpu.SemaphoreType.DMA,
+            pltpu.SemaphoreType.DMA((IMAGE_MOVES,)),
+        ],
         compiler_params=pltpu.CompilerParams(vmem_limit_bytes=VMEM_LIMIT),
         cost_estimate=pl.CostEstimate(
             flops=30 * count * fourier * fourier, bytes_accessed=6 * count * fourier * width, transcendentals=0
         ),
         name="weigh_images",
-    )(defocus, images)
+    )(*(pltpu.with_memory_space_constraint(value, pltpu.HBM) for value in (defocus, images)))
 
 
 class Places:
@@ -199,6 +215,35 @@
     )(me, block_index, orient, *tables[:2], u, *parts)
 
 
+def more_scores(first, orient, tables, u, parts, flips, scores):
+    count, fourier, width = u.shape
+    picks = orient.shape[0]
+    block_rows = parts[0].shape[1]
+
+    def kernel(first_ref, orient_ref, row_ref, fwd_ref, u_ref, old_ref, *rest):
+        part_refs, score_ref = rest[:-1], rest[-1]
+        places = Places(first_ref, orient_ref, block_rows)
+
+        def store(k, i, value):
+            score_ref[k, i : i + 1, :] = value + old_ref[k, i : i + 1, :]
+
+        add_up_scores(places, flips, row_ref, fwd_ref, u_ref, part_refs, store)
+
+    return pl.pallas_call(
+        kernel,
+        out_shape=pltpu.VMEM((picks, count, LANES), jnp.float32),
+        in_specs=[SMEM] * 2 + [VMEM] * (4 + len(parts)),
+        out_specs=VMEM,
+        compiler_params=pltpu.CompilerParams(vmem_limit_bytes=VMEM_LIMIT),
+        cost_estimate=pl.CostEstimate(
+            flops=len(parts) * count * picks * block_rows * width * LANES * 2,
+            bytes_accessed=4 * count * fourier * width,
+            transcendentals=0,
+        ),
+        name="more_scores",
+    )(first, orient, *tables[:2], u, scores, *parts)
+
+
 def expectation(first, orient, tables, u, parts, flips, scores, out_flips):
     count, fourier, width = u.shape
     picks = orient.shape[0]
@@ -299,33 +344,34 @@
     weigher = interp[0].reshape(orient_count * block_rows, slab_rows)
     own = jnp.dot(weigher, volume, preferred_element_type=jnp.float32).astype(jnp.bfloat16)
     own = own.reshape(orient_count, block_rows, width)
-    from_other, from_far, from_near, from_side = (to(own, flip) for flip in (other, far, near, side))
+    from_near, from_far, from_other, from_side = (to(own, flip) for flip in (near, far, other, side))
     from_near_side = to(from_near, side)
     me = lax.axis_index("slab").astype(jnp.int32).reshape(1)
     u = weigh_images(images, defocus)
-    from_far, from_other, u, from_side, from_near_side = lax.optimization_barrier((from_far, from_other, u, from_side, from_near_side))
-    from_far_side, from_other_side = to(jnp.stack([from_far, from_other]), side)
+    from_far, u = lax.optimization_barrier((from_far, u))
+    from_other, _ = lax.optimization_barrier((from_other, from_far))
+    from_far_side, from_other_side = to(from_far, side), to(from_other, side)
 
     tables = separable_tables(fourier)
     scores, first, choice = first_scores(me, block_index[0], orient[0].T, tables, u, [own, from_near, from_far, from_other, from_side, from_near_side], (0, near, far, other, side, near + side))
-    late_weigher, scores = lax.optimization_barrier((weigher, scores))
-    weigher_across = swap(late_weigher, "img", group_count, 2)
     common = first, choice, tables, u
+    scores = more_scores(*common, [from_far_side], (far + side,), scores)
     weights, rounded, side_rows = expectation(
         *common,
-        [from_far_side, from_other_side],
-        (far + side, other + side),
+        [from_other_side],
+        (other + side,),
         scores,
         (other + side,),
     )
     sent_first = to(side_rows[0], side)
     rest = to(more_slices(*common, rounded, block_rows, (far + side, near + side, side)), side)
-    weigher_across, sent_first = lax.optimization_barrier((weigher_across, sent_first))
     rows = more_slices(*common, rounded, block_rows, (other, far, near, 0))
+    last = to(together(rows[0], sent_first), other)
+    late_weigher, last = lax.optimization_barrier((weigher, last))
     back = together(
         rows[3],
         rest[2],
-        to(together(rows[0], sent_first), other),
+        last,
         to(together(rows[1], rest[0]), far),
         to(together(rows[2], rest[1]), near),
     ).reshape(orient_count * block_rows, width)
@@ -334,7 +380,7 @@
         across = swap(value, "img", group_count, 2)
         return [value, swap(value, "img", group_count, 1), across, swap(across, "img", group_count, 1)]
 
-    weighers = [weigher, swap(weigher, "img", group_count, 1), weigher_across, swap(weigher_across, "img", group_count, 1)]
+    weighers = all_groups(late_weigher)
     backs = all_groups(back)
     update = lax.dot_general(
         jnp.concatenate(weighers, axis=0),

time: 42.6 us -> 41.3 us (0.969)
  local copies, waits for them, and re-layouts: 3.43 us -> 1.54 us
  Pallas kernels: 7.1 us -> 7.64 us
    unnamed x19 -> x15, local copies, waits for them, and re-layouts: 3.42 us -> 1.54 us
    pallas_call x1, Pallas kernels: 1.6 us -> 2.06 us  [weigh_images(): pl.pallas_call(kernel, out_shape=pltpu.VMEM(images.shape[1:], jnp.float32...]
    ppermute x17 -> x18, starting transfers between devices: 22.5 us -> 22.8 us  [swap(): lax.ppermute(value, axis, [(source, source ^ flip) for source in range(si...]
    ppermute x17 -> x18, waiting for transfers between devices: 6.23 us -> 6 us  [swap(): lax.ppermute(value, axis, [(source, source ^ flip) for source in range(si...]
  transfers between devices with their start and end apart: 17 -> 18, of which waited for: 6 -> 9; matrix products, arithmetic and copies ran while one was open for 2% -> 2% of each run, Pallas kernels for 17% -> 16%
where the time goes in v6:
time: 41.3 us; the launch traced here: 41.1 us
  starting transfers between devices  22.8 us (55%)
  Pallas kernels  7.64 us (18%)
  waiting for transfers between devices  6 us (15%)
  matrix products  2.22 us (5%)
  local copies, waits for them, and re-layouts  1.54 us (4%)
  between operations  0.8 us (2%)
    ppermute x18, starting transfers between devices, swap(): lax.ppermute(value, axis, [(source, source ^ flip) for source in range(si...  22.8 us
    ppermute x18, waiting for transfers between devices, swap(): lax.ppermute(value, axis, [(source, source ^ flip) for source in range(si...  6 us
    pallas_call x1, Pallas kernels, first_scores(): pl.pallas_call(kernel, out_shape=(pltpu.VMEM((picks, count, LANES), jnp.f...  2.13 us
    pallas_call x1, Pallas kernels, weigh_images(): pl.pallas_call(kernel, out_shape=pltpu.VMEM(images.shape[1:], jnp.float32...  2.06 us
    pallas_call x2, Pallas kernels, more_slices(): pl.pallas_call(kernel, out_shape=pltpu.VMEM((len(out_flips), orient_count...  2.06 us
    unnamed x15, local copies, waits for them, and re-layouts  1.54 us
    dot_general x1, matrix products, direct(): lax.dot_general(jnp.concatenate(weighers, axis=0), jnp.concatenate(backs,...  1.13 us
    dot_general x1, matrix products, direct(): jnp.dot(weigher, volume, preferred_element_type=jnp.float32)  1.09 us
  transfers between devices with their start and end apart: 18, of which 9 were waited for; matrix products, arithmetic and copies ran while one was open for 2% of the time, Pallas kernels for 16%

profile of v6, /device:TPU:0, one launch (start us, length us, event | category | flops | bytes accessed | tf_op | source)
XLA Modules:
  0.0 41.1 jit_solution(8094317602661122883)
XLA Ops:
  0.7 0.9 %copy-done = bf16[512,256]{1,0:T(8,128)(2,1)S(1)} copy-done((bf16[512,256]{1,0:T(8,128)(2,1)S(1)}, bf16[512,256]{1,0:T(8,128)(2,1)}, u32[]{:S(2)}) %copy-start) | copy-done | bytes 262168
  1.6 1.1 %convolution_convert_fusion = bf16[128,256]{1,0:T(8,128)(2,1)S(1)} fusion(bf16[128,512]{1,0:T(8,128)(2,1)} %bitcast.36, bf16[512,256]{1,0:T(8,128)(2,1)S(1)} %copy-done), kind=kOutput, calls=%fused_computation.1 | convolution fusion | flops 33587200 | bytes 458752 | tf_op jit(solution)/shard_map/dot_general | solution.py:345
  2.7 3.1 %collective-permute-start.1 = (bf16[8,16,256]{2,1,0:T(8,128)(2,1)S(1)}, bf16[8,16,256]{2,1,0:T(8,128)(2,1)S(1)}, u32[]{:S(2)}, u32[]{:S(2)}) collective-permute-start(bf16[8,16,256]{2,1,0:T(8,128)(2,1)S(1)} %bitcast.28), channel_id=1, source_target_pairs={{0,8},{4,12},{8,0},{12,4},{16,24},{20,28},{24,16},{28,20},{1,9},{5... | collective-permute-start | bytes 196616 | tf_op jit(solution)/shard_map/ppermute | solution.py:326
  5.8 2.6 %collective-permute-start = (bf16[8,16,256]{2,1,0:T(8,128)(2,1)S(1)}, bf16[8,16,256]{2,1,0:T(8,128)(2,1)S(1)}, u32[]{:S(2)}, u32[]{:S(2)}) collective-permute-start(bf16[8,16,256]{2,1,0:T(8,128)(2,1)S(1)} %bitcast.29), channel_id=1, source_target_pairs={{0,16},{4,20},{8,24},{12,28},{16,0},{20,4},{24,8},{28,12},{1,17},{... | collective-permute-start | bytes 196616 | tf_op jit(solution)/shard_map/ppermute | solution.py:326
  8.4 1.7 %collective-permute-start.3 = (bf16[8,16,256]{2,1,0:T(8,128)(2,1)S(1)}, bf16[8,16,256]{2,1,0:T(8,128)(2,1)S(1)}, u32[]{:S(2)}, u32[]{:S(2)}) collective-permute-start(bf16[8,16,256]{2,1,0:T(8,128)(2,1)S(1)} %bitcast.31), channel_id=1, source_target_pairs={{0,4},{4,0},{8,12},{12,8},{16,20},{20,16},{24,28},{28,24},{1,5},{5... | collective-permute-start | bytes 196616 | tf_op jit(solution)/shard_map/ppermute | solution.py:326
  10.1 0.3 collective-permute-start.4
  10.4 2.1 %weigh_images.1.u_ref = f32[16,128,256]{2,1,0:T(8,128)S(1)} custom-call(f32[1,16]{1,0:T(1,128)} %defocus_hbm.1, bf16[1,16,128,256]{3,2,1,0:T(8,128)(2,1)} %image_hbm.1), custom_call_target="tpu_custom_call" | custom-call | flops 7864320 | bytes 3145728 | tf_op jit(solution)/shard_map/weigh_images/pallas_call | solution.py:89
  12.5 0.6 %collective-permute-done.rest_2_ = bf16[8,16,256]{2,1,0:T(8,128)(2,1)S(1)} collective-permute-done((bf16[8,16,256]{2,1,0:T(8,128)(2,1)S(1)}, bf16[8,16,256]{2,1,0:T(8,128)(2,1)S(1)}, u32[]{:S(2)}, u32[]{:S(2)}) %collective-permute-start) | collective-permute-done | bytes 65568 | tf_op jit(solution)/shard_map/ppermute | solution.py:326
  13.0 1.5 %collective-permute-start.5 = (bf16[8,16,256]{2,1,0:T(8,128)(2,1)S(1)}, bf16[8,16,256]{2,1,0:T(8,128)(2,1)S(1)}, u32[]{:S(2)}, u32[]{:S(2)}) collective-permute-start(bf16[8,16,256]{2,1,0:T(8,128)(2,1)S(1)} %collective-permute-done.rest_2_), channel_id=1, source_target_pairs={{0,4},{4,0},{8,12},{12,8},{16,20},{20,16},{24,28},{28,24},{1,5},{5... | collective-permute-start | bytes 196616 | tf_op jit(solution)/shard_map/ppermute | solution.py:326
  14.5 1.4 %collective-permute-start.6 = (bf16[8,16,256]{2,1,0:T(8,128)(2,1)S(1)}, bf16[8,16,256]{2,1,0:T(8,128)(2,1)S(1)}, u32[]{:S(2)}, u32[]{:S(2)}) collective-permute-start(bf16[8,16,256]{2,1,0:T(8,128)(2,1)S(1)} %collective-permute-done.2.rest_3_), channel_id=1, source_target_pairs={{0,4},{4,0},{8,12},{12,8},{16,20},{20,16},{24,28},{28,24},{1,5},{5... | collective-permute-start | bytes 196616 | tf_op jit(solution)/shard_map/ppermute | solution.py:326
  16.0 2.1 %first_scores.1 = (f32[4,16,128]{2,1,0:T(8,128)S(1)}, s32[8,8]{1,0:T(8,128)S(4)}, s32[4,16]{1,0:T(4,128)S(4)}) custom-call(s32[1]{0:T(128)} %bitcast.1.me_ref, s32[8,8]{1,0:T(8,128)S(1)} %bitcast.33, s32[4,16]{1,0:T(4,128)S(1)} %bitcast.34, f32[128,128]{1,0:T(8,128)S(1)} %copy-done.1, bf16[256,128]{1,0:T(8,128)(2,1)S(1)} %copy-done.3, ...), custom_call_target="tpu_custom_call" | custom-call | flops 402653184 | bytes 2097152 | tf_op jit(solution)/shard_map/first_scores/pallas_call | solution.py:199
  18.1 0.4 more_scores.1.score_ref
  18.8 1.0 %expectation.1 = (f32[1,16,64]{2,1,0:T(8,128)S(1)}, f32[4,16,128]{2,1,0:T(8,128)S(1)}, bf16[1,8,16,256]{3,2,1,0:T(8,128)(2,1)S(1)}) custom-call(s32[8,8]{1,0:T(8,128)S(4)} %get-tuple-element.16.first_ref, s32[4,16]{1,0:T(4,128)S(4)} %get-tuple-element.17.orient_ref, f32[128,128]{1,0:T(8,128)S(1)} %copy-done.1, bf16[256,128]{1,0:T(8,128)(2,1)S(1)} %copy-done.3, ...), custom_call_target="tpu_custom_call" | custom-call | flops 134217728 | bytes 2097152 | tf_op jit(solution)/shard_map/expectation/pallas_call | solution.py:280
  19.8 1.5 %collective-permute-start.7 = (bf16[8,16,256]{2,1,0:T(8,128)(2,1)S(1)}, bf16[8,16,256]{2,1,0:T(8,128)(2,1)S(1)}, u32[]{:S(2)}, u32[]{:S(2)}) collective-permute-start(bf16[8,16,256]{2,1,0:T(8,128)(2,1)S(1)} %bitcast.35), channel_id=1, source_target_pairs={{0,4},{4,0},{8,12},{12,8},{16,20},{20,16},{24,28},{28,24},{1,5},{5... | collective-permute-start | bytes 196616 | tf_op jit(solution)/shard_map/ppermute | solution.py:326
  21.3 0.9 %more_slices.3 = bf16[3,8,16,256]{3,2,1,0:T(8,128)(2,1)S(1)} custom-call(s32[8,8]{1,0:T(8,128)S(4)} %get-tuple-element.16.first_ref, s32[4,16]{1,0:T(4,128)S(4)} %get-tuple-element.17.orient_ref, f32[128,128]{1,0:T(8,128)S(1)} %copy-done.1, bf16[128,256]{1,0:T(8,128)(2,1)S(1)} %copy-done.2, f32[16,128,256]{2,1,0:T(8,128)S(1)} %weigh_images.1.u_ref, ...), custom_call_target="tpu_custom_call" | custom-call | flops 201326592 | bytes 2097152 | tf_op jit(solution)/shard_map/more_slices/pallas_call | solution.py:309
  22.2 0.7 %collective-permute-start.12 = (bf16[3,8,16,256]{3,2,1,0:T(8,128)(2,1)S(1)}, bf16[3,8,16,256]{3,2,1,0:T(8,128)(2,1)S(1)}, u32[]{:S(2)}, u32[]{:S(2)}) collective-permute-start(bf16[3,8,16,256]{3,2,1,0:T(8,128)(2,1)S(1)} %more_slices.3), channel_id=1, source_target_pairs={{0,4},{4,0},{8,12},{12,8},{16,20},{20,16},{24,28},{28,24},{1,5},{5... | collective-permute-start | bytes 589832 | tf_op jit(solution)/shard_map/ppermute | solution.py:326
  22.9 1.2 %more_slices.2 = bf16[4,8,16,256]{3,2,1,0:T(8,128)(2,1)S(1)} custom-call(s32[8,8]{1,0:T(8,128)S(4)} %get-tuple-element.16.first_ref, s32[4,16]{1,0:T(4,128)S(4)} %get-tuple-element.17.orient_ref, f32[128,128]{1,0:T(8,128)S(1)} %copy-done.1, bf16[128,256]{1,0:T(8,128)(2,1)S(1)} %copy-done.2, f32[16,128,256]{2,1,0:T(8,128)S(1)} %weigh_images.1.u_ref, ...), custom_call_target="tpu_custom_call" | custom-call | flops 268435456 | bytes 2097152 | tf_op jit(solution)/shard_map/more_slices/pallas_call | solution.py:309
  24.1 0.4 collective-permute-done.7
  24.5 3.1 %collective-permute-start.8 = (bf16[8,16,256]{2,1,0:T(8,128)(2,1)S(1)}, bf16[8,16,256]{2,1,0:T(8,128)(2,1)S(1)}, u32[]{:S(2)}, u32[]{:S(2)}) collective-permute-start(bf16[8,16,256]{2,1,0:T(8,128)(2,1)S(1)} %fusion.14), channel_id=1, source_target_pairs={{0,24},{4,28},{8,16},{12,20},{16,8},{20,12},{24,0},{28,4},{1,25},{... | collective-permute-start | bytes 196616 | tf_op jit(solution)/shard_map/ppermute | solution.py:326
  27.6 0.3 collective-permute-done.12
  28.0 1.7 %collective-permute-start.13 = (bf16[8,16,256]{2,1,0:T(8,128)(2,1)S(1)}, bf16[8,16,256]{2,1,0:T(8,128)(2,1)S(1)}, u32[]{:S(2)}, u32[]{:S(2)}) collective-permute-start(bf16[8,16,256]{2,1,0:T(8,128)(2,1)S(1)} %get-tuple-element.24), channel_id=1, source_target_pairs={{0,16},{4,20},{8,24},{12,28},{16,0},{20,4},{24,8},{28,12},{1,17},{... | collective-permute-start | bytes 196616 | tf_op jit(solution)/shard_map/ppermute | solution.py:326
  29.7 1.6 %collective-permute-start.14 = (bf16[8,16,256]{2,1,0:T(8,128)(2,1)S(1)}, bf16[8,16,256]{2,1,0:T(8,128)(2,1)S(1)}, u32[]{:S(2)}, u32[]{:S(2)}) collective-permute-start(bf16[8,16,256]{2,1,0:T(8,128)(2,1)S(1)} %get-tuple-element.25), channel_id=1, source_target_pairs={{0,8},{4,12},{8,0},{12,4},{16,24},{20,28},{24,16},{28,20},{1,9},{5... | collective-permute-start | bytes 196616 | tf_op jit(solution)/shard_map/ppermute | solution.py:326
  31.3 1.5 %collective-permute-start.10 = (bf16[128,512]{1,0:T(8,128)(2,1)S(1)}, bf16[128,512]{1,0:T(8,128)(2,1)S(1)}, u32[]{:S(2)}, u32[]{:S(2)}) collective-permute-start(bf16[128,512]{1,0:T(8,128)(2,1)S(1)} %bitcast.37), channel_id=1, source_target_pairs={{0,2},{1,3},{2,0},{3,1},{4,6},{5,7},{6,4},{7,5},{8,10},{9,11},{10,... | collective-permute-start | bytes 393224 | tf_op jit(solution)/shard_map/ppermute | solution.py:326
  32.8 0.9 %collective-permute-done.13 = bf16[8,16,256]{2,1,0:T(8,128)(2,1)S(1)} collective-permute-done((bf16[8,16,256]{2,1,0:T(8,128)(2,1)S(1)}, bf16[8,16,256]{2,1,0:T(8,128)(2,1)S(1)}, u32[]{:S(2)}, u32[]{:S(2)}) %collective-permute-start.13) | collective-permute-done | bytes 65568 | tf_op jit(solution)/shard_map/ppermute | solution.py:326
  33.7 0.7 %collective-permute-done.14 = bf16[8,16,256]{2,1,0:T(8,128)(2,1)S(1)} collective-permute-done((bf16[8,16,256]{2,1,0:T(8,128)(2,1)S(1)}, bf16[8,16,256]{2,1,0:T(8,128)(2,1)S(1)}, u32[]{:S(2)}, u32[]{:S(2)}) %collective-permute-start.14) | collective-permute-done | bytes 65568 | tf_op jit(solution)/shard_map/ppermute | solution.py:326
  34.4 1.6 %collective-permute-start.16 = (bf16[128,256]{1,0:T(8,128)(2,1)S(1)}, bf16[128,256]{1,0:T(8,128)(2,1)S(1)}, u32[]{:S(2)}, u32[]{:S(2)}) collective-permute-start(bf16[128,256]{1,0:T(8,128)(2,1)S(1)} %bitcast.40), channel_id=1, source_target_pairs={{0,2},{1,3},{2,0},{3,1},{4,6},{5,7},{6,4},{7,5},{8,10},{9,11},{10,... | collective-permute-start | bytes 196616 | tf_op jit(solution)/shard_map/ppermute | solution.py:326
  36.0 0.4 collective-permute-done.10
  36.4 0.5 %collective-permute-start.15 = (bf16[128,256]{1,0:T(8,128)(2,1)S(1)}, bf16[128,256]{1,0:T(8,128)(2,1)S(1)}, u32[]{:S(2)}, u32[]{:S(2)}) collective-permute-start(bf16[128,256]{1,0:T(8,128)(2,1)S(1)} %bitcast.41), channel_id=1, source_target_pairs={{0,1},{1,0},{2,3},{3,2},{4,5},{5,4},{6,7},{7,6},{8,9},{9,8},{10,11... | collective-permute-start | bytes 196616 | tf_op jit(solution)/shard_map/ppermute | solution.py:326
  36.9 1.8 %collective-permute-done.16 = bf16[128,256]{1,0:T(8,128)(2,1)S(1)} collective-permute-done((bf16[128,256]{1,0:T(8,128)(2,1)S(1)}, bf16[128,256]{1,0:T(8,128)(2,1)S(1)}, u32[]{:S(2)}, u32[]{:S(2)}) %collective-permute-start.16) | collective-permute-done | bytes 65568 | tf_op jit(solution)/shard_map/ppermute | solution.py:326
  38.7 0.6 %copy.11 = f32[1,16,64]{2,1,0:T(8,128)} copy(f32[1,16,64]{2,1,0:T(8,128)S(1)} %get-tuple-element.27) | data formatting | bytes 8192
  39.4 0.6 %collective-permute-done.17 = bf16[128,256]{1,0:T(8,128)(2,1)S(1)} collective-permute-done((bf16[128,256]{1,0:T(8,128)(2,1)S(1)}, bf16[128,256]{1,0:T(8,128)(2,1)S(1)}, u32[]{:S(2)}, u32[]{:S(2)}) %collective-permute-start.17) | collective-permute-done | bytes 65568 | tf_op jit(solution)/shard_map/ppermute | solution.py:326
  40.0 1.1 %convolution_multiply_fusion = f32[512,256]{1,0:T(8,128)} fusion(bf16[128,512]{1,0:T(8,128)(2,1)S(1)} %collective-permute-done.11, bf16[128,512]{1,0:T(8,128)(2,1)S(1)} %collective-permute-done.10, bf16[128,512]{1,0:T(8,128)(2,1)S(1)} %collective-permute-done.9, bf16[128,512]{1,0:T(8,128)(2,1)S(1)} %bitcast.39, ...), kind=kOutput, calls=%fused_computation | convolution fusion | flops 137494528 | bytes 1310720 | tf_op jit(solution)/shard_map/dot_general | solution.py:385
  (30 shorter events, 0.5 us)
Async XLA Ops:
  0.6 1.0 %copy-start = (bf16[512,256]{1,0:T(8,128)(2,1)S(1)}, bf16[512,256]{1,0:T(8,128)(2,1)}, u32[]{:S(2)}) copy-start(bf16[512,256]{1,0:T(8,128)(2,1)} %param.9) | copy-start | bytes 786436
  0.6 15.3 %copy-start.1 = (f32[128,128]{1,0:T(8,128)S(1)}, f32[128,128]{1,0:T(8,128)}, u32[]{:S(2)}) copy-start(f32[128,128]{1,0:T(8,128)} %constant.15.clone.row_ref) | copy-start | bytes 196612
  0.7 15.3 %copy-start.3 = (bf16[256,128]{1,0:T(8,128)(2,1)S(1)}, bf16[256,128]{1,0:T(8,128)(2,1)}, u32[]{:S(2)}) copy-start(bf16[256,128]{1,0:T(8,128)(2,1)} %constant.16.clone.fwd_ref) | copy-start | bytes 196612
  0.7 15.3 %copy-start.5 = (s32[1,16,4]{1,2,0:T(4,128)S(1)}, s32[1,16,4]{1,2,0:T(4,128)}, u32[]{:S(2)}) copy-start(s32[1,16,4]{1,2,0:T(4,128)} %param.14) | copy-start | bytes 772
  0.7 15.3 %copy-start.4 = (s32[1,8,8]{2,1,0:T(8,128)S(1)}, s32[1,8,8]{2,1,0:T(8,128)}, u32[]{:S(2)}) copy-start(s32[1,8,8]{2,1,0:T(8,128)} %param.11) | copy-start | bytes 772
  2.7 7.4 %collective-permute-start.1 = (bf16[8,16,256]{2,1,0:T(8,128)(2,1)S(1)}, bf16[8,16,256]{2,1,0:T(8,128)(2,1)S(1)}, u32[]{:S(2)}, u32[]{:S(2)}) collective-permute-start(bf16[8,16,256]{2,1,0:T(8,128)(2,1)S(1)} %bitcast.28), channel_id=1, source_target_pairs={{0,8},{4,12},{8,0},{12,4},{16,24},{20,28},{24,16},{28,20},{1,9},{5... | collective-permute-start | bytes 196616 | tf_op jit(solution)/shard_map/ppermute | solution.py:326
  5.8 7.3 %collective-permute-start = (bf16[8,16,256]{2,1,0:T(8,128)(2,1)S(1)}, bf16[8,16,256]{2,1,0:T(8,128)(2,1)S(1)}, u32[]{:S(2)}, u32[]{:S(2)}) collective-permute-start(bf16[8,16,256]{2,1,0:T(8,128)(2,1)S(1)} %bitcast.29), channel_id=1, source_target_pairs={{0,16},{4,20},{8,24},{12,28},{16,0},{20,4},{24,8},{28,12},{1,17},{... | collective-permute-start | bytes 196616 | tf_op jit(solution)/shard_map/ppermute | solution.py:326
  8.4 6.2 %collective-permute-start.2 = (bf16[8,16,256]{2,1,0:T(8,128)(2,1)S(1)}, bf16[8,16,256]{2,1,0:T(8,128)(2,1)S(1)}, u32[]{:S(2)}, u32[]{:S(2)}) collective-permute-start(bf16[8,16,256]{2,1,0:T(8,128)(2,1)S(1)} %bitcast.30), channel_id=1, source_target_pairs={{0,24},{4,28},{8,16},{12,20},{16,8},{20,12},{24,0},{28,4},{1,25},{... | collective-permute-start | bytes 196616 | tf_op jit(solution)/shard_map/ppermute | solution.py:326
  8.4 7.6 %collective-permute-start.3 = (bf16[8,16,256]{2,1,0:T(8,128)(2,1)S(1)}, bf16[8,16,256]{2,1,0:T(8,128)(2,1)S(1)}, u32[]{:S(2)}, u32[]{:S(2)}) collective-permute-start(bf16[8,16,256]{2,1,0:T(8,128)(2,1)S(1)} %bitcast.31), channel_id=1, source_target_pairs={{0,4},{4,0},{8,12},{12,8},{16,20},{20,16},{24,28},{28,24},{1,5},{5... | collective-permute-start | bytes 196616 | tf_op jit(solution)/shard_map/ppermute | solution.py:326
  10.1 5.9 %collective-permute-start.4 = (bf16[8,16,256]{2,1,0:T(8,128)(2,1)S(1)}, bf16[8,16,256]{2,1,0:T(8,128)(2,1)S(1)}, u32[]{:S(2)}, u32[]{:S(2)}) collective-permute-start(bf16[8,16,256]{2,1,0:T(8,128)(2,1)S(1)} %collective-permute-done.1.rest_1_), channel_id=1, source_target_pairs={{0,4},{4,0},{8,12},{12,8},{16,20},{20,16},{24,28},{28,24},{1,5},{5... | collective-permute-start | bytes 196616 | tf_op jit(solution)/shard_map/ppermute | solution.py:326
  13.0 5.1 %collective-permute-start.5 = (bf16[8,16,256]{2,1,0:T(8,128)(2,1)S(1)}, bf16[8,16,256]{2,1,0:T(8,128)(2,1)S(1)}, u32[]{:S(2)}, u32[]{:S(2)}) collective-permute-start(bf16[8,16,256]{2,1,0:T(8,128)(2,1)S(1)} %collective-permute-done.rest_2_), channel_id=1, source_target_pairs={{0,4},{4,0},{8,12},{12,8},{16,20},{20,16},{24,28},{28,24},{1,5},{5... | collective-permute-start | bytes 196616 | tf_op jit(solution)/shard_map/ppermute | solution.py:326
  14.5 4.3 %collective-permute-start.6 = (bf16[8,16,256]{2,1,0:T(8,128)(2,1)S(1)}, bf16[8,16,256]{2,1,0:T(8,128)(2,1)S(1)}, u32[]{:S(2)}, u32[]{:S(2)}) collective-permute-start(bf16[8,16,256]{2,1,0:T(8,128)(2,1)S(1)} %collective-permute-done.2.rest_3_), channel_id=1, source_target_pairs={{0,4},{4,0},{8,12},{12,8},{16,20},{20,16},{24,28},{28,24},{1,5},{5... | collective-permute-start | bytes 196616 | tf_op jit(solution)/shard_map/ppermute | solution.py:326
  16.0 2.8 %copy-start.2 = (bf16[128,256]{1,0:T(8,128)(2,1)S(1)}, bf16[128,256]{1,0:T(8,128)(2,1)}, u32[]{:S(2)}) copy-start(bf16[128,256]{1,0:T(8,128)(2,1)} %constant.17.clone.back_ref) | copy-start | bytes 196612
  19.8 4.6 %collective-permute-start.7 = (bf16[8,16,256]{2,1,0:T(8,128)(2,1)S(1)}, bf16[8,16,256]{2,1,0:T(8,128)(2,1)S(1)}, u32[]{:S(2)}, u32[]{:S(2)}) collective-permute-start(bf16[8,16,256]{2,1,0:T(8,128)(2,1)S(1)} %bitcast.35), channel_id=1, source_target_pairs={{0,4},{4,0},{8,12},{12,8},{16,20},{20,16},{24,28},{28,24},{1,5},{5... | collective-permute-start | bytes 196616 | tf_op jit(solution)/shard_map/ppermute | solution.py:326
  22.2 9.1 %copy-start.6 = (bf16[1,8,16,512]{3,2,1,0:T(8,128)(2,1)S(1)}, bf16[1,8,16,512]{3,2,1,0:T(8,128)(2,1)}, u32[]{:S(2)}) copy-start(bf16[1,8,16,512]{3,2,1,0:T(8,128)(2,1)} %param.10) | copy-start | bytes 393220
  22.2 5.7 %collective-permute-start.12 = (bf16[3,8,16,256]{3,2,1,0:T(8,128)(2,1)S(1)}, bf16[3,8,16,256]{3,2,1,0:T(8,128)(2,1)S(1)}, u32[]{:S(2)}, u32[]{:S(2)}) collective-permute-start(bf16[3,8,16,256]{3,2,1,0:T(8,128)(2,1)S(1)} %more_slices.3), channel_id=1, source_target_pairs={{0,4},{4,0},{8,12},{12,8},{16,20},{20,16},{24,28},{28,24},{1,5},{5... | collective-permute-start | bytes 589832 | tf_op jit(solution)/shard_map/ppermute | solution.py:326
  24.5 6.8 %collective-permute-start.8 = (bf16[8,16,256]{2,1,0:T(8,128)(2,1)S(1)}, bf16[8,16,256]{2,1,0:T(8,128)(2,1)S(1)}, u32[]{:S(2)}, u32[]{:S(2)}) collective-permute-start(bf16[8,16,256]{2,1,0:T(8,128)(2,1)S(1)} %fusion.14), channel_id=1, source_target_pairs={{0,24},{4,28},{8,16},{12,20},{16,8},{20,12},{24,0},{28,4},{1,25},{... | collective-permute-start | bytes 196616 | tf_op jit(solution)/shard_map/ppermute | solution.py:326
  28.0 5.7 %collective-permute-start.13 = (bf16[8,16,256]{2,1,0:T(8,128)(2,1)S(1)}, bf16[8,16,256]{2,1,0:T(8,128)(2,1)S(1)}, u32[]{:S(2)}, u32[]{:S(2)}) collective-permute-start(bf16[8,16,256]{2,1,0:T(8,128)(2,1)S(1)} %get-tuple-element.24), channel_id=1, source_target_pairs={{0,16},{4,20},{8,24},{12,28},{16,0},{20,4},{24,8},{28,12},{1,17},{... | collective-permute-start | bytes 196616 | tf_op jit(solution)/shard_map/ppermute | solution.py:326
  29.7 4.7 %collective-permute-start.14 = (bf16[8,16,256]{2,1,0:T(8,128)(2,1)S(1)}, bf16[8,16,256]{2,1,0:T(8,128)(2,1)S(1)}, u32[]{:S(2)}, u32[]{:S(2)}) collective-permute-start(bf16[8,16,256]{2,1,0:T(8,128)(2,1)S(1)} %get-tuple-element.25), channel_id=1, source_target_pairs={{0,8},{4,12},{8,0},{12,4},{16,24},{20,28},{24,16},{28,20},{1,9},{5... | collective-permute-start | bytes 196616 | tf_op jit(solution)/shard_map/ppermute | solution.py:326
  31.3 5.1 %collective-permute-start.10 = (bf16[128,512]{1,0:T(8,128)(2,1)S(1)}, bf16[128,512]{1,0:T(8,128)(2,1)S(1)}, u32[]{:S(2)}, u32[]{:S(2)}) collective-permute-start(bf16[128,512]{1,0:T(8,128)(2,1)S(1)} %bitcast.37), channel_id=1, source_target_pairs={{0,2},{1,3},{2,0},{3,1},{4,6},{5,7},{6,4},{7,5},{8,10},{9,11},{10,... | collective-permute-start | bytes 393224 | tf_op jit(solution)/shard_map/ppermute | solution.py:326
  32.8 6.5 %collective-permute-start.9 = (bf16[128,512]{1,0:T(8,128)(2,1)S(1)}, bf16[128,512]{1,0:T(8,128)(2,1)S(1)}, u32[]{:S(2)}, u32[]{:S(2)}) collective-permute-start(bf16[128,512]{1,0:T(8,128)(2,1)S(1)} %bitcast.38), channel_id=1, source_target_pairs={{0,1},{1,0},{2,3},{3,2},{4,5},{5,4},{6,7},{7,6},{8,9},{9,8},{10,11... | collective-permute-start | bytes 393224 | tf_op jit(solution)/shard_map/ppermute | solution.py:326
  34.4 4.3 %collective-permute-start.16 = (bf16[128,256]{1,0:T(8,128)(2,1)S(1)}, bf16[128,256]{1,0:T(8,128)(2,1)S(1)}, u32[]{:S(2)}, u32[]{:S(2)}) collective-permute-start(bf16[128,256]{1,0:T(8,128)(2,1)S(1)} %bitcast.40), channel_id=1, source_target_pairs={{0,2},{1,3},{2,0},{3,1},{4,6},{5,7},{6,4},{7,5},{8,10},{9,11},{10,... | collective-permute-start | bytes 196616 | tf_op jit(solution)/shard_map/ppermute | solution.py:326
  36.4 2.9 %collective-permute-start.11 = (bf16[128,512]{1,0:T(8,128)(2,1)S(1)}, bf16[128,512]{1,0:T(8,128)(2,1)S(1)}, u32[]{:S(2)}, u32[]{:S(2)}) collective-permute-start(bf16[128,512]{1,0:T(8,128)(2,1)S(1)} %collective-permute-done.10), channel_id=1, source_target_pairs={{0,1},{1,0},{2,3},{3,2},{4,5},{5,4},{6,7},{7,6},{8,9},{9,8},{10,11... | collective-permute-start | bytes 393224 | tf_op jit(solution)/shard_map/ppermute | solution.py:326
  36.4 2.9 %collective-permute-start.15 = (bf16[128,256]{1,0:T(8,128)(2,1)S(1)}, bf16[128,256]{1,0:T(8,128)(2,1)S(1)}, u32[]{:S(2)}, u32[]{:S(2)}) collective-permute-start(bf16[128,256]{1,0:T(8,128)(2,1)S(1)} %bitcast.41), channel_id=1, source_target_pairs={{0,1},{1,0},{2,3},{3,2},{4,5},{5,4},{6,7},{7,6},{8,9},{9,8},{10,11... | collective-permute-start | bytes 196616 | tf_op jit(solution)/shard_map/ppermute | solution.py:326
  38.7 1.3 %collective-permute-start.17 = (bf16[128,256]{1,0:T(8,128)(2,1)S(1)}, bf16[128,256]{1,0:T(8,128)(2,1)S(1)}, u32[]{:S(2)}, u32[]{:S(2)}) collective-permute-start(bf16[128,256]{1,0:T(8,128)(2,1)S(1)} %collective-permute-done.16), channel_id=1, source_target_pairs={{0,1},{1,0},{2,3},{3,2},{4,5},{5,4},{6,7},{7,6},{8,9},{9,8},{10,11... | collective-permute-start | bytes 196616 | tf_op jit(solution)/shard_map/ppermute | solution.py:326

commit v7 on v6

--- a/solution.py
+++ b/solution.py
@@ -367,7 +367,7 @@
     rest = to(more_slices(*common, rounded, block_rows, (far + side, near + side, side)), side)
     rows = more_slices(*common, rounded, block_rows, (other, far, near, 0))
     last = to(together(rows[0], sent_first), other)
-    late_weigher, last = lax.optimization_barrier((weigher, last))
+    late_weigher, rest = lax.optimization_barrier((weigher, rest))
     back = together(
         rows[3],
         rest[2],
@@ -380,14 +380,18 @@
         across = swap(value, "img", group_count, 2)
         return [value, swap(value, "img", group_count, 1), across, swap(across, "img", group_count, 1)]
 
-    weighers = all_groups(late_weigher)
+    across = swap(late_weigher, "img", group_count, 2)
+    weighers = [weigher, swap(weigher, "img", group_count, 1), across, swap(across, "img", group_count, 1)]
     backs = all_groups(back)
-    update = lax.dot_general(
-        jnp.concatenate(weighers, axis=0),
-        jnp.concatenate(backs, axis=0),
-        (((0,), (0,)), ((), ())),
-        preferred_element_type=jnp.float32,
-    )
+    def give_back(pair):
+        return lax.dot_general(
+            jnp.concatenate([weighers[i] for i in pair], axis=0),
+            jnp.concatenate([backs[i] for i in pair], axis=0),
+            (((0,), (0,)), ((), ())),
+            preferred_element_type=jnp.float32,
+        )
+
+    update = lax.optimization_barrier(give_back((0, 2))) + give_back((1, 3))
     return update / math.sqrt(image_count), weights
 
 

time: 41.3 us -> 41.2 us (level)
    dot_general x1 -> x2, matrix products: 1.13 us -> 1.33 us  [give_back(): lax.dot_general(jnp.concatenate([weighers[i] for i in pair], axis=0), jnp...]
where the time goes in v7:
time: 41.2 us; the launch traced here: 41.1 us
  starting transfers between devices  22.8 us (55%)
  Pallas kernels  7.63 us (19%)
  waiting for transfers between devices  5.78 us (14%)
  matrix products  2.41 us (6%)
  local copies, waits for them, and re-layouts  1.54 us (4%)
  between operations  0.82 us (2%)
    ppermute x18, starting transfers between devices, swap(): lax.ppermute(value, axis, [(source, source ^ flip) for source in range(si...  22.8 us
    ppermute x18, waiting for transfers between devices, swap(): lax.ppermute(value, axis, [(source, source ^ flip) for source in range(si...  5.78 us
    pallas_call x1, Pallas kernels, first_scores(): pl.pallas_call(kernel, out_shape=(pltpu.VMEM((picks, count, LANES), jnp.f...  2.12 us
    pallas_call x1, Pallas kernels, weigh_images(): pl.pallas_call(kernel, out_shape=pltpu.VMEM(images.shape[1:], jnp.float32...  2.06 us
    pallas_call x2, Pallas kernels, more_slices(): pl.pallas_call(kernel, out_shape=pltpu.VMEM((len(out_flips), orient_count...  2.05 us
    unnamed x15, local copies, waits for them, and re-layouts  1.54 us
    dot_general x2, matrix products, give_back(): lax.dot_general(jnp.concatenate([weighers[i] for i in pair], axis=0), jnp...  1.33 us
    dot_general x1, matrix products, direct(): jnp.dot(weigher, volume, preferred_element_type=jnp.float32)  1.09 us
  transfers between devices with their start and end apart: 18, of which 9 were waited for; matrix products, arithmetic and copies ran while one was open for 2% of the time, Pallas kernels for 16%

profile of v7, /device:TPU:0, one launch (start us, length us, event | category | flops | bytes accessed | tf_op | source)
XLA Modules:
  0.0 41.1 jit_solution(4615923872736161817)
XLA Ops:
  0.7 0.9 %copy-done = bf16[512,256]{1,0:T(8,128)(2,1)S(1)} copy-done((bf16[512,256]{1,0:T(8,128)(2,1)S(1)}, bf16[512,256]{1,0:T(8,128)(2,1)}, u32[]{:S(2)}) %copy-start) | copy-done | bytes 262168
  1.6 1.1 %convolution_convert_fusion = bf16[128,256]{1,0:T(8,128)(2,1)S(1)} fusion(bf16[128,512]{1,0:T(8,128)(2,1)} %bitcast.36, bf16[512,256]{1,0:T(8,128)(2,1)S(1)} %copy-done), kind=kOutput, calls=%fused_computation.2 | convolution fusion | flops 33587200 | bytes 458752 | tf_op jit(solution)/shard_map/dot_general | solution.py:345
  2.7 3.1 %collective-permute-start.1 = (bf16[8,16,256]{2,1,0:T(8,128)(2,1)S(1)}, bf16[8,16,256]{2,1,0:T(8,128)(2,1)S(1)}, u32[]{:S(2)}, u32[]{:S(2)}) collective-permute-start(bf16[8,16,256]{2,1,0:T(8,128)(2,1)S(1)} %bitcast.28), channel_id=1, source_target_pairs={{0,8},{4,12},{8,0},{12,4},{16,24},{20,28},{24,16},{28,20},{1,9},{5... | collective-permute-start | bytes 196616 | tf_op jit(solution)/shard_map/ppermute | solution.py:326
  5.8 2.6 %collective-permute-start = (bf16[8,16,256]{2,1,0:T(8,128)(2,1)S(1)}, bf16[8,16,256]{2,1,0:T(8,128)(2,1)S(1)}, u32[]{:S(2)}, u32[]{:S(2)}) collective-permute-start(bf16[8,16,256]{2,1,0:T(8,128)(2,1)S(1)} %bitcast.29), channel_id=1, source_target_pairs={{0,16},{4,20},{8,24},{12,28},{16,0},{20,4},{24,8},{28,12},{1,17},{... | collective-permute-start | bytes 196616 | tf_op jit(solution)/shard_map/ppermute | solution.py:326
  8.4 1.7 %collective-permute-start.3 = (bf16[8,16,256]{2,1,0:T(8,128)(2,1)S(1)}, bf16[8,16,256]{2,1,0:T(8,128)(2,1)S(1)}, u32[]{:S(2)}, u32[]{:S(2)}) collective-permute-start(bf16[8,16,256]{2,1,0:T(8,128)(2,1)S(1)} %bitcast.31), channel_id=1, source_target_pairs={{0,4},{4,0},{8,12},{12,8},{16,20},{20,16},{24,28},{28,24},{1,5},{5... | collective-permute-start | bytes 196616 | tf_op jit(solution)/shard_map/ppermute | solution.py:326
  10.1 0.3 collective-permute-start.4
  10.4 2.1 %weigh_images.1.u_ref = f32[16,128,256]{2,1,0:T(8,128)S(1)} custom-call(f32[1,16]{1,0:T(1,128)} %defocus_hbm.1, bf16[1,16,128,256]{3,2,1,0:T(8,128)(2,1)} %image_hbm.1), custom_call_target="tpu_custom_call" | custom-call | flops 7864320 | bytes 3145728 | tf_op jit(solution)/shard_map/weigh_images/pallas_call | solution.py:89
  12.5 0.6 %collective-permute-done.rest_2_ = bf16[8,16,256]{2,1,0:T(8,128)(2,1)S(1)} collective-permute-done((bf16[8,16,256]{2,1,0:T(8,128)(2,1)S(1)}, bf16[8,16,256]{2,1,0:T(8,128)(2,1)S(1)}, u32[]{:S(2)}, u32[]{:S(2)}) %collective-permute-start) | collective-permute-done | bytes 65568 | tf_op jit(solution)/shard_map/ppermute | solution.py:326
  13.0 1.5 %collective-permute-start.5 = (bf16[8,16,256]{2,1,0:T(8,128)(2,1)S(1)}, bf16[8,16,256]{2,1,0:T(8,128)(2,1)S(1)}, u32[]{:S(2)}, u32[]{:S(2)}) collective-permute-start(bf16[8,16,256]{2,1,0:T(8,128)(2,1)S(1)} %collective-permute-done.rest_2_), channel_id=1, source_target_pairs={{0,4},{4,0},{8,12},{12,8},{16,20},{20,16},{24,28},{28,24},{1,5},{5... | collective-permute-start | bytes 196616 | tf_op jit(solution)/shard_map/ppermute | solution.py:326
  14.5 1.4 %collective-permute-start.6 = (bf16[8,16,256]{2,1,0:T(8,128)(2,1)S(1)}, bf16[8,16,256]{2,1,0:T(8,128)(2,1)S(1)}, u32[]{:S(2)}, u32[]{:S(2)}) collective-permute-start(bf16[8,16,256]{2,1,0:T(8,128)(2,1)S(1)} %collective-permute-done.2.rest_3_), channel_id=1, source_target_pairs={{0,4},{4,0},{8,12},{12,8},{16,20},{20,16},{24,28},{28,24},{1,5},{5... | collective-permute-start | bytes 196616 | tf_op jit(solution)/shard_map/ppermute | solution.py:326
  16.0 2.1 %first_scores.1 = (f32[4,16,128]{2,1,0:T(8,128)S(1)}, s32[8,8]{1,0:T(8,128)S(4)}, s32[4,16]{1,0:T(4,128)S(4)}) custom-call(s32[1]{0:T(128)} %bitcast.1.me_ref, s32[8,8]{1,0:T(8,128)S(1)} %bitcast.33, s32[4,16]{1,0:T(4,128)S(1)} %bitcast.34, f32[128,128]{1,0:T(8,128)S(1)} %copy-done.1, bf16[256,128]{1,0:T(8,128)(2,1)S(1)} %copy-done.3, ...), custom_call_target="tpu_custom_call" | custom-call | flops 402653184 | bytes 2097152 | tf_op jit(solution)/shard_map/first_scores/pallas_call | solution.py:199
  18.1 0.4 more_scores.1.score_ref
  18.5 0.3 collective-permute-done.6.rest_0_
  18.8 1.1 %expectation.1 = (f32[1,16,64]{2,1,0:T(8,128)S(1)}, f32[4,16,128]{2,1,0:T(8,128)S(1)}, bf16[1,8,16,256]{3,2,1,0:T(8,128)(2,1)S(1)}) custom-call(s32[8,8]{1,0:T(8,128)S(4)} %get-tuple-element.16.first_ref, s32[4,16]{1,0:T(4,128)S(4)} %get-tuple-element.17.orient_ref, f32[128,128]{1,0:T(8,128)S(1)} %copy-done.1, bf16[256,128]{1,0:T(8,128)(2,1)S(1)} %copy-done.3, ...), custom_call_target="tpu_custom_call" | custom-call | flops 134217728 | bytes 2097152 | tf_op jit(solution)/shard_map/expectation/pallas_call | solution.py:280
  19.9 1.5 %collective-permute-start.9 = (bf16[8,16,256]{2,1,0:T(8,128)(2,1)S(1)}, bf16[8,16,256]{2,1,0:T(8,128)(2,1)S(1)}, u32[]{:S(2)}, u32[]{:S(2)}) collective-permute-start(bf16[8,16,256]{2,1,0:T(8,128)(2,1)S(1)} %bitcast.35), channel_id=1, source_target_pairs={{0,4},{4,0},{8,12},{12,8},{16,20},{20,16},{24,28},{28,24},{1,5},{5... | collective-permute-start | bytes 196616 | tf_op jit(solution)/shard_map/ppermute | solution.py:326
  21.3 0.9 %more_slices.2 = bf16[3,8,16,256]{3,2,1,0:T(8,128)(2,1)S(1)} custom-call(s32[8,8]{1,0:T(8,128)S(4)} %get-tuple-element.16.first_ref, s32[4,16]{1,0:T(4,128)S(4)} %get-tuple-element.17.orient_ref, f32[128,128]{1,0:T(8,128)S(1)} %copy-done.1, bf16[128,256]{1,0:T(8,128)(2,1)S(1)} %copy-done.2, f32[16,128,256]{2,1,0:T(8,128)S(1)} %weigh_images.1.u_ref, ...), custom_call_target="tpu_custom_call" | custom-call | flops 201326592 | bytes 2097152 | tf_op jit(solution)/shard_map/more_slices/pallas_call | solution.py:309
  22.2 0.7 %collective-permute-start.7 = (bf16[3,8,16,256]{3,2,1,0:T(8,128)(2,1)S(1)}, bf16[3,8,16,256]{3,2,1,0:T(8,128)(2,1)S(1)}, u32[]{:S(2)}, u32[]{:S(2)}) collective-permute-start(bf16[3,8,16,256]{3,2,1,0:T(8,128)(2,1)S(1)} %more_slices.2), channel_id=1, source_target_pairs={{0,4},{4,0},{8,12},{12,8},{16,20},{20,16},{24,28},{28,24},{1,5},{5... | collective-permute-start | bytes 589832 | tf_op jit(solution)/shard_map/ppermute | solution.py:326
  22.9 1.1 %more_slices.3 = bf16[4,8,16,256]{3,2,1,0:T(8,128)(2,1)S(1)} custom-call(s32[8,8]{1,0:T(8,128)S(4)} %get-tuple-element.16.first_ref, s32[4,16]{1,0:T(4,128)S(4)} %get-tuple-element.17.orient_ref, f32[128,128]{1,0:T(8,128)S(1)} %copy-done.1, bf16[128,256]{1,0:T(8,128)(2,1)S(1)} %copy-done.2, f32[16,128,256]{2,1,0:T(8,128)S(1)} %weigh_images.1.u_ref, ...), custom_call_target="tpu_custom_call" | custom-call | flops 268435456 | bytes 2097152 | tf_op jit(solution)/shard_map/more_slices/pallas_call | solution.py:309
  24.1 0.4 collective-permute-done.9
  24.5 3.1 %collective-permute-start.10 = (bf16[8,16,256]{2,1,0:T(8,128)(2,1)S(1)}, bf16[8,16,256]{2,1,0:T(8,128)(2,1)S(1)}, u32[]{:S(2)}, u32[]{:S(2)}) collective-permute-start(bf16[8,16,256]{2,1,0:T(8,128)(2,1)S(1)} %fusion.14), channel_id=1, source_target_pairs={{0,24},{4,28},{8,16},{12,20},{16,8},{20,12},{24,0},{28,4},{1,25},{... | collective-permute-start | bytes 196616 | tf_op jit(solution)/shard_map/ppermute | solution.py:326
  27.7 0.3 collective-permute-done.7
  28.0 1.6 %collective-permute-start.11 = (bf16[8,16,256]{2,1,0:T(8,128)(2,1)S(1)}, bf16[8,16,256]{2,1,0:T(8,128)(2,1)S(1)}, u32[]{:S(2)}, u32[]{:S(2)}) collective-permute-start(bf16[8,16,256]{2,1,0:T(8,128)(2,1)S(1)} %get-tuple-element.24), channel_id=1, source_target_pairs={{0,16},{4,20},{8,24},{12,28},{16,0},{20,4},{24,8},{28,12},{1,17},{... | collective-permute-start | bytes 196616 | tf_op jit(solution)/shard_map/ppermute | solution.py:326
  29.7 1.6 %collective-permute-start.12 = (bf16[8,16,256]{2,1,0:T(8,128)(2,1)S(1)}, bf16[8,16,256]{2,1,0:T(8,128)(2,1)S(1)}, u32[]{:S(2)}, u32[]{:S(2)}) collective-permute-start(bf16[8,16,256]{2,1,0:T(8,128)(2,1)S(1)} %get-tuple-element.25), channel_id=1, source_target_pairs={{0,8},{4,12},{8,0},{12,4},{16,24},{20,28},{24,16},{28,20},{1,9},{5... | collective-permute-start | bytes 196616 | tf_op jit(solution)/shard_map/ppermute | solution.py:326
  31.3 1.5 %collective-permute-start.8 = (bf16[128,512]{1,0:T(8,128)(2,1)S(1)}, bf16[128,512]{1,0:T(8,128)(2,1)S(1)}, u32[]{:S(2)}, u32[]{:S(2)}) collective-permute-start(bf16[128,512]{1,0:T(8,128)(2,1)S(1)} %bitcast.37), channel_id=1, source_target_pairs={{0,2},{1,3},{2,0},{3,1},{4,6},{5,7},{6,4},{7,5},{8,10},{9,11},{10,... | collective-permute-start | bytes 393224 | tf_op jit(solution)/shard_map/ppermute | solution.py:326
  32.8 0.9 %collective-permute-done.11 = bf16[8,16,256]{2,1,0:T(8,128)(2,1)S(1)} collective-permute-done((bf16[8,16,256]{2,1,0:T(8,128)(2,1)S(1)}, bf16[8,16,256]{2,1,0:T(8,128)(2,1)S(1)}, u32[]{:S(2)}, u32[]{:S(2)}) %collective-permute-start.11) | collective-permute-done | bytes 65568 | tf_op jit(solution)/shard_map/ppermute | solution.py:326
  33.7 0.7 %collective-permute-done.12 = bf16[8,16,256]{2,1,0:T(8,128)(2,1)S(1)} collective-permute-done((bf16[8,16,256]{2,1,0:T(8,128)(2,1)S(1)}, bf16[8,16,256]{2,1,0:T(8,128)(2,1)S(1)}, u32[]{:S(2)}, u32[]{:S(2)}) %collective-permute-start.12) | collective-permute-done | bytes 65568 | tf_op jit(solution)/shard_map/ppermute | solution.py:326
  34.4 1.6 %collective-permute-start.13 = (bf16[128,256]{1,0:T(8,128)(2,1)S(1)}, bf16[128,256]{1,0:T(8,128)(2,1)S(1)}, u32[]{:S(2)}, u32[]{:S(2)}) collective-permute-start(bf16[128,256]{1,0:T(8,128)(2,1)S(1)} %bitcast.40), channel_id=1, source_target_pairs={{0,2},{1,3},{2,0},{3,1},{4,6},{5,7},{6,4},{7,5},{8,10},{9,11},{10,... | collective-permute-start | bytes 196616 | tf_op jit(solution)/shard_map/ppermute | solution.py:326
  36.5 0.6 %copy.11 = f32[1,16,64]{2,1,0:T(8,128)} copy(f32[1,16,64]{2,1,0:T(8,128)S(1)} %get-tuple-element.27) | data formatting | bytes 8192
  37.3 1.4 %collective-permute-done.13 = bf16[128,256]{1,0:T(8,128)(2,1)S(1)} collective-permute-done((bf16[128,256]{1,0:T(8,128)(2,1)S(1)}, bf16[128,256]{1,0:T(8,128)(2,1)S(1)}, u32[]{:S(2)}, u32[]{:S(2)}) %collective-permute-start.13) | collective-permute-done | bytes 65568 | tf_op jit(solution)/shard_map/ppermute | solution.py:326
  38.7 0.3 fusion.1
  39.0 1.0 %collective-permute-done.17 = bf16[128,256]{1,0:T(8,128)(2,1)S(1)} collective-permute-done((bf16[128,256]{1,0:T(8,128)(2,1)S(1)}, bf16[128,256]{1,0:T(8,128)(2,1)S(1)}, u32[]{:S(2)}, u32[]{:S(2)}) %collective-permute-start.17) | collective-permute-done | bytes 65568 | tf_op jit(solution)/shard_map/ppermute | solution.py:326
  40.0 1.1 %fusion = f32[512,256]{1,0:T(8,128)} fusion(f32[512,256]{1,0:T(8,128)S(1)} %fusion.1, bf16[128,512]{1,0:T(8,128)(2,1)S(1)} %collective-permute-done.15, bf16[128,512]{1,0:T(8,128)(2,1)S(1)} %collective-permute-done.14, bf16[128,256]{1,0:T(8,128)(2,1)S(1)} %collective-permute-done.17, bf16[128,256]{1,0:T(8,128)(2,1)S(1)} %collective-permute-done.16), kind=kOutput, calls=%fused_computation.1 | convolution fusion | flops 68157440 | bytes 1441792 | tf_op jit(solution)/shard_map/dot_general | solution.py:387
  (31 shorter events, 0.9 us)
Async XLA Ops:
  0.6 1.0 %copy-start = (bf16[512,256]{1,0:T(8,128)(2,1)S(1)}, bf16[512,256]{1,0:T(8,128)(2,1)}, u32[]{:S(2)}) copy-start(bf16[512,256]{1,0:T(8,128)(2,1)} %param.9) | copy-start | bytes 786436
  0.6 15.3 %copy-start.1 = (f32[128,128]{1,0:T(8,128)S(1)}, f32[128,128]{1,0:T(8,128)}, u32[]{:S(2)}) copy-start(f32[128,128]{1,0:T(8,128)} %constant.15.clone.row_ref) | copy-start | bytes 196612
  0.7 15.3 %copy-start.3 = (bf16[256,128]{1,0:T(8,128)(2,1)S(1)}, bf16[256,128]{1,0:T(8,128)(2,1)}, u32[]{:S(2)}) copy-start(bf16[256,128]{1,0:T(8,128)(2,1)} %constant.16.clone.fwd_ref) | copy-start | bytes 196612
  0.7 15.3 %copy-start.4 = (s32[1,8,8]{2,1,0:T(8,128)S(1)}, s32[1,8,8]{2,1,0:T(8,128)}, u32[]{:S(2)}) copy-start(s32[1,8,8]{2,1,0:T(8,128)} %param.11) | copy-start | bytes 772
  0.7 15.3 %copy-start.5 = (s32[1,16,4]{1,2,0:T(4,128)S(1)}, s32[1,16,4]{1,2,0:T(4,128)}, u32[]{:S(2)}) copy-start(s32[1,16,4]{1,2,0:T(4,128)} %param.14) | copy-start | bytes 772
  2.7 7.4 %collective-permute-start.1 = (bf16[8,16,256]{2,1,0:T(8,128)(2,1)S(1)}, bf16[8,16,256]{2,1,0:T(8,128)(2,1)S(1)}, u32[]{:S(2)}, u32[]{:S(2)}) collective-permute-start(bf16[8,16,256]{2,1,0:T(8,128)(2,1)S(1)} %bitcast.28), channel_id=1, source_target_pairs={{0,8},{4,12},{8,0},{12,4},{16,24},{20,28},{24,16},{28,20},{1,9},{5... | collective-permute-start | bytes 196616 | tf_op jit(solution)/shard_map/ppermute | solution.py:326
  5.8 7.3 %collective-permute-start = (bf16[8,16,256]{2,1,0:T(8,128)(2,1)S(1)}, bf16[8,16,256]{2,1,0:T(8,128)(2,1)S(1)}, u32[]{:S(2)}, u32[]{:S(2)}) collective-permute-start(bf16[8,16,256]{2,1,0:T(8,128)(2,1)S(1)} %bitcast.29), channel_id=1, source_target_pairs={{0,16},{4,20},{8,24},{12,28},{16,0},{20,4},{24,8},{28,12},{1,17},{... | collective-permute-start | bytes 196616 | tf_op jit(solution)/shard_map/ppermute | solution.py:326
  8.4 6.2 %collective-permute-start.2 = (bf16[8,16,256]{2,1,0:T(8,128)(2,1)S(1)}, bf16[8,16,256]{2,1,0:T(8,128)(2,1)S(1)}, u32[]{:S(2)}, u32[]{:S(2)}) collective-permute-start(bf16[8,16,256]{2,1,0:T(8,128)(2,1)S(1)} %bitcast.30), channel_id=1, source_target_pairs={{0,24},{4,28},{8,16},{12,20},{16,8},{20,12},{24,0},{28,4},{1,25},{... | collective-permute-start | bytes 196616 | tf_op jit(solution)/shard_map/ppermute | solution.py:326
  8.4 7.6 %collective-permute-start.3 = (bf16[8,16,256]{2,1,0:T(8,128)(2,1)S(1)}, bf16[8,16,256]{2,1,0:T(8,128)(2,1)S(1)}, u32[]{:S(2)}, u32[]{:S(2)}) collective-permute-start(bf16[8,16,256]{2,1,0:T(8,128)(2,1)S(1)} %bitcast.31), channel_id=1, source_target_pairs={{0,4},{4,0},{8,12},{12,8},{16,20},{20,16},{24,28},{28,24},{1,5},{5... | collective-permute-start | bytes 196616 | tf_op jit(solution)/shard_map/ppermute | solution.py:326
  10.1 5.9 %collective-permute-start.4 = (bf16[8,16,256]{2,1,0:T(8,128)(2,1)S(1)}, bf16[8,16,256]{2,1,0:T(8,128)(2,1)S(1)}, u32[]{:S(2)}, u32[]{:S(2)}) collective-permute-start(bf16[8,16,256]{2,1,0:T(8,128)(2,1)S(1)} %collective-permute-done.1.rest_1_), channel_id=1, source_target_pairs={{0,4},{4,0},{8,12},{12,8},{16,20},{20,16},{24,28},{28,24},{1,5},{5... | collective-permute-start | bytes 196616 | tf_op jit(solution)/shard_map/ppermute | solution.py:326
  13.0 5.1 %collective-permute-start.5 = (bf16[8,16,256]{2,1,0:T(8,128)(2,1)S(1)}, bf16[8,16,256]{2,1,0:T(8,128)(2,1)S(1)}, u32[]{:S(2)}, u32[]{:S(2)}) collective-permute-start(bf16[8,16,256]{2,1,0:T(8,128)(2,1)S(1)} %collective-permute-done.rest_2_), channel_id=1, source_target_pairs={{0,4},{4,0},{8,12},{12,8},{16,20},{20,16},{24,28},{28,24},{1,5},{5... | collective-permute-start | bytes 196616 | tf_op jit(solution)/shard_map/ppermute | solution.py:326
  14.5 4.3 %collective-permute-start.6 = (bf16[8,16,256]{2,1,0:T(8,128)(2,1)S(1)}, bf16[8,16,256]{2,1,0:T(8,128)(2,1)S(1)}, u32[]{:S(2)}, u32[]{:S(2)}) collective-permute-start(bf16[8,16,256]{2,1,0:T(8,128)(2,1)S(1)} %collective-permute-done.2.rest_3_), channel_id=1, source_target_pairs={{0,4},{4,0},{8,12},{12,8},{16,20},{20,16},{24,28},{28,24},{1,5},{5... | collective-permute-start | bytes 196616 | tf_op jit(solution)/shard_map/ppermute | solution.py:326
  16.0 2.8 %copy-start.2 = (bf16[128,256]{1,0:T(8,128)(2,1)S(1)}, bf16[128,256]{1,0:T(8,128)(2,1)}, u32[]{:S(2)}) copy-start(bf16[128,256]{1,0:T(8,128)(2,1)} %constant.17.clone.back_ref) | copy-start | bytes 196612
  19.9 4.6 %collective-permute-start.9 = (bf16[8,16,256]{2,1,0:T(8,128)(2,1)S(1)}, bf16[8,16,256]{2,1,0:T(8,128)(2,1)S(1)}, u32[]{:S(2)}, u32[]{:S(2)}) collective-permute-start(bf16[8,16,256]{2,1,0:T(8,128)(2,1)S(1)} %bitcast.35), channel_id=1, source_target_pairs={{0,4},{4,0},{8,12},{12,8},{16,20},{20,16},{24,28},{28,24},{1,5},{5... | collective-permute-start | bytes 196616 | tf_op jit(solution)/shard_map/ppermute | solution.py:326
  22.2 9.0 %copy-start.6 = (bf16[1,8,16,512]{3,2,1,0:T(8,128)(2,1)S(1)}, bf16[1,8,16,512]{3,2,1,0:T(8,128)(2,1)}, u32[]{:S(2)}) copy-start(bf16[1,8,16,512]{3,2,1,0:T(8,128)(2,1)} %param.10) | copy-start | bytes 393220
  22.2 5.7 %collective-permute-start.7 = (bf16[3,8,16,256]{3,2,1,0:T(8,128)(2,1)S(1)}, bf16[3,8,16,256]{3,2,1,0:T(8,128)(2,1)S(1)}, u32[]{:S(2)}, u32[]{:S(2)}) collective-permute-start(bf16[3,8,16,256]{3,2,1,0:T(8,128)(2,1)S(1)} %more_slices.2), channel_id=1, source_target_pairs={{0,4},{4,0},{8,12},{12,8},{16,20},{20,16},{24,28},{28,24},{1,5},{5... | collective-permute-start | bytes 589832 | tf_op jit(solution)/shard_map/ppermute | solution.py:326
  24.5 8.3 %collective-permute-start.10 = (bf16[8,16,256]{2,1,0:T(8,128)(2,1)S(1)}, bf16[8,16,256]{2,1,0:T(8,128)(2,1)S(1)}, u32[]{:S(2)}, u32[]{:S(2)}) collective-permute-start(bf16[8,16,256]{2,1,0:T(8,128)(2,1)S(1)} %fusion.14), channel_id=1, source_target_pairs={{0,24},{4,28},{8,16},{12,20},{16,8},{20,12},{24,0},{28,4},{1,25},{... | collective-permute-start | bytes 196616 | tf_op jit(solution)/shard_map/ppermute | solution.py:326
  28.0 5.7 %collective-permute-start.11 = (bf16[8,16,256]{2,1,0:T(8,128)(2,1)S(1)}, bf16[8,16,256]{2,1,0:T(8,128)(2,1)S(1)}, u32[]{:S(2)}, u32[]{:S(2)}) collective-permute-start(bf16[8,16,256]{2,1,0:T(8,128)(2,1)S(1)} %get-tuple-element.24), channel_id=1, source_target_pairs={{0,16},{4,20},{8,24},{12,28},{16,0},{20,4},{24,8},{28,12},{1,17},{... | collective-permute-start | bytes 196616 | tf_op jit(solution)/shard_map/ppermute | solution.py:326
  29.7 4.7 %collective-permute-start.12 = (bf16[8,16,256]{2,1,0:T(8,128)(2,1)S(1)}, bf16[8,16,256]{2,1,0:T(8,128)(2,1)S(1)}, u32[]{:S(2)}, u32[]{:S(2)}) collective-permute-start(bf16[8,16,256]{2,1,0:T(8,128)(2,1)S(1)} %get-tuple-element.25), channel_id=1, source_target_pairs={{0,8},{4,12},{8,0},{12,4},{16,24},{20,28},{24,16},{28,20},{1,9},{5... | collective-permute-start | bytes 196616 | tf_op jit(solution)/shard_map/ppermute | solution.py:326
  31.3 5.0 %collective-permute-start.8 = (bf16[128,512]{1,0:T(8,128)(2,1)S(1)}, bf16[128,512]{1,0:T(8,128)(2,1)S(1)}, u32[]{:S(2)}, u32[]{:S(2)}) collective-permute-start(bf16[128,512]{1,0:T(8,128)(2,1)S(1)} %bitcast.37), channel_id=1, source_target_pairs={{0,2},{1,3},{2,0},{3,1},{4,6},{5,7},{6,4},{7,5},{8,10},{9,11},{10,... | collective-permute-start | bytes 393224 | tf_op jit(solution)/shard_map/ppermute | solution.py:326
  34.4 4.3 %collective-permute-start.13 = (bf16[128,256]{1,0:T(8,128)(2,1)S(1)}, bf16[128,256]{1,0:T(8,128)(2,1)S(1)}, u32[]{:S(2)}, u32[]{:S(2)}) collective-permute-start(bf16[128,256]{1,0:T(8,128)(2,1)S(1)} %bitcast.40), channel_id=1, source_target_pairs={{0,2},{1,3},{2,0},{3,1},{4,6},{5,7},{6,4},{7,5},{8,10},{9,11},{10,... | collective-permute-start | bytes 196616 | tf_op jit(solution)/shard_map/ppermute | solution.py:326
  36.0 3.0 %collective-permute-start.14 = (bf16[128,512]{1,0:T(8,128)(2,1)S(1)}, bf16[128,512]{1,0:T(8,128)(2,1)S(1)}, u32[]{:S(2)}, u32[]{:S(2)}) collective-permute-start(bf16[128,512]{1,0:T(8,128)(2,1)S(1)} %bitcast.38), channel_id=1, source_target_pairs={{0,1},{1,0},{2,3},{3,2},{4,5},{5,4},{6,7},{7,6},{8,9},{9,8},{10,11... | collective-permute-start | bytes 393224 | tf_op jit(solution)/shard_map/ppermute | solution.py:326
  36.2 3.8 %collective-permute-start.15 = (bf16[128,512]{1,0:T(8,128)(2,1)S(1)}, bf16[128,512]{1,0:T(8,128)(2,1)S(1)}, u32[]{:S(2)}, u32[]{:S(2)}) collective-permute-start(bf16[128,512]{1,0:T(8,128)(2,1)S(1)} %collective-permute-done.8), channel_id=1, source_target_pairs={{0,1},{1,0},{2,3},{3,2},{4,5},{5,4},{6,7},{7,6},{8,9},{9,8},{10,11... | collective-permute-start | bytes 393224 | tf_op jit(solution)/shard_map/ppermute | solution.py:326
  37.1 1.9 %collective-permute-start.16 = (bf16[128,256]{1,0:T(8,128)(2,1)S(1)}, bf16[128,256]{1,0:T(8,128)(2,1)S(1)}, u32[]{:S(2)}, u32[]{:S(2)}) collective-permute-start(bf16[128,256]{1,0:T(8,128)(2,1)S(1)} %bitcast.41), channel_id=1, source_target_pairs={{0,1},{1,0},{2,3},{3,2},{4,5},{5,4},{6,7},{7,6},{8,9},{9,8},{10,11... | collective-permute-start | bytes 196616 | tf_op jit(solution)/shard_map/ppermute | solution.py:326
  38.7 1.3 %collective-permute-start.17 = (bf16[128,256]{1,0:T(8,128)(2,1)S(1)}, bf16[128,256]{1,0:T(8,128)(2,1)S(1)}, u32[]{:S(2)}, u32[]{:S(2)}) collective-permute-start(bf16[128,256]{1,0:T(8,128)(2,1)S(1)} %collective-permute-done.13), channel_id=1, source_target_pairs={{0,1},{1,0},{2,3},{3,2},{4,5},{5,4},{6,7},{7,6},{8,9},{9,8},{10,11... | collective-permute-start | bytes 196616 | tf_op jit(solution)/shard_map/ppermute | solution.py:326
